TPU v7x, 32 devices: a whole 2x2x4 slice. The times are simulated.
32 devices in a mesh: dp: 8 (over y, x, core), mp: 4 (over z).
Axes of the slice: x: 2, y: 2, z: 4, core: 2. Of those that a mesh axis runs over, the one named last changes fastest.
Arguments:
- tokens: int32 [8192], P('dp'), may hold values from 0 to 31999
- targets: int32 [8192], P('dp'), may hold values from 0 to 31999
- select: int32 [8192], P('dp'), may hold values from 0 to 1
- bucket: int32 [8192], P('dp'), may hold values from 1 to 4
- embed_table: float32 [32000, 2048], P('mp', 'dp'), may hold values from -6 to 6
- query_weight: float32 [2048, 2048], P('dp', 'mp'), may hold values from -0.125 to 0.125
- keyvalue_weight: float32 [2048, 512], P('dp'), may hold values from -0.125 to 0.125
- output_weight: float32 [2048, 2048], P('mp', 'dp'), may hold values from -0.5 to 0.5
- gateup_weight: float32 [2, 2048, 5632], P(None, 'dp', 'mp'), may hold values from -0.125 to 0.125
- down_weight: float32 [5632, 2048], P('mp', 'dp'), may hold values from -0.078125 to 0.078125
- head_weight: float32 [2048, 32000], P('dp', 'mp'), may hold values from -0.22097087 to 0.22097087
- norm_gains: float32 [3, 2048], P(None, 'dp'), may hold values from 0.3 to 2.4
- embed_mean: float32 [32000, 2048], P('mp', 'dp'), may hold values from -4.7683716e-07 to 4.7683716e-07
- query_mean: float32 [2048, 2048], P('dp', 'mp'), may hold values from -4.7683716e-07 to 4.7683716e-07
- keyvalue_mean: float32 [2048, 512], P('dp'), may hold values from -4.7683716e-07 to 4.7683716e-07
- output_mean: float32 [2048, 2048], P('mp', 'dp'), may hold values from -4.7683716e-07 to 4.7683716e-07
- gateup_mean: float32 [2, 2048, 5632], P(None, 'dp', 'mp'), may hold values from -4.7683716e-07 to 4.7683716e-07
- down_mean: float32 [5632, 2048], P('mp', 'dp'), may hold values from -4.7683716e-07 to 4.7683716e-07
- head_mean: float32 [2048, 32000], P('dp', 'mp'), may hold values from -4.7683716e-07 to 4.7683716e-07
- gains_mean: float32 [3, 2048], P(None, 'dp'), may hold values from -4.7683716e-06 to 4.7683716e-06
- embed_square: float32 [32000, 2048], P('mp', 'dp'), may hold values from 3.0036832e-14 to 1.1991891e-13
- query_square: float32 [2048, 2048], P('dp', 'mp'), may hold values from 3.0036832e-14 to 1.1991891e-13
- keyvalue_square: float32 [2048, 512], P('dp'), may hold values from 3.0036832e-14 to 1.1991891e-13
- output_square: float32 [2048, 2048], P('mp', 'dp'), may hold values from 3.0036832e-14 to 1.1991891e-13
- gateup_square: float32 [2, 2048, 5632], P(None, 'dp', 'mp'), may hold values from 3.0036832e-14 to 1.1991891e-13
- down_square: float32 [5632, 2048], P('mp', 'dp'), may hold values from 3.0036832e-14 to 1.1991891e-13
- head_square: float32 [2048, 32000], P('dp', 'mp'), may hold values from 1.1991891e-13 to 4.7967565e-13
- gains_square: float32 [3, 2048], P(None, 'dp'), may hold values from 3.0036832e-12 to 1.1991891e-11
Outputs:
- loss_sum: float32 [], replicated
- weight_total: float32 [], replicated
- grad_norm: float32 [], replicated
- embed_final: float32 [32000, 2048], P('mp', 'dp')
- embed_clipped: float32 [32000, 2048], P('mp', 'dp')
- embed_square_out: float32 [32000, 2048], P('mp', 'dp')
- query_final: float32 [2048, 2048], P('dp', 'mp')
- query_mean_out: float32 [2048, 2048], P('dp', 'mp')
- query_square_out: float32 [2048, 2048], P('dp', 'mp')
- keyvalue_final: float32 [2048, 512], P('dp')
- keyvalue_mean_out: float32 [2048, 512], P('dp')
- keyvalue_square_out: float32 [2048, 512], P('dp')
- output_final: float32 [2048, 2048], P('mp', 'dp')
- output_mean_out: float32 [2048, 2048], P('mp', 'dp')
- output_square_out: float32 [2048, 2048], P('mp', 'dp')
- gateup_final: float32 [2, 2048, 5632], P(None, 'dp', 'mp')
- gateup_mean_out: float32 [2, 2048, 5632], P(None, 'dp', 'mp')
- gateup_square_out: float32 [2, 2048, 5632], P(None, 'dp', 'mp')
- down_final: float32 [5632, 2048], P('mp', 'dp')
- down_mean_out: float32 [5632, 2048], P('mp', 'dp')
- down_square_out: float32 [5632, 2048], P('mp', 'dp')
- head_final: float32 [2048, 32000], P('dp', 'mp')
- head_mean_out: float32 [2048, 32000], P('dp', 'mp')
- head_square_out: float32 [2048, 32000], P('dp', 'mp')
- gains_final: float32 [3, 2048], P(None, 'dp')
- gains_mean_out: float32 [3, 2048], P(None, 'dp')
- gains_square_out: float32 [3, 2048], P(None, 'dp')
All inputs are finite; a program needn't handle non-finite values.
Results may differ from a plain program's by a relative error of at most 0.023.
Values may be sent and summed in bfloat16 or wider, within the bound.
No kernel may reach another device: no remote copies, remote signals or barrier semaphores. Data moves between devices by JAX's collectives and lax.ppermute only.
A program may use at most 448 MiB of HBM per device.

v0:
```python
import jax
import jax.numpy as jnp
from jax import lax
from jax.sharding import PartitionSpec as P

HD = 64
KVH = 4
LEN = 1024
STEP = 5


EPS = 1e-05
SCALE = 0.125
CLIP = 0.01
BETA_ONE = 0.9
BETA_TWO = 0.95
ADAM_EPS = 1e-08
RATES = (0.9, 0.01, 0.01, 0.06, 0.01, 0.01, 0.08, 0.9)
DECAYS = (0.1, 0.1, 0.1, 0.1, 0.1, 0.1, 0.1, 0.0)


def combined_all(part, axis, combine):
    gathered = jax.tree.map(lambda a: lax.all_gather(a, axis), part)

    def take(source):
        return jax.tree.map(lambda a: lax.dynamic_index_in_dim(a, source, 0, False), gathered)

    return lax.fori_loop(
        1, lax.axis_size(axis), lambda source, state: combine(state, take(source)), take(0)
    )


def normed(hidden, gain):
    return hidden * lax.rsqrt(jnp.mean(hidden * hidden, axis=-1, keepdims=True) + EPS) * gain


def norm_back(hidden, gain, upstream):
    _, pullback = jax.vjp(normed, hidden, gain)
    return pullback(upstream)


def rotary_tables(length):
    positions = (jnp.arange(length) % LEN).astype(jnp.float32)
    freqs = 10000.0 ** (-(2 * jnp.arange(HD // 2)).astype(jnp.float32) / HD)
    angles = positions[:, None] * freqs[None, :]
    cosine = jnp.cos(angles)
    sine = jnp.sin(angles)
    return (jnp.concatenate([cosine, cosine], -1), jnp.concatenate([sine, sine], -1))


def rotate(values, cosine, sine):
    half = HD // 2
    turned = jnp.concatenate([-values[..., half:], values[..., :half]], -1)
    return values * cosine[:, None, :] + turned * sine[:, None, :]


def rotate_back(grads, cosine, sine):
    half = HD // 2
    shifted = grads * sine[:, None, :]
    turned = jnp.concatenate([shifted[..., half:], -shifted[..., :half]], -1)
    return grads * cosine[:, None, :] + turned


def spread(shard, gain):
    return lax.all_gather(normed(shard, gain).astype(jnp.bfloat16), "mp", axis=0, tiled=True)


def regather(shard, gain):
    return lax.all_gather(normed(shard, gain).astype(jnp.bfloat16), "mp", axis=0, tiled=True)


def collect(partial_value):
    return lax.psum_scatter(
        partial_value.astype(jnp.bfloat16), "mp", scatter_dimension=0, tiled=True
    ).astype(jnp.float32)


def collect_grad(partial_value):
    return lax.psum_scatter(
        partial_value.astype(jnp.bfloat16), "mp", scatter_dimension=0, tiled=True
    ).astype(jnp.float32)


def spread_grad(shard):
    return lax.all_gather(shard.astype(jnp.bfloat16), "mp", axis=0, tiled=True)


def project(inputs, query_full, keyvalue_full):
    head_kv = lax.axis_index("mp") * KVH // lax.axis_size("mp")
    rows = inputs.shape[0]
    cosine, sine = rotary_tables(rows)
    key_cols = lax.dynamic_slice_in_dim(keyvalue_full, head_kv * HD, HD, 1)
    value_cols = lax.dynamic_slice_in_dim(keyvalue_full, (KVH + head_kv) * HD, HD, 1)
    columns = jnp.concatenate([key_cols, value_cols], 1)
    queries_pre = jnp.dot(inputs, query_full, preferred_element_type=jnp.float32).reshape(
        rows, -1, HD
    )
    pairs = jnp.dot(inputs, columns, preferred_element_type=jnp.float32)
    queries = rotate(queries_pre, cosine, sine).astype(jnp.bfloat16)
    keys = rotate(pairs[:, None, :HD], cosine, sine)[:, 0].astype(jnp.bfloat16)
    values = pairs[:, HD:].astype(jnp.bfloat16)
    return (queries, keys, values, columns, head_kv, cosine, sine)


def block_parts(start, queries, keys, values):
    size = min(512, LEN)
    anchor = start // LEN * LEN
    chosen = lax.dynamic_slice_in_dim(queries, start, size, 0)
    scores = jnp.einsum("qhd,kd->hqk", chosen, keys, preferred_element_type=jnp.float32) * SCALE
    places = start - anchor + jnp.arange(size)
    causal = jnp.arange(LEN)[None, :] <= places[:, None]
    masked = jnp.where(causal[None], scores, -1e30)
    return (chosen, keys, values, masked, anchor)


def attend(queries, keys, values):
    size = min(512, LEN)

    def one_block(index):
        chosen, keys_seq, values_seq, masked, anchor = block_parts(
            index * size, queries, keys, values
        )
        peak = jnp.max(masked, -1, keepdims=True)
        expo = jnp.exp(masked - peak)
        total = jnp.sum(expo, -1, keepdims=True)
        probs = (expo / total).astype(jnp.bfloat16)
        mixed = jnp.einsum("hqk,kd->qhd", probs, values_seq, preferred_element_type=jnp.float32)
        return (mixed.astype(jnp.bfloat16), (peak + jnp.log(total))[..., 0])

    mixed, logsum = lax.map(one_block, jnp.arange(queries.shape[0] // size))
    return (mixed.reshape(queries.shape), logsum)


def attend_back(queries, keys, values, out_grad, logsum):
    size = min(512, LEN)
    rows = queries.shape[0]

    def one_block(carry, index):
        key_acc, value_acc = carry
        start = index * size
        chosen, keys_seq, values_seq, masked, anchor = block_parts(start, queries, keys, values)
        probs = jnp.exp(masked - logsum[index][..., None])
        grad_block = lax.dynamic_slice_in_dim(out_grad, start, size, 0)
        prob_grad = jnp.einsum(
            "qhd,kd->hqk", grad_block, values_seq, preferred_element_type=jnp.float32
        )
        inner = jnp.sum(probs * prob_grad, -1, keepdims=True)
        score_grad = (probs * (prob_grad - inner)).astype(jnp.bfloat16)
        query_grad = (
            jnp.einsum("hqk,kd->qhd", score_grad, keys_seq, preferred_element_type=jnp.float32)
            * SCALE
        )
        key_part = (
            jnp.einsum("hqk,qhd->kd", score_grad, chosen, preferred_element_type=jnp.float32)
            * SCALE
        )
        value_part = jnp.einsum(
            "hqk,qhd->kd",
            probs.astype(jnp.bfloat16),
            grad_block,
            preferred_element_type=jnp.float32,
        )
        key_acc = key_acc + key_part
        value_acc = value_acc + value_part
        return ((key_acc, value_acc), query_grad)

    zeros = jnp.zeros((rows, HD), jnp.float32)
    (key_grad, value_grad), query_grad = lax.scan(
        one_block, (zeros, zeros), jnp.arange(rows // size)
    )
    return (query_grad.reshape(rows, -1, HD), key_grad, value_grad)


def merge_totals(first, second):
    top = jnp.maximum(first[0], second[0])
    summed = first[1] * jnp.exp(first[0] - top) + second[1] * jnp.exp(second[0] - top)
    return (top, summed, first[2] + second[2])


def adamw(weight, grad, mean_old, square_old, factor, rate, decay):
    clipped = grad * factor
    mean_new = BETA_ONE * mean_old + (1 - BETA_ONE) * clipped
    square_new = BETA_TWO * square_old + (1 - BETA_TWO) * clipped * clipped
    ratio = (
        mean_new / (1 - BETA_ONE**STEP) / (jnp.sqrt(square_new / (1 - BETA_TWO**STEP)) + ADAM_EPS)
    )
    return (weight - rate * (ratio + decay * weight), mean_new, square_new)


def body(
    tokens,
    targets,
    select,
    bucket,
    embed_table,
    query_weight,
    keyvalue_weight,
    output_weight,
    gateup_weight,
    down_weight,
    head_weight,
    norm_gains,
    embed_mean,
    query_mean,
    keyvalue_mean,
    output_mean,
    gateup_mean,
    down_mean,
    head_mean,
    gains_mean,
    embed_square,
    query_square,
    keyvalue_square,
    output_square,
    gateup_square,
    down_square,
    head_square,
    gains_square,
):
    bf16 = jnp.bfloat16
    f32 = jnp.float32
    (
        embed_full,
        query_full,
        keyvalue_full,
        output_full,
        gateup_full,
        down_full,
        head_full,
        gains_full,
    ) = (
        lax.all_gather(embed_table.astype(bf16), "dp", axis=1, tiled=True),
        lax.all_gather(query_weight.astype(bf16), "dp", axis=0, tiled=True),
        lax.all_gather(keyvalue_weight.astype(bf16), "dp", axis=0, tiled=True),
        lax.all_gather(output_weight.astype(bf16), "dp", axis=1, tiled=True),
        lax.all_gather(gateup_weight.astype(bf16), "dp", axis=1, tiled=True),
        lax.all_gather(down_weight.astype(bf16), "dp", axis=1, tiled=True),
        lax.all_gather(head_weight.astype(bf16), "dp", axis=0, tiled=True),
        lax.all_gather(norm_gains.astype(bf16), "dp", axis=1, tiled=True),
    )
    gains_rows = gains_full.astype(f32)
    group = lax.axis_index("mp")
    rows = tokens.shape[0]
    vocab_part = embed_full.shape[0]
    vocab_start = group * vocab_part
    local_ids = tokens - vocab_start
    inside = (local_ids >= 0) & (local_ids < vocab_part)
    looked = jnp.where(
        inside[:, None], embed_full[jnp.clip(local_ids, 0, vocab_part - 1)], 0
    ).astype(f32)
    start_rows = collect(looked)
    first_in = spread(start_rows, gains_rows[0])
    queries, keys, values, columns, head_kv, cosine, sine = project(
        first_in, query_full, keyvalue_full
    )
    mixed, logsum = attend(queries, keys, values)
    middle_rows = start_rows + collect(
        jnp.dot(mixed.reshape(rows, -1), output_full, preferred_element_type=f32)
    )
    second_in = spread(middle_rows, gains_rows[1])
    gate = jnp.dot(second_in, gateup_full[0], preferred_element_type=f32)
    upper = jnp.dot(second_in, gateup_full[1], preferred_element_type=f32)
    active = (jax.nn.silu(gate) * upper).astype(bf16)
    final_rows = middle_rows + collect(jnp.dot(active, down_full, preferred_element_type=f32))
    final_in = spread(final_rows, gains_rows[2])
    logits = jnp.dot(final_in, head_full, preferred_element_type=f32)
    hits = jnp.arange(vocab_part)[None, :] == (targets - vocab_start)[:, None]
    local_top = jnp.max(logits, -1)
    top, expsum, picked = combined_all(
        (
            local_top,
            jnp.sum(jnp.exp(logits - local_top[:, None]), -1),
            jnp.sum(jnp.where(hits, logits, 0.0), -1),
        ),
        "mp",
        merge_totals,
    )
    logsum_all = top + jnp.log(expsum)
    scales = (select * bucket).astype(f32)
    loss_sum, weight_total = lax.psum(
        (jnp.sum(scales * (logsum_all - picked)), jnp.sum(scales)), "dp"
    )
    coef = scales * (1.0 / weight_total)
    logit_grad = (
        (jnp.exp(logits - logsum_all[:, None]) - hits.astype(f32)) * coef[:, None]
    ).astype(bf16)
    final_back = regather(final_rows, gains_rows[2])
    second_back = regather(middle_rows, gains_rows[1])
    first_back = regather(start_rows, gains_rows[0])
    head_grad = jnp.einsum("td,tv->dv", final_back, logit_grad, preferred_element_type=f32)
    final_grad = collect_grad(
        jnp.einsum("tv,dv->td", logit_grad, head_full, preferred_element_type=f32)
    )
    residual, final_gain = norm_back(final_rows, gains_rows[2], final_grad)
    branch = spread_grad(residual)
    gate = jnp.dot(second_back, gateup_full[0], preferred_element_type=f32)
    upper = jnp.dot(second_back, gateup_full[1], preferred_element_type=f32)
    sigmoid = jax.nn.sigmoid(gate)
    silu_gate = jax.nn.silu(gate)
    active = (silu_gate * upper).astype(bf16)
    active_grad = jnp.einsum("td,fd->tf", branch, down_full, preferred_element_type=f32)
    down_grad = jnp.einsum("tf,td->fd", active, branch, preferred_element_type=f32)
    gate_grad = (active_grad * upper * sigmoid * (1.0 + gate * (1.0 - sigmoid))).astype(bf16)
    upper_grad = (active_grad * silu_gate).astype(bf16)
    gateup_grad = jnp.stack(
        [
            jnp.einsum("td,tf->df", second_back, gate_grad, preferred_element_type=f32),
            jnp.einsum("td,tf->df", second_back, upper_grad, preferred_element_type=f32),
        ]
    )
    second_grad = collect_grad(
        jnp.einsum("tf,df->td", gate_grad, gateup_full[0], preferred_element_type=f32)
        + jnp.einsum("tf,df->td", upper_grad, gateup_full[1], preferred_element_type=f32)
    )
    middle_extra, middle_gain = norm_back(middle_rows, gains_rows[1], second_grad)
    residual = residual + middle_extra
    branch = spread_grad(residual)
    queries, keys, values, columns, head_kv, cosine, sine = project(
        first_back, query_full, keyvalue_full
    )
    mixed, logsum = attend(queries, keys, values)
    mixed_flat = mixed.reshape(rows, -1)
    output_grad = jnp.einsum("tc,td->cd", mixed_flat, branch, preferred_element_type=f32)
    mixed_grad = jnp.einsum("td,cd->tc", branch, output_full, preferred_element_type=f32).astype(
        bf16
    )
    query_grad, key_grad, value_grad = attend_back(
        queries, keys, values, mixed_grad.reshape(rows, -1, HD), logsum
    )
    query_pre = rotate_back(query_grad, cosine, sine).astype(bf16).reshape(rows, -1)
    pair_grad = jnp.concatenate(
        [rotate_back(key_grad[:, None], cosine, sine)[:, 0], value_grad], 1
    ).astype(bf16)
    query_grad_w = jnp.einsum("td,tc->dc", first_back, query_pre, preferred_element_type=f32)
    pair_weight = jnp.einsum("td,tc->dc", first_back, pair_grad, preferred_element_type=f32)
    keyvalue_grad = jnp.zeros((pair_weight.shape[0], 2 * KVH * HD), f32)
    keyvalue_grad = lax.dynamic_update_slice_in_dim(
        keyvalue_grad, pair_weight[:, :HD], head_kv * HD, 1
    )
    keyvalue_grad = lax.dynamic_update_slice_in_dim(
        keyvalue_grad, pair_weight[:, HD:], (KVH + head_kv) * HD, 1
    )
    first_grad = collect_grad(
        jnp.einsum("tc,dc->td", query_pre, query_full, preferred_element_type=f32)
        + jnp.einsum("tc,dc->td", pair_grad, columns, preferred_element_type=f32)
    )
    start_extra, start_gain = norm_back(start_rows, gains_rows[0], first_grad)
    start_grad = spread_grad(residual + start_extra)
    gains_grad = jnp.stack([start_gain, middle_gain, final_gain])
    embed_grad = (
        jnp.zeros((vocab_part, start_grad.shape[1]), f32)
        .at[jnp.where(inside, local_ids, vocab_part)]
        .add(start_grad.astype(f32), mode="drop")
    )
    (
        embed_part,
        query_part,
        keyvalue_part,
        output_part,
        gateup_part,
        down_part,
        head_part,
        gains_part,
    ) = (
        lax.psum_scatter(
            embed_grad.astype(jnp.bfloat16), "dp", scatter_dimension=1, tiled=True
        ).astype(jnp.float32),
        lax.psum_scatter(
            query_grad_w.astype(jnp.bfloat16), "dp", scatter_dimension=0, tiled=True
        ).astype(jnp.float32),
        lax.psum_scatter(
            keyvalue_grad.astype(jnp.bfloat16), "dp", scatter_dimension=0, tiled=True
        ).astype(jnp.float32),
        lax.psum_scatter(
            output_grad.astype(jnp.bfloat16), "dp", scatter_dimension=1, tiled=True
        ).astype(jnp.float32),
        lax.psum_scatter(
            gateup_grad.astype(jnp.bfloat16), "dp", scatter_dimension=1, tiled=True
        ).astype(jnp.float32),
        lax.psum_scatter(
            down_grad.astype(jnp.bfloat16), "dp", scatter_dimension=1, tiled=True
        ).astype(jnp.float32),
        lax.psum_scatter(
            head_grad.astype(jnp.bfloat16), "dp", scatter_dimension=0, tiled=True
        ).astype(jnp.float32),
        lax.psum_scatter(
            gains_grad.astype(jnp.bfloat16), "dp", scatter_dimension=1, tiled=True
        ).astype(jnp.float32),
    )
    keyvalue_part, gains_part = (
        lax.psum(keyvalue_part.astype(jnp.bfloat16), "mp").astype(jnp.float32),
        lax.psum(gains_part.astype(jnp.bfloat16), "mp").astype(jnp.float32),
    )
    leading = (group == 0).astype(f32)
    squared = sum(
        (
            jnp.sum(piece * piece)
            for piece in (embed_part, query_part, output_part, gateup_part, down_part, head_part)
        )
    )
    squared = squared + leading * (
        jnp.sum(keyvalue_part * keyvalue_part) + jnp.sum(gains_part * gains_part)
    )
    grad_norm = jnp.sqrt(lax.psum(squared, ("dp", "mp")))
    factor = jnp.minimum(1.0, CLIP / (grad_norm + 1e-06))
    embed_out = adamw(
        embed_table, embed_part, embed_mean, embed_square, factor, RATES[0], DECAYS[0]
    )
    query_out = adamw(
        query_weight, query_part, query_mean, query_square, factor, RATES[1], DECAYS[1]
    )
    keyvalue_out = adamw(
        keyvalue_weight, keyvalue_part, keyvalue_mean, keyvalue_square, factor, RATES[2], DECAYS[2]
    )
    output_out = adamw(
        output_weight, output_part, output_mean, output_square, factor, RATES[3], DECAYS[3]
    )
    gateup_out = adamw(
        gateup_weight, gateup_part, gateup_mean, gateup_square, factor, RATES[4], DECAYS[4]
    )
    down_out = adamw(down_weight, down_part, down_mean, down_square, factor, RATES[5], DECAYS[5])
    head_out = adamw(head_weight, head_part, head_mean, head_square, factor, RATES[6], DECAYS[6])
    gains_out = adamw(norm_gains, gains_part, gains_mean, gains_square, factor, RATES[7], DECAYS[7])
    embed_clipped = embed_part * factor
    return (
        loss_sum,
        weight_total,
        grad_norm,
        embed_out[0],
        embed_clipped,
        embed_out[2],
        query_out[0],
        query_out[1],
        query_out[2],
        keyvalue_out[0],
        keyvalue_out[1],
        keyvalue_out[2],
        output_out[0],
        output_out[1],
        output_out[2],
        gateup_out[0],
        gateup_out[1],
        gateup_out[2],
        down_out[0],
        down_out[1],
        down_out[2],
        head_out[0],
        head_out[1],
        head_out[2],
        gains_out[0],
        gains_out[1],
        gains_out[2],
    )


def solution(mesh):
    in_specs = (
        P("dp"),
        P("dp"),
        P("dp"),
        P("dp"),
        P("mp", "dp"),
        P("dp", "mp"),
        P("dp", None),
        P("mp", "dp"),
        P(None, "dp", "mp"),
        P("mp", "dp"),
        P("dp", "mp"),
        P(None, "dp"),
        P("mp", "dp"),
        P("dp", "mp"),
        P("dp", None),
        P("mp", "dp"),
        P(None, "dp", "mp"),
        P("mp", "dp"),
        P("dp", "mp"),
        P(None, "dp"),
        P("mp", "dp"),
        P("dp", "mp"),
        P("dp", None),
        P("mp", "dp"),
        P(None, "dp", "mp"),
        P("mp", "dp"),
        P("dp", "mp"),
        P(None, "dp"),
    )
    out_specs = (
        P(),
        P(),
        P(),
        P("mp", "dp"),
        P("mp", "dp"),
        P("mp", "dp"),
        P("dp", "mp"),
        P("dp", "mp"),
        P("dp", "mp"),
        P("dp", None),
        P("dp", None),
        P("dp", None),
        P("mp", "dp"),
        P("mp", "dp"),
        P("mp", "dp"),
        P(None, "dp", "mp"),
        P(None, "dp", "mp"),
        P(None, "dp", "mp"),
        P("mp", "dp"),
        P("mp", "dp"),
        P("mp", "dp"),
        P("dp", "mp"),
        P("dp", "mp"),
        P("dp", "mp"),
        P(None, "dp"),
        P(None, "dp"),
        P(None, "dp"),
    )
    return jax.shard_map(body, mesh=mesh, in_specs=in_specs, out_specs=out_specs, check_vma=False)
```

profile of v0, /device:TPU:0, one launch (start us, length us, event | category | flops | bytes accessed | tf_op | source)
XLA Modules:
  0.0 2896.8 jit_solution(12342428335376877957)
XLA Ops:
  13.7 166.1 %all-gather.17.cloned.1.call-done = bf16[8000,2048]{1,0:T(8,128)(2,1)} async-done(((bf16[8000,256]{1,0:T(8,128)(2,1)}), bf16[8000,2048]{1,0:T(8,128)(2,1)}) %all-gather.17.cloned.1.call-update) | async-done | bytes 32768016 | tf_op jit(solution)/shard_map/all_gather | solution.py:232
  179.8 44.5 %gather_fusion = bf16[1024,2048]{1,0:T(8,128)(2,1)} fusion(bf16[8000,2048]{1,0:T(8,128)(2,1)} %all-gather.17.cloned.1.call-done, s32[1024]{0:T(1024)S(1)} %get-tuple-element.678), kind=kCustom, calls=%fused_computation | custom fusion | bytes 8392704 | tf_op jit(solution)/shard_map/gather | solution.py:249
  241.1 68.7 %reduce-scatter.17.cloned.1.call-done = bf16[256,2048]{1,0:T(8,128)(2,1)} async-done(((bf16[1024,2048]{1,0:T(8,128)(2,1)}), bf16[256,2048]{1,0:T(8,128)(2,1)}) %reduce-scatter.17.cloned.1.call-update) | async-done | bytes 1048592 | tf_op jit(solution)/shard_map/reduce_scatter | solution.py:73
  342.4 81.3 %all-gather.19.cloned.1.call-done = bf16[1024,2048]{1,0:T(8,128)(2,1)} async-done(((bf16[256,2048]{1,0:T(8,128)(2,1)}), bf16[1024,2048]{1,0:T(8,128)(2,1)}) %all-gather.19.cloned.1.call-update) | async-done | bytes 4194320 | tf_op jit(solution)/shard_map/all_gather | solution.py:65
  427.6 25.0 all-gather.21.cloned.1.call-done
  459.0 80.8 %while.62 = (s32[]{:T(128)}, bf16[2,512,8,64]{1,3,2,0:T(8,128)(2,1)S(1)}, s32[2]{0:T(128)S(1)}, bf16[1024,8,64]{0,2,1:T(8,128)(2,1)S(1)}, bf16[1024,64]{0,1:T(8,...) while((s32[]{:T(128)}, ...), condition=%wide.region_5.6_spmd, body=%wide.region_2.5_spmd.sunk | while | flops 1108084224 | bytes 69505376 | solution.py:130
  550.5 73.6 %reduce-scatter.19.cloned.1.call-done = bf16[256,2048]{1,0:T(8,128)(2,1)} async-done(((bf16[1024,2048]{1,0:T(8,128)(2,1)}), bf16[256,2048]{1,0:T(8,128)(2,1)}) %reduce-scatter.19.cloned.1.call-update) | async-done | bytes 1048592 | tf_op jit(solution)/shard_map/reduce_scatter | solution.py:73
  630.7 64.2 %all-gather.29.cloned.1.call-done = bf16[2,2048,1408]{2,1,0:T(8,128)(2,1)} async-done(((bf16[2,256,1408]{2,1,0:T(8,128)(2,1)}), bf16[2,2048,1408]{2,1,0:T(8,128)(2,1)}) %all-gather.29.cloned.1.call-update) | async-done | bytes 11534352 | tf_op jit(solution)/shard_map/all_gather | solution.py:236
  694.9 82.9 %all-gather.27.cloned.1.call-done = bf16[1024,2048]{1,0:T(8,128)(2,1)} async-done(((bf16[256,2048]{1,0:T(8,128)(2,1)}), bf16[1024,2048]{1,0:T(8,128)(2,1)}) %all-gather.27.cloned.1.call-update) | async-done | bytes 4194320 | tf_op jit(solution)/shard_map/all_gather | solution.py:65
  839.8 71.1 %reduce-scatter.21.cloned.1.call-done = bf16[256,2048]{1,0:T(8,128)(2,1)} async-done(((bf16[1024,2048]{1,0:T(8,128)(2,1)}), bf16[256,2048]{1,0:T(8,128)(2,1)}) %reduce-scatter.21.cloned.1.call-update) | async-done | bytes 1048592 | tf_op jit(solution)/shard_map/reduce_scatter | solution.py:73
  915.6 162.2 %all-gather.35.cloned.1.call-done = bf16[2048,8000]{0,1:T(8,128)(2,1)} async-done(((bf16[256,8000]{0,1:T(8,128)(2,1)}), bf16[2048,8000]{0,1:T(8,128)(2,1)}) %all-gather.35.cloned.1.call-update) | async-done | bytes 32768016 | tf_op jit(solution)/shard_map/all_gather | solution.py:238
  1077.8 83.0 %all-gather.33.cloned.1.call-done = bf16[1024,2048]{1,0:T(8,128)(2,1)} async-done(((bf16[256,2048]{1,0:T(8,128)(2,1)}), bf16[1024,2048]{1,0:T(8,128)(2,1)}) %all-gather.33.cloned.1.call-update) | async-done | bytes 4194320 | tf_op jit(solution)/shard_map/all_gather | solution.py:65
  1160.8 42.3 %fusion.162 = (f32[1024]{0:T(1024)S(1)}, f32[1024,8000]{0,1:T(8,128)}) fusion(bf16[1024,2048]{1,0:T(8,128)(2,1)} %all-gather.33.cloned.1.call-done, bf16[2048,8000]{0,1:T(8,128)(2,1)} %all-gather.35.cloned.1.call-done), kind=kOutput, calls=%fused_computation.283 | convolution fusion | flops 33562624000 | bytes 69734400 | tf_op jit(solution)/shard_map/dot_general | solution.py:266
  1272.3 44.7 %convolution_convert_fusion.4 = bf16[1024,2048]{1,0:T(8,128)(2,1)} fusion(bf16[2048,8000]{0,1:T(8,128)(2,1)} %all-gather.35.cloned.1.call-done, f32[1024,8000]{0,1:T(8,128)} %get-tuple-element.682, f32[1024]{0:T(1024)S(1)} %convert_multiply_fusion.26, f32[1024]{0:T(1024)S(1)} %get-tuple-element.646, s32[1024]{0:T(1024)S(1)} %broadcast_subtract_fusion), kind=kOutput, calls=%fused_computation.129 | convolution fusion | flops 33605681152 | bytes 69742592 | tf_op jit(solution)/shard_map/tv,dv->td/dot_general | solution.py:292
  1317.0 74.3 %reduce-scatter.23.cloned.1.call-done = bf16[256,2048]{1,0:T(8,128)(2,1)} async-done(((bf16[1024,2048]{1,0:T(8,128)(2,1)}), bf16[256,2048]{1,0:T(8,128)(2,1)}) %reduce-scatter.23.cloned.1.call-update) | async-done | bytes 1048592 | tf_op jit(solution)/shard_map/reduce_scatter | solution.py:79
  1396.5 81.4 %all-gather.37.cloned.1.call-done = bf16[1024,2048]{1,0:T(8,128)(2,1)} async-done(((bf16[256,2048]{1,0:T(8,128)(2,1)}), bf16[1024,2048]{1,0:T(8,128)(2,1)}) %all-gather.37.cloned.1.call-update) | async-done | bytes 4194320 | tf_op jit(solution)/shard_map/all_gather | solution.py:85
  1515.8 75.4 %reduce-scatter.25.cloned.1.call-done = bf16[256,2048]{1,0:T(8,128)(2,1)} async-done(((bf16[1024,2048]{1,0:T(8,128)(2,1)}), bf16[256,2048]{1,0:T(8,128)(2,1)}) %reduce-scatter.25.cloned.1.call-update) | async-done | bytes 1048592 | tf_op jit(solution)/shard_map/reduce_scatter | solution.py:79
  1599.2 30.9 %while.64 = (s32[]{:T(128)}, bf16[2,512,8,64]{1,3,2,0:T(8,128)(2,1)S(1)}, f32[2,8,512]{2,1,0:T(8,128)S(1)}, s32[2]{0:T(128)S(1)}, bf16[1024,8,64]{0,2,1:T(8,128)...) while((s32[]{:T(128)}, ...), condition=%wide.region_26.27_spmd, body=%wide.region_23.26_spmd.sunk | while | flops 1124856320 | bytes 53875060 | solution.py:130
  1631.1 49.4 %all-gather.39.cloned.1.call-done = bf16[1024,2048]{1,0:T(8,128)(2,1)} async-done(((bf16[256,2048]{1,0:T(8,128)(2,1)}), bf16[1024,2048]{1,0:T(8,128)(2,1)}) %all-gather.39.cloned.1.call-update) | async-done | bytes 4194320 | tf_op jit(solution)/shard_map/all_gather | solution.py:85
  1685.7 148.5 %while.65 = (s32[]{:T(128)}, f32[1024,64]{0,1:T(8,128)}, f32[1024,64]{0,1:T(8,128)}, f32[2,512,8,64]{1,0,3,2:T(2,128)}, s32[2]{0:T(128)S(1)}, /*index=5*/bf16[10...) while((s32[]{:T(128)}, f32[1024,64]{0,1:T(8,128)}, ...), condition=%wide.region_29.30_spmd.clone, body=%wide.region_27.29_spmd.clone.sunk | while | flops 2723213824 | bytes 234050464 | solution.py:168
  1864.8 59.3 %reduce-scatter.27.cloned.1.call-done = bf16[256,2048]{1,0:T(8,128)(2,1)} async-done(((bf16[1024,2048]{1,0:T(8,128)(2,1)}), bf16[256,2048]{1,0:T(8,128)(2,1)}) %reduce-scatter.27.cloned.1.call-update) | async-done | bytes 1048592 | tf_op jit(solution)/shard_map/reduce_scatter | solution.py:79
  1978.4 46.3 %convolution_convert_fusion = bf16[2048,8000]{0,1:T(8,128)(2,1)} fusion(bf16[1024,2048]{1,0:T(8,128)(2,1)} %all-gather.33.cloned.1.call-done, f32[1024,8000]{0,1:T(8,128)} %get-tuple-element.682, f32[1024]{0:T(1024)S(1)} %copy-done.89, f32[1024]{0:T(1024)S(1)} %copy-done.87, s32[1024]{0:T(1024)S(1)} %copy-done.71), kind=kOutput, calls=%fused_computation.87 | convolution fusion | flops 33619968000 | bytes 69742592 | tf_op jit(solution)/shard_map/td,tv->dv/dot_general | solution.py:290
  2059.1 62.1 %scatter_custom_fusion = f32[8000,2048]{1,0:T(8,128)} fusion(s32[1024]{0:T(1024)S(1)} %get-tuple-element.544, f32[]{:T(128)} %constant.403.clone.1, f32[1024,2048]{1,0:T(8,128)} %convert_element_type.282, s32[1024]{0:T(1024)S(1)} %broadcast_clamp_fusion), kind=kCustom, calls=%fused_computation.82 | custom fusion | flops 2097152 | bytes 65536512 | tf_op jit(solution)/shard_map/scatter-add | solution.py:353
  2121.2 37.4 %convert_element_type.283 = bf16[8000,2048]{1,0:T(8,128)(2,1)} convert(f32[8000,2048]{1,0:T(8,128)} %scatter_custom_fusion) | non-fusion elementwise | flops 16384000 | bytes 98304000 | tf_op jit(solution)/shard_map/convert_element_type | solution.py:366
  2160.7 44.2 %reduce-scatter.35.cloned.1.call-done = bf16[2,256,1408]{2,1,0:T(8,128)(2,1)} async-done(((bf16[2,2048,1408]{2,1,0:T(8,128)(2,1)}), bf16[2,256,1408]{2,1,0:T(8,128)(2,1)}) %reduce-scatter.35.cloned.1.call-update) | async-done | bytes 1441808 | tf_op jit(solution)/shard_map/reduce_scatter | solution.py:377
  2207.7 42.4 %reduce-scatter.31.cloned.1.call-done = bf16[256,512]{1,0:T(8,128)(2,1)} async-done(((bf16[2048,512]{1,0:T(8,128)(2,1)}), bf16[256,512]{1,0:T(8,128)(2,1)}) %reduce-scatter.31.cloned.1.call-update) | async-done | bytes 262160 | tf_op jit(solution)/shard_map/reduce_scatter | solution.py:368
  2251.8 43.6 %reduce-scatter.33.cloned.1.call-done = bf16[512,256]{1,0:T(8,128)(2,1)} async-done(((bf16[512,2048]{1,0:T(8,128)(2,1)}), bf16[512,256]{1,0:T(8,128)(2,1)}) %reduce-scatter.33.cloned.1.call-update) | async-done | bytes 262160 | tf_op jit(solution)/shard_map/reduce_scatter | solution.py:374
  2297.1 36.0 %all-reduce.3.cloned.1.call-done = bf16[256,512]{1,0:T(8,128)(2,1)} async-done(((bf16[256,512]{1,0:T(8,128)(2,1)}), bf16[256,512]{1,0:T(8,128)(2,1)}) %all-reduce.3.cloned.1.call-update) | async-done | bytes 262160 | tf_op jit(solution)/shard_map/psum | solution.py:391
  2334.8 36.0 %reduce-scatter.43.cloned.1.call-done = bf16[256,3]{1,0:T(8,128)(2,1)} async-done(((bf16[2048,3]{1,0:T(8,128)(2,1)}), bf16[256,3]{1,0:T(8,128)(2,1)}) %reduce-scatter.43.cloned.1.call-update) | async-done | bytes 1552
  2385.4 190.8 %reduce-scatter.39.cloned.1.call-done = bf16[256,8000]{0,1:T(8,128)(2,1)} async-done(((bf16[2048,8000]{0,1:T(8,128)(2,1)}), bf16[256,8000]{0,1:T(8,128)(2,1)}) %reduce-scatter.39.cloned.1.call-update) | async-done | bytes 4096016 | tf_op jit(solution)/shard_map/reduce_scatter | solution.py:383
  2581.0 200.6 %reduce-scatter.29.cloned.1.call-done = bf16[8000,256]{1,0:T(8,128)(2,1)} async-done(((bf16[8000,2048]{1,0:T(8,128)(2,1)}), bf16[8000,256]{1,0:T(8,128)(2,1)}) %reduce-scatter.29.cloned.1.call-update) | async-done | bytes 4096016 | tf_op jit(solution)/shard_map/reduce_scatter | solution.py:365
  2790.4 39.6 %psum.39 = f32[]{:T(128)} all-reduce(f32[]{:T(128)S(6)} %add.512), channel_id=1, replica_groups=mesh['dp'=8,'mp'=4] {'dp','mp'}, use_global_device_ids=true, to_apply=%region_54.55 | all-reduce | flops 1 | bytes 8 | tf_op jit(solution)/shard_map/psum | solution.py:404
  (505 shorter events, 735.1 us)
Async XLA Ops:
  7.2 172.6 %all-gather.17.cloned.1.call-start = ((), (), s32[]{:S(2)}) async-start(), calls=%async_computation.14 | async-start | bytes 36864000 | tf_op jit(solution)/shard_map/all_gather | solution.py:232
  13.0 296.8 %reduce-scatter.17.cloned.1.call-start = ((), (), s32[]{:S(2)}) async-start(), calls=%async_computation.15 | async-start | bytes 5242880 | tf_op jit(solution)/shard_map/reduce_scatter | solution.py:73
  228.9 112.0 %all-gather.23.cloned.1.call-start = ((), (), s32[]{:S(2)}) async-start(), calls=%async_computation.18 | async-start | bytes 2359296 | tf_op jit(solution)/shard_map/all_gather | solution.py:234
  230.6 193.1 %all-gather.19.cloned.1.call-start = ((), (), s32[]{:S(2)}) async-start(), calls=%async_computation.16 | async-start | bytes 5242880 | tf_op jit(solution)/shard_map/all_gather | solution.py:65
  313.9 138.8 %all-gather.21.cloned.1.call-start = ((), (), s32[]{:S(2)}) async-start(), calls=%async_computation.17 | async-start | bytes 2359296 | tf_op jit(solution)/shard_map/all_gather | solution.py:233
  314.7 226.6 %all-gather.25.cloned.1.call-start = ((), (), s32[]{:S(2)}) async-start(), calls=%async_computation.19 | async-start | bytes 2359296 | tf_op jit(solution)/shard_map/all_gather | solution.py:235
  315.5 308.7 %reduce-scatter.19.cloned.1.call-start = ((), (), s32[]{:S(2)}) async-start(), calls=%async_computation.20 | async-start | bytes 5242880 | tf_op jit(solution)/shard_map/reduce_scatter | solution.py:73
  547.3 147.6 %all-gather.29.cloned.1.call-start = ((), (), s32[]{:S(2)}) async-start(), calls=%async_computation.22 | async-start | bytes 12976128 | tf_op jit(solution)/shard_map/all_gather | solution.py:236
  550.5 227.4 %all-gather.27.cloned.1.call-start = ((), (), s32[]{:S(2)}) async-start(), calls=%async_computation.21 | async-start | bytes 5242880 | tf_op jit(solution)/shard_map/all_gather | solution.py:65
  629.6 193.5 %all-gather.31.cloned.1.call-start = ((), (), s32[]{:S(2)}) async-start(), calls=%async_computation.23 | async-start | bytes 6488064 | tf_op jit(solution)/shard_map/all_gather | solution.py:237
  630.6 280.3 %reduce-scatter.21.cloned.1.call-start = ((), (), s32[]{:S(2)}) async-start(), calls=%async_computation.24 | async-start | bytes 5242880 | tf_op jit(solution)/shard_map/reduce_scatter | solution.py:73
  834.0 243.9 %all-gather.35.cloned.1.call-start = ((), (), s32[]{:S(2)}) async-start(), calls=%async_computation.26 | async-start | bytes 36864000 | tf_op jit(solution)/shard_map/all_gather | solution.py:238
  839.7 321.1 %all-gather.33.cloned.1.call-start = ((), (), s32[]{:S(2)}) async-start(), calls=%async_computation.25 | async-start | bytes 5242880 | tf_op jit(solution)/shard_map/all_gather | solution.py:65
  915.5 475.8 %reduce-scatter.23.cloned.1.call-start = ((), (), s32[]{:S(2)}) async-start(), calls=%async_computation.27 | async-start | bytes 5242880 | tf_op jit(solution)/shard_map/reduce_scatter | solution.py:79
  915.6 356.1 %copy-start.70 = (s32[1024]{0:T(1024)}, s32[1024]{0:T(1024)S(1)}, u32[]{:S(2)}) copy-start(s32[1024]{0:T(1024)S(1)} %broadcast_subtract_fusion) | copy-start | bytes 12292
  1316.9 160.9 %all-gather.37.cloned.1.call-start = ((), (), s32[]{:S(2)}) async-start(), calls=%async_computation.28 | async-start | bytes 5242880 | tf_op jit(solution)/shard_map/all_gather | solution.py:85
  1396.4 194.8 %reduce-scatter.25.cloned.1.call-start = ((), (), s32[]{:S(2)}) async-start(), calls=%async_computation.29 | async-start | bytes 5242880 | tf_op jit(solution)/shard_map/reduce_scatter | solution.py:79
  1515.7 164.7 %all-gather.39.cloned.1.call-start = ((), (), s32[]{:S(2)}) async-start(), calls=%async_computation.30 | async-start | bytes 5242880 | tf_op jit(solution)/shard_map/all_gather | solution.py:85
  1599.0 325.1 %reduce-scatter.27.cloned.1.call-start = ((), (), s32[]{:S(2)}) async-start(), calls=%async_computation.31 | async-start | bytes 5242880 | tf_op jit(solution)/shard_map/reduce_scatter | solution.py:79
  1848.7 127.5 %reduce-scatter.41.cloned.1.call-start = ((), (), s32[]{:S(2)}) async-start(), calls=%async_computation.39 | async-start | bytes 2359296 | tf_op jit(solution)/shard_map/reduce_scatter | solution.py:371
  1864.8 187.9 %all-gather.41.cloned.1.call-start = ((), (), s32[]{:S(2)}) async-start(), calls=%async_computation.32 | async-start | bytes 5242880 | tf_op jit(solution)/shard_map/all_gather | solution.py:85
  1929.9 228.8 %reduce-scatter.37.cloned.1.call-start = ((), (), s32[]{:S(2)}) async-start(), calls=%async_computation.37 | async-start | bytes 6488064 | tf_op jit(solution)/shard_map/reduce_scatter | solution.py:380
  1940.8 264.2 %reduce-scatter.35.cloned.1.call-start = ((), (), s32[]{:S(2)}) async-start(), calls=%async_computation.36 | async-start | bytes 12976128 | tf_op jit(solution)/shard_map/reduce_scatter | solution.py:377
  1962.9 287.2 %reduce-scatter.31.cloned.1.call-start = ((), (), s32[]{:S(2)}) async-start(), calls=%async_computation.34 | async-start | bytes 2359296 | tf_op jit(solution)/shard_map/reduce_scatter | solution.py:368
  1970.2 325.2 %reduce-scatter.33.cloned.1.call-start = ((), (), s32[]{:S(2)}) async-start(), calls=%async_computation.35 | async-start | bytes 2359296 | tf_op jit(solution)/shard_map/reduce_scatter | solution.py:374
  1976.1 357.0 %all-reduce.3.cloned.1.call-start = ((), (), s32[]{:S(2)}) async-start(), calls=%async_computation.40 | async-start | bytes 524288 | tf_op jit(solution)/shard_map/psum | solution.py:391
  1976.9 393.9 %reduce-scatter.43.cloned.1.call-start = ((), (), s32[]{:S(2)}) async-start(), calls=%async_computation.41 | async-start | bytes 589824
  1978.1 598.0 %reduce-scatter.39.cloned.1.call-start = ((), (), s32[]{:S(2)}) async-start(), calls=%async_computation.38 | async-start | bytes 36864000 | tf_op jit(solution)/shard_map/reduce_scatter | solution.py:383
  2024.8 756.8 %reduce-scatter.29.cloned.1.call-start = ((), (), s32[]{:S(2)}) async-start(), calls=%async_computation.33 | async-start | bytes 36864000 | tf_op jit(solution)/shard_map/reduce_scatter | solution.py:365
  2334.8 495.9 %copy-start.77 = (f32[3,256]{1,0:T(4,128)S(1)}, f32[3,256]{1,0:T(4,128)}, u32[]{:S(2)}) copy-start(f32[3,256]{1,0:T(4,128)} %param.47) | copy-start | bytes 9220
  2334.8 495.9 %copy-start.91 = (f32[3,256]{1,0:T(4,128)S(1)}, f32[3,256]{1,0:T(4,128)}, u32[]{:S(2)}) copy-start(f32[3,256]{1,0:T(4,128)} %param.55) | copy-start | bytes 9220
  2334.8 495.9 %copy-start.92 = (f32[3,256]{1,0:T(4,128)S(1)}, f32[3,256]{1,0:T(4,128)}, u32[]{:S(2)}) copy-start(f32[3,256]{1,0:T(4,128)} %param.63) | copy-start | bytes 9220
  (121 other events, 2850.9 us)
Sparse Core Ops, SparseCore 0:
  13.1 166.6 all-gather.16
  229.0 80.7 reduce-scatter.16
  312.4 28.3 all-gather.22
  342.9 80.7 all-gather.18
  426.2 26.4 all-gather.20
  455.1 28.1 all-gather.24
  547.4 76.7 reduce-scatter.18
  626.7 68.2 all-gather.28
  697.1 80.7 all-gather.26
  780.2 42.8 all-gather.30
  834.1 76.7 reduce-scatter.20
  913.3 164.4 all-gather.34
  1080.0 80.7 all-gather.32
  1317.1 74.2 reduce-scatter.22
  1396.6 81.2 all-gather.36
  1515.9 75.2 reduce-scatter.24
  1599.1 81.2 all-gather.38
  1848.8 75.2 reduce-scatter.26
  1928.0 41.7 reduce-scatter.40
  1971.8 80.7 all-gather.40
  2057.1 57.5 reduce-scatter.36
  2118.2 86.7 reduce-scatter.34
  2208.8 41.1 reduce-scatter.30
  2254.1 41.2 reduce-scatter.32
  2297.7 35.3 all-reduce.2
  2336.9 33.8 reduce-scatter.42
  2374.4 201.6 reduce-scatter.38
  2579.9 201.6 reduce-scatter.28
where the time goes:
time: 2910 us; the launch traced here: 2900 us
  waiting for transfers between devices  1880 us (65%)
  matrix products  397 us (14%)
  other arithmetic  336 us (12%)
  local copies, waits for them, and re-layouts  132 us (5%)
  blocking collectives  113 us (4%)
    all_gather x3, waiting for transfers between devices, spread(): lax.all_gather(normed(shard, gain).astype(jnp.bfloat16), 'mp', axis=0, ti...  247 us
    reduce_scatter x3, waiting for transfers between devices, collect(): lax.psum_scatter(partial_value.astype(jnp.bfloat16), 'mp', scatter_dimens...  213 us
    reduce_scatter x3, waiting for transfers between devices, collect_grad(): lax.psum_scatter(partial_value.astype(jnp.bfloat16), 'mp', scatter_dimens...  209 us
    reduce_scatter x1, waiting for transfers between devices, body(): lax.psum_scatter(embed_grad.astype(jnp.bfloat16), 'dp', scatter_dimension...  201 us
    reduce_scatter x1, waiting for transfers between devices, body(): lax.psum_scatter(head_grad.astype(jnp.bfloat16), 'dp', scatter_dimension=...  191 us
    all_gather x1, waiting for transfers between devices, body(): lax.all_gather(embed_table.astype(bf16), 'dp', axis=1, tiled=True)  166 us
    all_gather x1, waiting for transfers between devices, body(): lax.all_gather(head_weight.astype(bf16), 'dp', axis=0, tiled=True)  162 us
    all_gather x3, waiting for transfers between devices, spread_grad(): return lax.all_gather(shard.astype(jnp.bfloat16), 'mp', axis=0, tiled=True)  154 us
  transfers between devices with their start and end apart: 28, of which 25 were waited for; matrix products, arithmetic and copies ran while one was open for 14% of the time, Pallas kernels for 0%

commit v1 on v0

v1 whole, which is shorter than its diff:
```python
import functools

import jax
import jax.numpy as jnp
from jax import lax
from jax.experimental import pallas as pl
from jax.experimental.pallas import tpu as pltpu
from jax.sharding import PartitionSpec as P

HD = 64
KVH = 4
LEN = 1024
STEP = 5

EPS = 1e-05
SCALE = 0.125
CLIP = 0.01
BETA_ONE = 0.9
BETA_TWO = 0.95
ADAM_EPS = 1e-08
RATES = (0.9, 0.01, 0.01, 0.06, 0.01, 0.01, 0.08, 0.9)
DECAYS = (0.1, 0.1, 0.1, 0.1, 0.1, 0.1, 0.1, 0.0)

LANES = 128
QB = 256
VMEM_LIMIT = 56 * 1024 * 1024

f32 = jnp.float32
bf16 = jnp.bfloat16


def normed(hidden, gain):
    return hidden * lax.rsqrt(jnp.mean(hidden * hidden, axis=-1, keepdims=True) + EPS) * gain


def norm_back(hidden, gain, upstream):
    _, pullback = jax.vjp(normed, hidden, gain)
    return pullback(upstream)


def rotary_tables(length):
    positions = (jnp.arange(length) % LEN).astype(f32)
    freqs = 10000.0 ** (-(2 * jnp.arange(HD // 2)).astype(f32) / HD)
    angles = positions[:, None] * freqs[None, :]
    cosine = jnp.cos(angles)
    sine = jnp.sin(angles)
    return (
        jnp.concatenate([cosine] * 4, -1),
        jnp.concatenate([-sine, sine, -sine, sine], -1),
    )


def swap_halves(x, lane):
    half = HD // 2
    return jnp.where(
        lane % HD < half, pltpu.roll(x, LANES - half, 1), pltpu.roll(x, half, 1)
    )


def attend_kernel(q_ref, kv_ref, cos_ref, sin_ref, mixed_ref, rope_ref, key_ref, value_ref, lse_ref):
    rows = q_ref.shape[0]
    lane = lax.broadcasted_iota(jnp.int32, (rows, LANES), 1)
    cosine, sine = cos_ref[...], sin_ref[...]

    @pl.when(pl.program_id(0) == 0)
    def _():
        pair = kv_ref[...]
        other = pltpu.roll(pair, HD, 1)
        key = jnp.where(lane < HD, pair, other)
        value = jnp.where(lane < HD, other, pair)
        key_ref[...] = (key * cosine + swap_halves(key, lane) * sine).astype(bf16)
        value_ref[...] = value.astype(bf16)

    q = q_ref[...]
    rope_ref[...] = (q * cosine + swap_halves(q, lane) * sine).astype(bf16)
    low = lax.broadcasted_iota(jnp.int32, (QB, LANES), 1) < HD
    for block in range(rows // QB):
        at = block * QB
        width = at + QB
        chosen = rope_ref[at : at + QB, :]
        keys = key_ref[:width, :]
        values = value_ref[:width, :]
        places = at + lax.broadcasted_iota(jnp.int32, (QB, width), 0)
        causal = lax.broadcasted_iota(jnp.int32, (QB, width), 1) <= places
        outs, sums = [], []
        for part in range(2):
            mask = low if part == 0 else jnp.logical_not(low)
            one = jnp.where(mask, chosen, jnp.zeros_like(chosen))
            scores = SCALE * lax.dot_general(
                one, keys, (((1,), (1,)), ((), ())), preferred_element_type=f32
            )
            scores = jnp.where(causal, scores, -1e30)
            peak = jnp.max(scores, -1, keepdims=True)
            expo = jnp.exp(scores - peak)
            total = jnp.sum(expo, -1, keepdims=True)
            probs = (expo * (1.0 / total)).astype(bf16)
            outs.append(jnp.dot(probs, values, preferred_element_type=f32))
            sums.append(peak + jnp.log(total))
        mixed_ref[at : at + QB, :] = jnp.where(low, outs[0], outs[1]).astype(bf16)
        lse_ref[0, at : at + QB, :] = jnp.where(low, sums[0], sums[1])


def attend(qkv, cosine, sine):
    rows, cols = qkv.shape
    pairs = cols // LANES - 1
    whole = pl.BlockSpec((rows, LANES), lambda p: (0, 0))
    column = pl.BlockSpec((rows, LANES), lambda p: (0, p))
    return pl.pallas_call(
        attend_kernel,
        grid=(pairs,),
        in_specs=[column, pl.BlockSpec((rows, LANES), lambda p: (0, pairs)), whole, whole],
        out_specs=[column, column, whole, whole, pl.BlockSpec((1, rows, LANES), lambda p: (p, 0, 0))],
        out_shape=[
            jax.ShapeDtypeStruct((rows, pairs * LANES), bf16),
            jax.ShapeDtypeStruct((rows, pairs * LANES), bf16),
            jax.ShapeDtypeStruct((rows, LANES), bf16),
            jax.ShapeDtypeStruct((rows, LANES), bf16),
            jax.ShapeDtypeStruct((pairs, rows, LANES), f32),
        ],
        compiler_params=pltpu.CompilerParams(
            dimension_semantics=("arbitrary",), vmem_limit_bytes=VMEM_LIMIT
        ),
        name="attend",
    )(qkv, qkv, cosine, sine)


def attend_back_kernel(
    q_ref, key_ref, value_ref, lse_ref, grad_ref, cos_ref, sin_ref, dq_ref, dkv_ref, dk_acc, dv_acc
):
    rows = q_ref.shape[0]
    lane = lax.broadcasted_iota(jnp.int32, (rows, LANES), 1)
    step = pl.program_id(0)

    @pl.when(step == 0)
    def _():
        dk_acc[...] = jnp.zeros_like(dk_acc)
        dv_acc[...] = jnp.zeros_like(dv_acc)

    low = lax.broadcasted_iota(jnp.int32, (QB, LANES), 1) < HD
    lane_block = lax.broadcasted_iota(jnp.int32, (QB, LANES), 1)
    for block in range(rows // QB):
        at = block * QB
        width = at + QB
        chosen = q_ref[at : at + QB, :]
        upstream = grad_ref[at : at + QB, :]
        keys = key_ref[:width, :]
        values = value_ref[:width, :]
        places = at + lax.broadcasted_iota(jnp.int32, (QB, width), 0)
        causal = lax.broadcasted_iota(jnp.int32, (QB, width), 1) <= places
        outs = []
        for part in range(2):
            mask = low if part == 0 else jnp.logical_not(low)
            one = jnp.where(mask, chosen, jnp.zeros_like(chosen))
            grad = jnp.where(mask, upstream, jnp.zeros_like(upstream))
            scores = SCALE * lax.dot_general(
                one, keys, (((1,), (1,)), ((), ())), preferred_element_type=f32
            )
            lse = lse_ref[0, at : at + QB, part * HD : part * HD + 1]
            probs = jnp.where(causal, jnp.exp(scores - lse), 0.0)
            prob_grad = lax.dot_general(
                grad, values, (((1,), (1,)), ((), ())), preferred_element_type=f32
            )
            inner = jnp.sum(probs * prob_grad, -1, keepdims=True)
            score_grad = (probs * (prob_grad - inner)).astype(bf16)
            outs.append(jnp.dot(score_grad, keys, preferred_element_type=f32) * SCALE)
            dk_acc[:width, :] += SCALE * lax.dot_general(
                score_grad, one, (((0,), (0,)), ((), ())), preferred_element_type=f32
            )
            dv_acc[:width, :] += lax.dot_general(
                probs.astype(bf16), grad, (((0,), (0,)), ((), ())), preferred_element_type=f32
            )
        total = jnp.where(low, outs[0], outs[1])
        turned = swap_halves(total, lane_block)
        dq_ref[at : at + QB, :] = (
            total * cos_ref[at : at + QB, :] - turned * sin_ref[at : at + QB, :]
        ).astype(bf16)

    @pl.when(step == pl.num_programs(0) - 1)
    def _():
        dk = dk_acc[...]
        dk = dk + pltpu.roll(dk, HD, 1)
        dk = dk * cos_ref[...] - swap_halves(dk, lane) * sin_ref[...]
        dv = dv_acc[...]
        dv = dv + pltpu.roll(dv, HD, 1)
        dkv_ref[...] = jnp.where(lane < HD, dk, dv).astype(bf16)


def attend_back(rope, key, value, lse, grad, cosine, sine):
    rows, cols = rope.shape
    pairs = cols // LANES
    whole = pl.BlockSpec((rows, LANES), lambda p: (0, 0))
    column = pl.BlockSpec((rows, LANES), lambda p: (0, p))
    return pl.pallas_call(
        attend_back_kernel,
        grid=(pairs,),
        in_specs=[
            column,
            whole,
            whole,
            pl.BlockSpec((1, rows, LANES), lambda p: (p, 0, 0)),
            column,
            whole,
            whole,
        ],
        out_specs=[column, whole],
        out_shape=[
            jax.ShapeDtypeStruct((rows, cols), bf16),
            jax.ShapeDtypeStruct((rows, LANES), bf16),
        ],
        scratch_shapes=[pltpu.VMEM((rows, LANES), f32), pltpu.VMEM((rows, LANES), f32)],
        compiler_params=pltpu.CompilerParams(
            dimension_semantics=("arbitrary",), vmem_limit_bytes=VMEM_LIMIT
        ),
        name="attend_back",
    )(rope, key, value, lse, grad, cosine, sine)


def shift_up(x, size):
    return lax.ppermute(x, "mp", [(i, i + 1) for i in range(size - 1)])


def shift_down(x, size):
    return lax.ppermute(x, "mp", [(i + 1, i) for i in range(size - 1)])


def line_gather(shard):
    size = lax.axis_size("mp")
    me = lax.axis_index("mp")
    ups, downs = [shard], [shard]
    for _ in range(size - 1):
        ups.append(shift_up(ups[-1], size))
        downs.append(shift_down(downs[-1], size))
    whole = jnp.zeros((size,) + shard.shape, shard.dtype)
    whole = lax.dynamic_update_index_in_dim(whole, shard, me, 0)
    for hop in range(1, size):
        piece = jnp.where(me >= hop, ups[hop], downs[size - hop])
        whole = lax.dynamic_update_index_in_dim(whole, piece, (me - hop) % size, 0)
    return whole


def line_scatter(parts):
    size = parts.shape[0]
    me = lax.axis_index("mp")

    def own(place):
        return lax.dynamic_index_in_dim(parts, jnp.clip(place, 0, size - 1), 0, False)

    up, down = None, None
    for step in range(1, size):
        mine_up, mine_down = own(me + size - step), own(me - size + step)
        up = shift_up(mine_up if up is None else mine_up + up, size)
        down = shift_down(mine_down if down is None else mine_down + down, size)
    return own(me).astype(f32) + up.astype(f32) + down.astype(f32)


def spread(shard):
    whole = line_gather(shard)
    return whole.reshape(-1, shard.shape[-1])


def collect(partial_value):
    size = lax.axis_size("mp")
    return line_scatter(
        partial_value.astype(bf16).reshape(size, -1, partial_value.shape[-1])
    )


def adamw(weight, grad, mean_old, square_old, factor, rate, decay):
    clipped = grad.astype(f32) * factor
    mean_new = BETA_ONE * mean_old + (1 - BETA_ONE) * clipped
    square_new = BETA_TWO * square_old + (1 - BETA_TWO) * clipped * clipped
    ratio = (
        mean_new / (1 - BETA_ONE**STEP) / (jnp.sqrt(square_new / (1 - BETA_TWO**STEP)) + ADAM_EPS)
    )
    return (weight - rate * (ratio + decay * weight), mean_new, square_new)


def dot(a, b, dims=((1,), (0,)), out=f32):
    return lax.dot_general(a, b, (dims, ((), ())), preferred_element_type=f32).astype(out)


def body(
    tokens,
    targets,
    select,
    bucket,
    embed_table,
    query_weight,
    keyvalue_weight,
    output_weight,
    gateup_weight,
    down_weight,
    head_weight,
    norm_gains,
    embed_mean,
    query_mean,
    keyvalue_mean,
    output_mean,
    gateup_mean,
    down_mean,
    head_mean,
    gains_mean,
    embed_square,
    query_square,
    keyvalue_square,
    output_square,
    gateup_square,
    down_square,
    head_square,
    gains_square,
):
    n_dp, n_mp = lax.axis_size("dp"), lax.axis_size("mp")
    group = lax.axis_index("mp")
    rows = tokens.shape[0]
    home = rows // n_mp
    head_kv = group * KVH // n_mp
    embed_part_rows, embed_cols = embed_table.shape
    vocab_start = group * embed_part_rows
    q_cols = query_weight.shape[1]

    key_cols = lax.dynamic_slice_in_dim(keyvalue_weight, head_kv * HD, HD, 1)
    value_cols = lax.dynamic_slice_in_dim(keyvalue_weight, (KVH + head_kv) * HD, HD, 1)
    qkv_own = jnp.concatenate([query_weight, key_cols, value_cols], 1).astype(bf16)
    ids = lax.all_gather(tokens, "dp", axis=0, tiled=True)
    gains_rows = lax.all_gather(norm_gains.astype(bf16), "dp", axis=1, tiled=True).astype(f32)
    qkv_full = lax.all_gather(qkv_own, "dp", axis=0, tiled=True)
    output_full = lax.all_gather(output_weight.astype(bf16), "dp", axis=1, tiled=True)
    gateup_full = lax.all_gather(gateup_weight.astype(bf16), "dp", axis=1, tiled=True)
    down_full = lax.all_gather(down_weight.astype(bf16), "dp", axis=1, tiled=True)
    head_full = lax.all_gather(head_weight.astype(bf16), "dp", axis=0, tiled=True)
    cosine, sine = rotary_tables(rows)

    ids_local = ids - vocab_start
    inside = (ids_local >= 0) & (ids_local < embed_part_rows)
    looked = embed_table[jnp.clip(ids_local, 0, embed_part_rows - 1)]
    looked = jnp.where(inside[:, None], looked, 0.0).astype(bf16)
    looked = looked.reshape(n_dp, n_mp, home, embed_cols).transpose(1, 0, 2, 3)
    looked = line_scatter(looked.reshape(n_mp, n_dp * home, embed_cols)).astype(bf16)
    looked = lax.all_to_all(looked.reshape(n_dp, home, embed_cols), "dp", 0, 0)
    start_rows = looked.transpose(1, 0, 2).reshape(home, -1).astype(f32)

    first_in = spread(normed(start_rows, gains_rows[0]).astype(bf16))
    qkv = dot(first_in, qkv_full)
    mixed, rope, key, value, lse = attend(qkv, cosine, sine)
    middle_rows = start_rows + collect(dot(mixed, output_full, out=bf16))
    second_in = spread(normed(middle_rows, gains_rows[1]).astype(bf16))
    gate = dot(second_in, gateup_full[0])
    upper = dot(second_in, gateup_full[1])
    active = (jax.nn.silu(gate) * upper).astype(bf16)
    final_rows = middle_rows + collect(dot(active, down_full, out=bf16))
    final_in = spread(normed(final_rows, gains_rows[2]).astype(bf16))
    logits = dot(final_in, head_full)
    hits = jnp.arange(head_full.shape[1])[None, :] == (targets - group * head_full.shape[1])[:, None]
    local_top = jnp.max(logits, -1)
    stats = lax.all_gather(
        jnp.stack(
            [
                local_top,
                jnp.sum(jnp.exp(logits - local_top[:, None]), -1),
                jnp.sum(jnp.where(hits, logits, 0.0), -1),
            ]
        ),
        "mp",
    )
    top = jnp.max(stats[:, 0], 0)
    expsum = jnp.sum(stats[:, 1] * jnp.exp(stats[:, 0] - top[None]), 0)
    logsum_all = top + jnp.log(expsum)
    picked = jnp.sum(stats[:, 2], 0)
    scales = (select * bucket).astype(f32)
    loss_sum, weight_total = lax.psum(
        (jnp.sum(scales * (logsum_all - picked)), jnp.sum(scales)), "dp"
    )
    coef = scales * (1.0 / weight_total)
    logit_grad = (
        (jnp.exp(logits - logsum_all[:, None]) - hits.astype(f32)) * coef[:, None]
    ).astype(bf16)

    def reduce_rows(grad):
        return lax.psum_scatter(grad, "dp", scatter_dimension=0, tiled=True)

    final_partial = dot(logit_grad, head_full, ((1,), (1,)), bf16)
    head_part = reduce_rows(dot(final_in, logit_grad, ((0,), (0,)), bf16))
    final_grad = collect(final_partial)
    residual, final_gain = norm_back(final_rows, gains_rows[2], final_grad)
    branch = spread(residual.astype(bf16))
    sigmoid = jax.nn.sigmoid(gate)
    silu_gate = gate * sigmoid
    active_grad = dot(branch, down_full, ((1,), (1,)))
    gate_grad = (active_grad * upper * sigmoid * (1.0 + gate * (1.0 - sigmoid))).astype(bf16)
    upper_grad = (active_grad * silu_gate).astype(bf16)
    second_partial = (
        dot(gate_grad, gateup_full[0], ((1,), (1,)))
        + dot(upper_grad, gateup_full[1], ((1,), (1,)))
    ).astype(bf16)
    down_part = lax.psum_scatter(
        dot(active, branch, ((0,), (0,)), bf16), "dp", scatter_dimension=1, tiled=True
    )
    gateup_part = lax.psum_scatter(
        jnp.stack(
            [
                dot(second_in, gate_grad, ((0,), (0,)), bf16),
                dot(second_in, upper_grad, ((0,), (0,)), bf16),
            ]
        ),
        "dp",
        scatter_dimension=1,
        tiled=True,
    )
    second_grad = collect(second_partial)
    middle_extra, middle_gain = norm_back(middle_rows, gains_rows[1], second_grad)
    residual = residual + middle_extra
    branch = spread(residual.astype(bf16))
    mixed_grad = dot(branch, output_full, ((1,), (1,)), bf16)
    query_pre, pair_grad = attend_back(rope, key, value, lse, mixed_grad, cosine, sine)
    output_part = lax.psum_scatter(
        dot(mixed, branch, ((0,), (0,)), bf16), "dp", scatter_dimension=1, tiled=True
    )
    qkv_grad = jnp.concatenate([query_pre, pair_grad], 1)
    first_grad = collect(dot(qkv_grad, qkv_full, ((1,), (1,)), bf16))
    start_extra, start_gain = norm_back(start_rows, gains_rows[0], first_grad)
    start_grad = (residual + start_extra).astype(bf16)
    gains_grad = jnp.stack([start_gain, middle_gain, final_gain], 1).astype(bf16)
    small = reduce_rows(
        jnp.concatenate([dot(first_in, qkv_grad, ((0,), (0,)), bf16), gains_grad], 1)
    )
    query_part = small[:, :q_cols]

    moved = start_grad.reshape(home, n_dp, embed_cols).transpose(1, 0, 2)
    moved = lax.all_to_all(moved, "dp", 0, 0)
    moved = spread(moved.reshape(n_dp * home, embed_cols))
    moved_ids = ids_local.reshape(n_dp, n_mp, home).transpose(1, 0, 2).reshape(-1)
    onehot_back = (moved_ids[None, :] == jnp.arange(embed_part_rows)[:, None]).astype(bf16)
    embed_part = dot(onehot_back, moved)

    shared = lax.all_gather(small[:, q_cols:], "mp").astype(f32)
    gains_part = jnp.sum(shared[:, :, 2 * HD :], 0).T
    keyvalue_part = jnp.zeros(keyvalue_weight.shape, f32)
    for source in range(n_mp):
        c = source * KVH // n_mp
        keyvalue_part = keyvalue_part.at[:, c * HD : (c + 1) * HD].add(shared[source, :, :HD])
        keyvalue_part = keyvalue_part.at[:, (KVH + c) * HD : (KVH + c + 1) * HD].add(
            shared[source, :, HD : 2 * HD]
        )

    leading = (group == 0).astype(f32)

    def square(piece):
        piece = piece.astype(f32)
        return jnp.sum(piece * piece)

    squared = sum(
        square(piece)
        for piece in (embed_part, query_part, output_part, gateup_part, down_part, head_part)
    )
    squared = squared + leading * (square(keyvalue_part) + square(gains_part))
    grad_norm = jnp.sqrt(lax.psum(squared, ("dp", "mp")))
    factor = jnp.minimum(1.0, CLIP / (grad_norm + 1e-06))
    outs = [loss_sum, weight_total, grad_norm]
    for number, (weight, grad, mean_old, square_old) in enumerate(
        (
            (embed_table, embed_part, embed_mean, embed_square),
            (query_weight, query_part, query_mean, query_square),
            (keyvalue_weight, keyvalue_part, keyvalue_mean, keyvalue_square),
            (output_weight, output_part, output_mean, output_square),
            (gateup_weight, gateup_part, gateup_mean, gateup_square),
            (down_weight, down_part, down_mean, down_square),
            (head_weight, head_part, head_mean, head_square),
            (norm_gains, gains_part, gains_mean, gains_square),
        )
    ):
        new, mean_new, square_new = adamw(
            weight, grad, mean_old, square_old, factor, RATES[number], DECAYS[number]
        )
        outs += [new, embed_part * factor if number == 0 else mean_new, square_new]
    return tuple(outs)


def solution(mesh):
    weights = (
        P("mp", "dp"),
        P("dp", "mp"),
        P("dp", None),
        P("mp", "dp"),
        P(None, "dp", "mp"),
        P("mp", "dp"),
        P("dp", "mp"),
        P(None, "dp"),
    )
    in_specs = (P("dp"),) * 4 + weights * 3
    out_specs = (P(),) * 3 + tuple(spec for spec in weights for _ in range(3))
    return jax.shard_map(body, mesh=mesh, in_specs=in_specs, out_specs=out_specs, check_vma=False)
```

time: 2910 us -> 1830 us (0.63)
  waiting for transfers between devices: 1880 us -> 615 us
  starting transfers between devices: 1.55 us -> 218 us
  matrix products: 397 us -> 298 us
  local copies, waits for them, and re-layouts: 132 us -> 213 us
  other arithmetic: 336 us -> 256 us
  Pallas kernels: 0 us -> 46.4 us
  blocking collectives: 113 us -> 150 us
    reduce_scatter x13 -> x5, waiting for transfers between devices: 944 us -> 95.9 us  [the longest x2 95.9 us: reduce_rows(): return lax.psum_scatter(grad, 'dp', scatter_dimension=0, tiled=True)]
    all_gather x9 -> x1, waiting for transfers between devices: 617 us -> 0.01 us  [body(): qkv_full = lax.all_gather(qkv_own, 'dp', axis=0, tiled=True)]
    ppermute x0 -> x72, waiting for transfers between devices: none -> 519 us  [the longest x36 392 us: shift_up(): return lax.ppermute(x, 'mp', [(i, i + 1) for i in range(size - 1)])]
    ppermute x0 -> x72, starting transfers between devices: none -> 213 us  [the longest x36 165 us: shift_up(): return lax.ppermute(x, 'mp', [(i, i + 1) for i in range(size - 1)])]
    all_gather x1, waiting for transfers between devices: 162 us -> 0.01 us  [body(): lax.all_gather(head_weight.astype(bf16), 'dp', axis=0, tiled=True)]
    dot_general x39 -> x19, matrix products: 397 us -> 298 us  [dot(): lax.dot_general(a, b, (dims, ((), ())), preferred_element_type=f32)]
    dynamic_slice x16 -> x35, local copies, waits for them, and re-layouts: 5.36 us -> 75.5 us  [own(): lax.dynamic_index_in_dim(parts, jnp.clip(place, 0, size - 1), 0, False)]
    convert_element_type x17 -> x11, other arithmetic: 84.3 us -> 19.9 us  [the longest x2 6.63 us: body(): branch = spread(residual.astype(bf16))]
  transfers between devices with their start and end apart: 28 -> 83, of which waited for: 25 -> 48; matrix products, arithmetic and copies ran while one was open for 14% -> 28% of each run, Pallas kernels for 0% -> 3%
where the time goes in v1:
time: 1830 us; the launch traced here: 1820 us
  waiting for transfers between devices  615 us (34%)
  matrix products  298 us (16%)
  other arithmetic  256 us (14%)
  starting transfers between devices  218 us (12%)
  local copies, waits for them, and re-layouts  213 us (12%)
  blocking collectives  150 us (8%)
  Pallas kernels  46.4 us (3%)
  between operations  24.2 us (1%)
    ppermute x36, waiting for transfers between devices, shift_up(): return lax.ppermute(x, 'mp', [(i, i + 1) for i in range(size - 1)])  392 us
    dot_general x19, matrix products, dot(): lax.dot_general(a, b, (dims, ((), ())), preferred_element_type=f32)  298 us
    ppermute x36, starting transfers between devices, shift_up(): return lax.ppermute(x, 'mp', [(i, i + 1) for i in range(size - 1)])  165 us
    ppermute x36, waiting for transfers between devices, shift_down(): return lax.ppermute(x, 'mp', [(i + 1, i) for i in range(size - 1)])  127 us
    reduce_scatter x2, waiting for transfers between devices, reduce_rows(): return lax.psum_scatter(grad, 'dp', scatter_dimension=0, tiled=True)  95.9 us
    dynamic_slice x35, local copies, waits for them, and re-layouts, own(): lax.dynamic_index_in_dim(parts, jnp.clip(place, 0, size - 1), 0, False)  75.5 us
    sub x8, other arithmetic, adamw(): return (weight - rate * (ratio + decay * weight), mean_new, square_new)  60 us
    ppermute x36, starting transfers between devices, shift_down(): return lax.ppermute(x, 'mp', [(i + 1, i) for i in range(size - 1)])  48 us
  transfers between devices with their start and end apart: 83, of which 48 were waited for; matrix products, arithmetic and copies ran while one was open for 28% of the time, Pallas kernels for 3%

profile of v1, /device:TPU:0, one launch (start us, length us, event | category | flops | bytes accessed | tf_op | source)
XLA Modules:
  0.0 1820.3 jit_solution(8110755905857340031)
XLA Ops:
  32.6 34.5 %gather_fusion = bf16[8192,256]{1,0:T(8,128)(2,1)} fusion(f32[8000,256]{1,0:T(8,128)} %param.48, s32[8192]{0:T(1024)S(1)} %fusion.59), kind=kCustom, calls=%fused_computation | custom fusion | bytes 8421376 | tf_op jit(solution)/shard_map/gather | solution.py:335
  77.8 21.5 %collective-permute-done = bf16[2048,256]{1,0:T(8,128)(2,1)S(1)} collective-permute-done((bf16[2048,256]{1,0:T(8,128)(2,1)S(1)}, bf16[2048,256]{1,0:T(8,128)(2,1)S(1)}, u32[]{:S(2)}, u32[]{:S(2)}) %collective-permute-start) | collective-permute-done | bytes 1048608 | tf_op jit(solution)/shard_map/ppermute | solution.py:219
  105.1 22.1 %collective-permute-done.1 = bf16[2048,256]{1,0:T(8,128)(2,1)S(1)} collective-permute-done((bf16[2048,256]{1,0:T(8,128)(2,1)S(1)}, bf16[2048,256]{1,0:T(8,128)(2,1)S(1)}, u32[]{:S(2)}, u32[]{:S(2)}) %collective-permute-start.1) | collective-permute-done | bytes 1048608 | tf_op jit(solution)/shard_map/ppermute | solution.py:219
  137.0 20.4 %collective-permute-done.4 = bf16[2048,256]{1,0:T(8,128)(2,1)S(1)} collective-permute-done((bf16[2048,256]{1,0:T(8,128)(2,1)}, bf16[2048,256]{1,0:T(8,128)(2,1)S(1)}, u32[]{:S(2)}, u32[]{:S(2)}) %collective-permute-start.4) | collective-permute-done | bytes 1048608 | tf_op jit(solution)/shard_map/ppermute | solution.py:223
  160.1 23.9 %collective-permute-done.5 = bf16[2048,256]{1,0:T(8,128)(2,1)S(1)} collective-permute-done((bf16[2048,256]{1,0:T(8,128)(2,1)S(1)}, bf16[2048,256]{1,0:T(8,128)(2,1)S(1)}, u32[]{:S(2)}, u32[]{:S(2)}) %collective-permute-start.5) | collective-permute-done | bytes 1048608 | tf_op jit(solution)/shard_map/ppermute | solution.py:223
  190.2 18.3 %all_gather.34 = bf16[3,2048]{1,0:T(4,128)(2,1)S(1)} all-gather(bf16[3,256]{1,0:T(4,128)(2,1)S(1)} %convert_element_type.286), channel_id=1, replica_groups=mesh['dp'=8,'mp'=4] {'dp'}, dimensions={1}, use_global_device_ids=true | all-gather | bytes 13824 | tf_op jit(solution)/shard_map/all_gather | solution.py:325
  219.2 20.6 %collective-permute-done.6 = bf16[256,2048]{0,1:T(8,128)(2,1)} collective-permute-done((bf16[256,2048]{0,1:T(8,128)(2,1)S(1)}, bf16[256,2048]{0,1:T(8,128)(2,1)}, u32[]{:S(2)}, u32[]{:S(2)}) %collective-permute-start.6) | collective-permute-done | bytes 1048608 | tf_op jit(solution)/shard_map/ppermute | solution.py:219
  318.3 20.5 %attend.1 = (bf16[1024,512]{1,0:T(8,128)(2,1)}, bf16[1024,512]{1,0:T(8,128)(2,1)}, bf16[1024,128]{1,0:T(8,128)(2,1)}, bf16[1024,128]{1,0:T(8,128)(2,1)}, f32[4,1024,128]{2,1,0:T(8,128)}) custom-call(f32[1024,640]{1,0:T(8,128)} %fusion.95.q_ref.kv_ref, f32[1024,640]{1,0:T(8,128)} %fusion.95.q_ref.kv_ref, f32[1024,128]{1,0:T(8,128)} %get-tuple-element.413.cos_ref, ...), custom_call_target="tpu_custom_call" | custom-call | tf_op jit(solution)/shard_map/attend/pallas_call | solution.py:108
  437.3 17.6 collective-permute-done.18
  461.5 16.3 collective-permute-done.22
  623.6 19.6 %collective-permute-done.30 = bf16[256,2048]{0,1:T(8,128)(2,1)S(1)} collective-permute-done((bf16[256,2048]{0,1:T(8,128)(2,1)S(1)}, bf16[256,2048]{0,1:T(8,128)(2,1)S(1)}, u32[]{:S(2)}, u32[]{:S(2)}) %collective-permute-start.30) | collective-permute-done | bytes 1048608 | tf_op jit(solution)/shard_map/ppermute | solution.py:219
  650.9 20.5 %collective-permute-done.34 = bf16[256,2048]{0,1:T(8,128)(2,1)} collective-permute-done((bf16[256,2048]{0,1:T(8,128)(2,1)S(1)}, bf16[256,2048]{0,1:T(8,128)(2,1)}, u32[]{:S(2)}, u32[]{:S(2)}) %collective-permute-start.34) | collective-permute-done | bytes 1048608 | tf_op jit(solution)/shard_map/ppermute | solution.py:219
  706.4 41.9 %fusion.94 = (f32[1024]{0:T(1024)S(1)}, f32[1024,8000]{0,1:T(8,128)}) fusion(bf16[1024,2048]{1,0:T(8,128)(2,1)} %bitcast.325, bf16[2048,8000]{0,1:T(8,128)(2,1)} %all-gather.17.cloned.1.call-done), kind=kOutput, calls=%fused_computation.315 | convolution fusion | flops 33562624000 | bytes 69734400 | tf_op jit(solution)/shard_map/dot_general | solution.py:279
  748.4 14.8 exponential_reduce_fusion
  790.6 42.8 %convolution_convert_fusion.4 = bf16[1024,2048]{1,0:T(8,128)(2,1)S(1)} fusion(bf16[2048,8000]{0,1:T(8,128)(2,1)} %all-gather.17.cloned.1.call-done, f32[1024,8000]{0,1:T(8,128)} %get-tuple-element.410, f32[1024]{0:T(1024)S(1)} %convert_multiply_fusion.11, f32[1024]{0:T(1024)S(1)} %get-tuple-element.339, s32[1024]{0:T(1024)S(1)} %broadcast_subtract_fusion.1), kind=kOutput, calls=%fused_computation.43 | convolution fusion | flops 33605681152 | bytes 69742592 | tf_op jit(solution)/shard_map/dot_general | solution.py:279
  849.0 13.9 collective-permute-done.36
  878.5 13.7 collective-permute-done.37
  905.7 14.7 collective-permute-done.38
  936.3 18.2 collective-permute-done.42
  961.1 16.5 collective-permute-done.46
  1021.2 15.3 multiply_convert_fusion.1
  1171.8 17.6 collective-permute-done.58
  1226.4 25.9 %attend_back.1 = (bf16[1024,512]{1,0:T(8,128)(2,1)}, bf16[1024,128]{1,0:T(8,128)(2,1)}) custom-call(bf16[1024,512]{1,0:T(8,128)(2,1)} %get-tuple-element.131.q_ref, bf16[1024,128]{1,0:T(8,128)(2,1)} %get-tuple-element.132.key_ref, bf16[1024,128]{1,0:T(8,128)(2,1)} %get-tuple-element.133.value_ref, f32[4,1024,128]{2,1,0:T(8,128)} %get-tuple-element.134.lse_ref, ...), custom_call_target="tpu_custom_call" | custom-call | tf_op jit(solution)/shard_map/attend_back/pallas_call | solution.py:193
  1367.8 45.4 %convolution_convert_fusion = bf16[2048,8000]{0,1:T(8,128)(2,1)} fusion(bf16[1024,2048]{1,0:T(8,128)(2,1)} %bitcast.326, f32[1024,8000]{0,1:T(8,128)} %get-tuple-element.410, f32[1024]{0:T(1024)S(1)} %copy-done.69, f32[1024]{0:T(1024)S(1)} %copy-done.67, s32[1024]{0:T(1024)S(1)} %copy-done.52), kind=kOutput, calls=%fused_computation.8 | convolution fusion | flops 33619968000 | bytes 69742592 | tf_op jit(solution)/shard_map/dot_general | solution.py:279
  1417.1 29.3 %all_to_all.10 = bf16[8,256,256]{1,2,0:T(8,128)(2,1)S(1)} all-to-all(bf16[8,256,256]{1,2,0:T(8,128)(2,1)S(1)} %bitcast.332), channel_id=1, replica_groups=mesh['dp'=8,'mp'=4] {'dp'}, dimensions={0} | all-to-all | bytes 2097152 | tf_op jit(solution)/shard_map/all_to_all | solution.py:429
  1453.8 17.3 collective-permute-done.67
  1503.5 26.5 %all-gather.1 = bf16[1024,131]{0,1:T(8,128)(2,1)S(1)} all-gather(bf16[256,131]{0,1:T(8,128)(2,1)S(1)} %slice.246), channel_id=3, replica_groups=mesh['dp'=8,'mp'=4] {'mp'}, dimensions={0}, use_global_device_ids=true | all-gather | bytes 335360 | tf_op jit(solution)/shard_map/all_gather | solution.py:435
  1546.4 45.9 %multiply_reduce_fusion = (f32[]{:T(128)}, f32[8000,256]{1,0:T(8,128)}) fusion(bf16[8192,256]{1,0:T(8,128)(2,1)} %bitcast.318, s32[8192]{0:T(1024)S(1)} %bitcast.358), kind=kOutput, calls=%fused_computation.24 | convolution fusion | flops 33624064000 | bytes 12419076 | tf_op jit(solution)/shard_map/dot_general | solution.py:279
  1598.5 95.9 %reduce-scatter.14.cloned.1.call-done = bf16[256,8000]{0,1:T(8,128)(2,1)} async-done(((bf16[2048,8000]{0,1:T(8,128)(2,1)}), bf16[256,8000]{0,1:T(8,128)(2,1)}) %reduce-scatter.14.cloned.1.call-update) | async-done | bytes 4096016 | tf_op jit(solution)/shard_map/reduce_scatter | solution.py:379
  1702.0 39.5 %psum.23 = f32[]{:T(128)} all-reduce(f32[]{:T(128)S(6)} %add.654), channel_id=1, replica_groups=mesh['dp'=8,'mp'=4] {'dp','mp'}, use_global_device_ids=true, to_apply=%region_40.41 | all-reduce | flops 1 | bytes 8 | tf_op jit(solution)/shard_map/psum | solution.py:456
  1755.9 21.7 %multiply_subtract_fusion.1 = (f32[8000,256]{1,0:T(8,128)}, f32[8000,256]{1,0:T(8,128)}, f32[8000,256]{1,0:T(8,128)}) fusion(f32[8000,256]{1,0:T(8,128)} %param.48, f32[8000,256]{1,0:T(8,128)} %param.56, f32[8000,256]{1,0:T(8,128)} %param.64, f32[8000,256]{1,0:T(8,128)} %get-tuple-element.412, f32[]{:T(128)S(6)} %min.77), kind=kLoop, calls=%fused_computation.23 | loop fusion | flops 32768000 | bytes 57344004 | tf_op jit(solution)/shard_map/sub | solution.py:275
  1777.7 20.6 %multiply_subtract_fusion = (f32[256,8000]{0,1:T(8,128)}, f32[256,8000]{0,1:T(8,128)}, f32[256,8000]{0,1:T(8,128)}) fusion(f32[256,8000]{0,1:T(8,128)} %param.54, f32[]{:T(128)S(6)} %min.77, bf16[256,8000]{0,1:T(8,128)(2,1)} %reduce-scatter.14.cloned.1.call-done, f32[256,8000]{0,1:T(8,128)} %param.62, f32[256,8000]{0,1:T(8,128)} %param.70), kind=kLoop, calls=%fused_computation.22 | loop fusion | flops 34816000 | bytes 53248004 | tf_op jit(solution)/shard_map/sub | solution.py:275
  (576 shorter events, 962.5 us)
Async XLA Ops:
  7.2 303.1 %all-gather.9.cloned.1.call-start = ((), (), s32[]{:S(2)}) async-start(), calls=%async_computation.7 | async-start | bytes 2949120 | tf_op jit(solution)/shard_map/all_gather | solution.py:326
  10.4 328.3 %all-gather.11.cloned.1.call-start = ((), (), s32[]{:S(2)}) async-start(), calls=%async_computation.8 | async-start | bytes 2359296 | tf_op jit(solution)/shard_map/all_gather | solution.py:327
  12.3 497.2 %all-gather.13.cloned.1.call-start = ((), (), s32[]{:S(2)}) async-start(), calls=%async_computation.9 | async-start | bytes 12976128 | tf_op jit(solution)/shard_map/all_gather | solution.py:328
  13.6 517.5 %all-gather.15.cloned.1.call-start = ((), (), s32[]{:S(2)}) async-start(), calls=%async_computation.10 | async-start | bytes 6488064 | tf_op jit(solution)/shard_map/all_gather | solution.py:329
  16.1 690.3 %all-gather.17.cloned.1.call-start = ((), (), s32[]{:S(2)}) async-start(), calls=%async_computation.11 | async-start | bytes 36864000 | tf_op jit(solution)/shard_map/all_gather | solution.py:330
  72.9 26.4 %collective-permute-start = (bf16[2048,256]{1,0:T(8,128)(2,1)S(1)}, bf16[2048,256]{1,0:T(8,128)(2,1)S(1)}, u32[]{:S(2)}, u32[]{:S(2)}) collective-permute-start(bf16[2048,256]{1,0:T(8,128)(2,1)S(1)} %get-tuple-element.385), channel_id=1, source_target_pairs={{0,1},{1,2},{2,3},{4,5},{5,6},{6,7},{8,9},{9,10},{10,11},{12,13},{... | collective-permute-start | bytes 3145736 | tf_op jit(solution)/shard_map/ppermute | solution.py:219
  76.5 28.7 %collective-permute-start.3 = (bf16[2048,256]{1,0:T(8,128)(2,1)S(1)}, bf16[2048,256]{1,0:T(8,128)(2,1)}, u32[]{:S(2)}, u32[]{:S(2)}) collective-permute-start(bf16[2048,256]{1,0:T(8,128)(2,1)S(1)} %get-tuple-element.386), channel_id=1, source_target_pairs={{1,0},{2,1},{3,2},{5,4},{6,5},{7,6},{9,8},{10,9},{11,10},{13,12},{... | collective-permute-start | bytes 3145736 | tf_op jit(solution)/shard_map/ppermute | solution.py:223
  100.6 26.6 %collective-permute-start.1 = (bf16[2048,256]{1,0:T(8,128)(2,1)S(1)}, bf16[2048,256]{1,0:T(8,128)(2,1)S(1)}, u32[]{:S(2)}, u32[]{:S(2)}) collective-permute-start(bf16[2048,256]{1,0:T(8,128)(2,1)S(1)} %bitcast_add_fusion.22), channel_id=1, source_target_pairs={{0,1},{1,2},{2,3},{4,5},{5,6},{6,7},{8,9},{9,10},{10,11},{12,13},{... | collective-permute-start | bytes 3145736 | tf_op jit(solution)/shard_map/ppermute | solution.py:219
  130.8 26.6 %collective-permute-start.4 = (bf16[2048,256]{1,0:T(8,128)(2,1)}, bf16[2048,256]{1,0:T(8,128)(2,1)S(1)}, u32[]{:S(2)}, u32[]{:S(2)}) collective-permute-start(bf16[2048,256]{1,0:T(8,128)(2,1)} %get-tuple-element.384), channel_id=1, source_target_pairs={{1,0},{2,1},{3,2},{5,4},{6,5},{7,6},{9,8},{10,9},{11,10},{13,12},{... | collective-permute-start | bytes 3145736 | tf_op jit(solution)/shard_map/ppermute | solution.py:223
  132.1 27.9 %collective-permute-start.2 = (bf16[2048,256]{1,0:T(8,128)(2,1)}, bf16[2048,256]{1,0:T(8,128)(2,1)S(1)}, u32[]{:S(2)}, u32[]{:S(2)}) collective-permute-start(bf16[2048,256]{1,0:T(8,128)(2,1)} %get-tuple-element.383), channel_id=1, source_target_pairs={{0,1},{1,2},{2,3},{4,5},{5,6},{6,7},{8,9},{9,10},{10,11},{12,13},{... | collective-permute-start | bytes 3145736 | tf_op jit(solution)/shard_map/ppermute | solution.py:219
  190.1 1299.2 %reduce-scatter.12.cloned.1.call-start = ((), (), s32[]{:S(2)}) async-start(), calls=%async_computation.15 | async-start | bytes 6488064 | tf_op jit(solution)/shard_map/reduce_scatter | solution.py:395
  213.5 26.3 %collective-permute-start.6 = (bf16[256,2048]{0,1:T(8,128)(2,1)S(1)}, bf16[256,2048]{0,1:T(8,128)(2,1)}, u32[]{:S(2)}, u32[]{:S(2)}) collective-permute-start(bf16[256,2048]{0,1:T(8,128)(2,1)S(1)} %multiply_convert_fusion.6), channel_id=1, source_target_pairs={{0,1},{1,2},{2,3},{4,5},{5,6},{6,7},{8,9},{9,10},{10,11},{12,13},{... | collective-permute-start | bytes 3145736 | tf_op jit(solution)/shard_map/ppermute | solution.py:219
  217.9 27.4 %collective-permute-start.7 = (bf16[256,2048]{0,1:T(8,128)(2,1)S(1)}, bf16[256,2048]{0,1:T(8,128)(2,1)}, u32[]{:S(2)}, u32[]{:S(2)}) collective-permute-start(bf16[256,2048]{0,1:T(8,128)(2,1)S(1)} %multiply_convert_fusion.6), channel_id=1, source_target_pairs={{1,0},{2,1},{3,2},{5,4},{6,5},{7,6},{9,8},{10,9},{11,10},{13,12},{... | collective-permute-start | bytes 3145736 | tf_op jit(solution)/shard_map/ppermute | solution.py:223
  239.8 26.9 %collective-permute-start.10 = (bf16[256,2048]{0,1:T(8,128)(2,1)}, bf16[256,2048]{0,1:T(8,128)(2,1)}, u32[]{:S(2)}, u32[]{:S(2)}) collective-permute-start(bf16[256,2048]{0,1:T(8,128)(2,1)} %collective-permute-done.6), channel_id=1, source_target_pairs={{0,1},{1,2},{2,3},{4,5},{5,6},{6,7},{8,9},{9,10},{10,11},{12,13},{... | collective-permute-start | bytes 3145736 | tf_op jit(solution)/shard_map/ppermute | solution.py:219
  245.3 30.2 %collective-permute-start.8 = (bf16[256,2048]{0,1:T(8,128)(2,1)}, bf16[256,2048]{0,1:T(8,128)(2,1)}, u32[]{:S(2)}, u32[]{:S(2)}) collective-permute-start(bf16[256,2048]{0,1:T(8,128)(2,1)} %collective-permute-done.7), channel_id=1, source_target_pairs={{1,0},{2,1},{3,2},{5,4},{6,5},{7,6},{9,8},{10,9},{11,10},{13,12},{... | collective-permute-start | bytes 3145736 | tf_op jit(solution)/shard_map/ppermute | solution.py:223
  266.7 25.9 %collective-permute-start.11 = (bf16[256,2048]{0,1:T(8,128)(2,1)}, bf16[256,2048]{0,1:T(8,128)(2,1)}, u32[]{:S(2)}, u32[]{:S(2)}) collective-permute-start(bf16[256,2048]{0,1:T(8,128)(2,1)} %collective-permute-done.10), channel_id=1, source_target_pairs={{0,1},{1,2},{2,3},{4,5},{5,6},{6,7},{8,9},{9,10},{10,11},{12,13},{... | collective-permute-start | bytes 3145736 | tf_op jit(solution)/shard_map/ppermute | solution.py:219
  622.3 27.3 %collective-permute-start.31 = (bf16[256,2048]{0,1:T(8,128)(2,1)S(1)}, bf16[256,2048]{0,1:T(8,128)(2,1)}, u32[]{:S(2)}, u32[]{:S(2)}) collective-permute-start(bf16[256,2048]{0,1:T(8,128)(2,1)S(1)} %multiply_convert_fusion.4), channel_id=1, source_target_pairs={{1,0},{2,1},{3,2},{5,4},{6,5},{7,6},{9,8},{10,9},{11,10},{13,12},{... | collective-permute-start | bytes 3145736 | tf_op jit(solution)/shard_map/ppermute | solution.py:223
  644.2 27.2 %collective-permute-start.34 = (bf16[256,2048]{0,1:T(8,128)(2,1)S(1)}, bf16[256,2048]{0,1:T(8,128)(2,1)}, u32[]{:S(2)}, u32[]{:S(2)}) collective-permute-start(bf16[256,2048]{0,1:T(8,128)(2,1)S(1)} %collective-permute-done.30), channel_id=1, source_target_pairs={{0,1},{1,2},{2,3},{4,5},{5,6},{6,7},{8,9},{9,10},{10,11},{12,13},{... | collective-permute-start | bytes 3145736 | tf_op jit(solution)/shard_map/ppermute | solution.py:219
  649.6 30.8 %collective-permute-start.32 = (bf16[256,2048]{0,1:T(8,128)(2,1)}, bf16[256,2048]{0,1:T(8,128)(2,1)}, u32[]{:S(2)}, u32[]{:S(2)}) collective-permute-start(bf16[256,2048]{0,1:T(8,128)(2,1)} %collective-permute-done.31), channel_id=1, source_target_pairs={{1,0},{2,1},{3,2},{5,4},{6,5},{7,6},{9,8},{10,9},{11,10},{13,12},{... | collective-permute-start | bytes 3145736 | tf_op jit(solution)/shard_map/ppermute | solution.py:223
  843.2 27.8 %collective-permute-start.39 = (bf16[256,2048]{0,1:T(8,128)(2,1)}, bf16[256,2048]{0,1:T(8,128)(2,1)}, u32[]{:S(2)}, u32[]{:S(2)}) collective-permute-start(bf16[256,2048]{0,1:T(8,128)(2,1)} %bitcast.335), channel_id=1, source_target_pairs={{1,0},{2,1},{3,2},{5,4},{6,5},{7,6},{9,8},{10,9},{11,10},{13,12},{... | collective-permute-start | bytes 3145736 | tf_op jit(solution)/shard_map/ppermute | solution.py:223
  865.6 26.6 %collective-permute-start.37 = (bf16[256,2048]{0,1:T(8,128)(2,1)}, bf16[256,2048]{0,1:T(8,128)(2,1)}, u32[]{:S(2)}, u32[]{:S(2)}) collective-permute-start(bf16[256,2048]{0,1:T(8,128)(2,1)} %bitcast_add_fusion.10), channel_id=1, source_target_pairs={{0,1},{1,2},{2,3},{4,5},{5,6},{6,7},{8,9},{9,10},{10,11},{12,13},{... | collective-permute-start | bytes 3145736 | tf_op jit(solution)/shard_map/ppermute | solution.py:219
  873.6 26.6 %collective-permute-start.40 = (bf16[256,2048]{0,1:T(8,128)(2,1)}, bf16[256,2048]{0,1:T(8,128)(2,1)}, u32[]{:S(2)}, u32[]{:S(2)}) collective-permute-start(bf16[256,2048]{0,1:T(8,128)(2,1)} %bitcast_add_fusion.8), channel_id=1, source_target_pairs={{1,0},{2,1},{3,2},{5,4},{6,5},{7,6},{9,8},{10,9},{11,10},{13,12},{... | collective-permute-start | bytes 3145736 | tf_op jit(solution)/shard_map/ppermute | solution.py:223
  894.8 25.7 %collective-permute-start.38 = (bf16[256,2048]{0,1:T(8,128)(2,1)}, bf16[256,2048]{0,1:T(8,128)(2,1)}, u32[]{:S(2)}, u32[]{:S(2)}) collective-permute-start(bf16[256,2048]{0,1:T(8,128)(2,1)} %bitcast_add_fusion.11), channel_id=1, source_target_pairs={{0,1},{1,2},{2,3},{4,5},{5,6},{6,7},{8,9},{9,10},{10,11},{12,13},{... | collective-permute-start | bytes 3145736 | tf_op jit(solution)/shard_map/ppermute | solution.py:219
  959.8 28.8 %collective-permute-start.44 = (bf16[256,2048]{0,1:T(8,128)(2,1)}, bf16[256,2048]{0,1:T(8,128)(2,1)}, u32[]{:S(2)}, u32[]{:S(2)}) collective-permute-start(bf16[256,2048]{0,1:T(8,128)(2,1)} %collective-permute-done.43), channel_id=1, source_target_pairs={{1,0},{2,1},{3,2},{5,4},{6,5},{7,6},{9,8},{10,9},{11,10},{13,12},{... | collective-permute-start | bytes 3145736 | tf_op jit(solution)/shard_map/ppermute | solution.py:223
  1156.4 335.1 %reduce-scatter.8.cloned.1.call-start = ((), (), s32[]{:S(2)}) async-start(), calls=%async_computation.13 | async-start | bytes 2359296 | tf_op jit(solution)/shard_map/reduce_scatter | solution.py:415
  1170.5 26.4 %collective-permute-start.56 = (bf16[256,2048]{0,1:T(8,128)(2,1)S(1)}, bf16[256,2048]{0,1:T(8,128)(2,1)}, u32[]{:S(2)}, u32[]{:S(2)}) collective-permute-start(bf16[256,2048]{0,1:T(8,128)(2,1)S(1)} %collective-permute-done.55), channel_id=1, source_target_pairs={{1,0},{2,1},{3,2},{5,4},{6,5},{7,6},{9,8},{10,9},{11,10},{13,12},{... | collective-permute-start | bytes 3145736 | tf_op jit(solution)/shard_map/ppermute | solution.py:223
  1295.4 25.9 %collective-permute-start.64 = (bf16[256,2048]{0,1:T(8,128)(2,1)}, bf16[256,2048]{0,1:T(8,128)(2,1)}, u32[]{:S(2)}, u32[]{:S(2)}) collective-permute-start(bf16[256,2048]{0,1:T(8,128)(2,1)} %bitcast_add_fusion), channel_id=1, source_target_pairs={{1,0},{2,1},{3,2},{5,4},{6,5},{7,6},{9,8},{10,9},{11,10},{13,12},{... | collective-permute-start | bytes 3145736 | tf_op jit(solution)/shard_map/ppermute | solution.py:223
  1300.5 202.1 %reduce-scatter.6.cloned.1.call-start = ((), (), s32[]{:S(2)}) async-start(), calls=%async_computation.12 | async-start | bytes 2985984 | tf_op jit(solution)/shard_map/reduce_scatter | solution.py:379
  1345.1 249.3 %reduce-scatter.10.cloned.1.call-start = ((), (), s32[]{:S(2)}) async-start(), calls=%async_computation.14 | async-start | bytes 12976128 | tf_op jit(solution)/shard_map/reduce_scatter | solution.py:398
  1367.1 327.4 %reduce-scatter.14.cloned.1.call-start = ((), (), s32[]{:S(2)}) async-start(), calls=%async_computation.16 | async-start | bytes 36864000 | tf_op jit(solution)/shard_map/reduce_scatter | solution.py:379
  1495.5 43.3 %collective-permute-start.69 = (bf16[2048,256]{1,0:T(8,128)(2,1)}, bf16[2048,256]{1,0:T(8,128)(2,1)}, u32[]{:S(2)}, u32[]{:S(2)}) collective-permute-start(bf16[2048,256]{1,0:T(8,128)(2,1)} %collective-permute-done.68), channel_id=1, source_target_pairs={{1,0},{2,1},{3,2},{5,4},{6,5},{7,6},{9,8},{10,9},{11,10},{13,12},{... | collective-permute-start | bytes 3145736 | tf_op jit(solution)/shard_map/ppermute | solution.py:223
  1496.8 47.1 %collective-permute-start.71 = (bf16[2048,256]{1,0:T(8,128)(2,1)}, bf16[2048,256]{1,0:T(8,128)(2,1)}, u32[]{:S(2)}, u32[]{:S(2)}) collective-permute-start(bf16[2048,256]{1,0:T(8,128)(2,1)} %collective-permute-done.70), channel_id=1, source_target_pairs={{0,1},{1,2},{2,3},{4,5},{5,6},{6,7},{8,9},{9,10},{10,11},{12,13},{... | collective-permute-start | bytes 3145736 | tf_op jit(solution)/shard_map/ppermute | solution.py:219
  (134 other events, 3338.3 us)
Sparse Core Ops, SparseCore 0:
  10.6 32.8 all-gather.8
  45.9 28.1 all-gather.10
  76.6 67.6 all-gather.12
  146.0 44.3 all-gather.14
  192.7 164.1 all-gather.16
  1156.5 58.9 reduce-scatter.11
  1300.6 40.4 reduce-scatter.7
  1345.2 43.7 reduce-scatter.5
  1392.9 95.6 reduce-scatter.9
  1492.7 201.6 reduce-scatter.13

commit v2 on v1

v2 whole, which is shorter than its diff:
```python
import functools

import jax
import jax.numpy as jnp
from jax import lax
from jax.experimental import pallas as pl
from jax.experimental.pallas import tpu as pltpu
from jax.sharding import PartitionSpec as P

HD = 64
KVH = 4
LEN = 1024
STEP = 5

EPS = 1e-05
SCALE = 0.125
CLIP = 0.01
BETA_ONE = 0.9
BETA_TWO = 0.95
ADAM_EPS = 1e-08
RATES = (0.9, 0.01, 0.01, 0.06, 0.01, 0.01, 0.08, 0.9)
DECAYS = (0.1, 0.1, 0.1, 0.1, 0.1, 0.1, 0.1, 0.0)

LANES = 128
VMEM_LIMIT = 56 * 1024 * 1024

f32 = jnp.float32
bf16 = jnp.bfloat16


def normed(hidden, gain):
    return hidden * lax.rsqrt(jnp.mean(hidden * hidden, axis=-1, keepdims=True) + EPS) * gain


def norm_back(hidden, gain, upstream):
    _, pullback = jax.vjp(normed, hidden, gain)
    return pullback(upstream)


def rotary_tables(places):
    freqs = 10000.0 ** (-(2 * jnp.arange(HD // 2)).astype(f32) / HD)
    angles = (places % LEN).astype(f32)[:, None] * freqs[None, :]
    cosine = jnp.cos(angles)
    sine = jnp.sin(angles)
    return (
        jnp.concatenate([cosine] * 4, -1),
        jnp.concatenate([-sine, sine, -sine, sine], -1),
    )


def swap_halves(x, lane):
    half = HD // 2
    return jnp.where(
        lane % HD < half, pltpu.roll(x, LANES - half, 1), pltpu.roll(x, half, 1)
    )


def lanes_of(shape):
    return lax.broadcasted_iota(jnp.int32, shape, 1)


def turn_kernel(sign, kv_ref, cos_ref, sin_ref, out_ref):
    rows = kv_ref.shape[0]
    lane = lanes_of((rows, LANES))
    x = kv_ref[...]
    turned = x * cos_ref[...] + sign * swap_halves(x, lane) * sin_ref[...]
    out_ref[...] = jnp.where(lane < HD, turned, x).astype(bf16)


def turn_keys(kv, cosine, sine, sign, n_heads):
    rows = kv.shape[0]
    column = pl.BlockSpec((rows, LANES), lambda p: (0, p))
    whole = pl.BlockSpec((rows, LANES), lambda p: (0, 0))
    return pl.pallas_call(
        functools.partial(turn_kernel, sign),
        grid=(n_heads,),
        in_specs=[column, whole, whole],
        out_specs=column,
        out_shape=jax.ShapeDtypeStruct((rows, n_heads * LANES), bf16),
        name="turn_keys",
    )(kv, cosine, sine)


def load_keys(step, per_head, kv_ref, key_ref, value_ref):
    @pl.when(step % per_head == 0)
    def _():
        pair = kv_ref[...].astype(f32)
        other = pltpu.roll(pair, HD, 1)
        lane = lanes_of(pair.shape)
        key_ref[...] = jnp.where(lane < HD, pair, other).astype(bf16)
        value_ref[...] = jnp.where(lane < HD, other, pair).astype(bf16)


def attend_kernel(
    per_head, q_ref, kv_ref, cos_ref, sin_ref, place_ref, key_place_ref,
    mixed_ref, rope_ref, lse_ref, key_ref, value_ref,
):
    rows = q_ref.shape[0]
    half_rows, n_keys = rows // 2, kv_ref.shape[0]
    load_keys(pl.program_id(0), per_head, kv_ref, key_ref, value_ref)
    q = q_ref[...]
    rope_ref[...] = (q * cos_ref[...] + swap_halves(q, lanes_of(q.shape)) * sin_ref[...]).astype(bf16)
    low = lanes_of((half_rows, LANES)) < HD
    for block in range(2):
        at, width = block * half_rows, (block + 1) * n_keys // 2
        chosen = rope_ref[at : at + half_rows, :]
        keys, values = key_ref[:width, :], value_ref[:width, :]
        causal = key_place_ref[:, :width] <= place_ref[at : at + half_rows, :]
        outs, sums = [], []
        for part in range(2):
            mask = low if part == 0 else jnp.logical_not(low)
            one = jnp.where(mask, chosen, jnp.zeros_like(chosen))
            scores = SCALE * lax.dot_general(
                one, keys, (((1,), (1,)), ((), ())), preferred_element_type=f32
            )
            scores = jnp.where(causal, scores, -1e30)
            peak = jnp.max(scores, -1, keepdims=True)
            expo = jnp.exp(scores - peak)
            total = jnp.sum(expo, -1, keepdims=True)
            probs = (expo * (1.0 / total)).astype(bf16)
            outs.append(jnp.dot(probs, values, preferred_element_type=f32))
            sums.append(peak + jnp.log(total))
        mixed_ref[at : at + half_rows, :] = jnp.where(low, outs[0], outs[1]).astype(bf16)
        lse_ref[0, at : at + half_rows, :] = jnp.where(low, sums[0], sums[1])


def attend(kvq, kv, cosine, sine, places, key_places):
    rows, cols = kvq.shape
    n_keys, kv_cols = kv.shape
    pairs, kv_heads = (cols - kv_cols) // LANES, kv_cols // LANES
    per_head = pairs // kv_heads
    whole = pl.BlockSpec((rows, LANES), lambda p: (0, 0))
    column = pl.BlockSpec((rows, LANES), lambda p: (0, p))
    return pl.pallas_call(
        functools.partial(attend_kernel, per_head),
        grid=(pairs,),
        in_specs=[
            pl.BlockSpec((rows, LANES), lambda p: (0, p + kv_heads)),
            pl.BlockSpec((n_keys, LANES), lambda p: (0, p // per_head)),
            whole,
            whole,
            pl.BlockSpec((rows, 1), lambda p: (0, 0)),
            pl.BlockSpec((1, n_keys), lambda p: (0, 0)),
        ],
        out_specs=[column, column, pl.BlockSpec((1, rows, LANES), lambda p: (p, 0, 0))],
        out_shape=[
            jax.ShapeDtypeStruct((rows, pairs * LANES), bf16),
            jax.ShapeDtypeStruct((rows, pairs * LANES), bf16),
            jax.ShapeDtypeStruct((pairs, rows, LANES), f32),
        ],
        scratch_shapes=[pltpu.VMEM((n_keys, LANES), bf16), pltpu.VMEM((n_keys, LANES), bf16)],
        compiler_params=pltpu.CompilerParams(
            dimension_semantics=("arbitrary",), vmem_limit_bytes=VMEM_LIMIT
        ),
        name="attend",
    )(kvq, kv, cosine, sine, places, key_places)


def attend_back_kernel(
    per_head, q_ref, kv_ref, lse_ref, grad_ref, cos_ref, sin_ref, place_ref, key_place_ref,
    dq_ref, dkv_ref, key_ref, value_ref, dk_acc, dv_acc,
):
    rows = q_ref.shape[0]
    half_rows, n_keys = rows // 2, kv_ref.shape[0]
    step = pl.program_id(0)
    load_keys(step, per_head, kv_ref, key_ref, value_ref)

    @pl.when(step % per_head == 0)
    def _():
        dk_acc[...] = jnp.zeros_like(dk_acc)
        dv_acc[...] = jnp.zeros_like(dv_acc)

    lane = lanes_of((half_rows, LANES))
    low = lane < HD
    for block in range(2):
        at, width = block * half_rows, (block + 1) * n_keys // 2
        chosen = q_ref[at : at + half_rows, :]
        upstream = grad_ref[at : at + half_rows, :]
        keys, values = key_ref[:width, :], value_ref[:width, :]
        causal = key_place_ref[:, :width] <= place_ref[at : at + half_rows, :]
        outs = []
        for part in range(2):
            mask = low if part == 0 else jnp.logical_not(low)
            one = jnp.where(mask, chosen, jnp.zeros_like(chosen))
            grad = jnp.where(mask, upstream, jnp.zeros_like(upstream))
            scores = SCALE * lax.dot_general(
                one, keys, (((1,), (1,)), ((), ())), preferred_element_type=f32
            )
            lse = lse_ref[0, at : at + half_rows, part * HD : part * HD + 1]
            probs = jnp.where(causal, jnp.exp(scores - lse), 0.0)
            prob_grad = lax.dot_general(
                grad, values, (((1,), (1,)), ((), ())), preferred_element_type=f32
            )
            inner = jnp.sum(probs * prob_grad, -1, keepdims=True)
            score_grad = (probs * (prob_grad - inner)).astype(bf16)
            outs.append(jnp.dot(score_grad, keys, preferred_element_type=f32) * SCALE)
            dk_acc[:width, :] += SCALE * lax.dot_general(
                score_grad, one, (((0,), (0,)), ((), ())), preferred_element_type=f32
            )
            dv_acc[:width, :] += lax.dot_general(
                probs.astype(bf16), grad, (((0,), (0,)), ((), ())), preferred_element_type=f32
            )
        total = jnp.where(low, outs[0], outs[1])
        dq_ref[at : at + half_rows, :] = (
            total * cos_ref[at : at + half_rows, :]
            - swap_halves(total, lane) * sin_ref[at : at + half_rows, :]
        ).astype(bf16)

    @pl.when(step % per_head == per_head - 1)
    def _():
        dk, dv = dk_acc[...], dv_acc[...]
        dk = dk + pltpu.roll(dk, HD, 1)
        dv = dv + pltpu.roll(dv, HD, 1)
        dkv_ref[...] = jnp.where(lanes_of(dk.shape) < HD, dk, dv).astype(bf16)


def attend_back(rope, kv, lse, grad, cosine, sine, places, key_places):
    rows, cols = rope.shape
    n_keys, kv_cols = kv.shape
    pairs, kv_heads = cols // LANES, kv_cols // LANES
    per_head = pairs // kv_heads
    whole = pl.BlockSpec((rows, LANES), lambda p: (0, 0))
    column = pl.BlockSpec((rows, LANES), lambda p: (0, p))
    keys = pl.BlockSpec((n_keys, LANES), lambda p: (0, p // per_head))
    return pl.pallas_call(
        functools.partial(attend_back_kernel, per_head),
        grid=(pairs,),
        in_specs=[
            column,
            keys,
            pl.BlockSpec((1, rows, LANES), lambda p: (p, 0, 0)),
            column,
            whole,
            whole,
            pl.BlockSpec((rows, 1), lambda p: (0, 0)),
            pl.BlockSpec((1, n_keys), lambda p: (0, 0)),
        ],
        out_specs=[column, keys],
        out_shape=[
            jax.ShapeDtypeStruct((rows, cols), bf16),
            jax.ShapeDtypeStruct((n_keys, kv_cols), bf16),
        ],
        scratch_shapes=[
            pltpu.VMEM((n_keys, LANES), bf16),
            pltpu.VMEM((n_keys, LANES), bf16),
            pltpu.VMEM((n_keys, LANES), f32),
            pltpu.VMEM((n_keys, LANES), f32),
        ],
        compiler_params=pltpu.CompilerParams(
            dimension_semantics=("arbitrary",), vmem_limit_bytes=VMEM_LIMIT
        ),
        name="attend_back",
    )(rope, kv, lse, grad, cosine, sine, places, key_places)


def ring(x, hop):
    size = lax.axis_size("mp")
    return lax.ppermute(x, "mp", [(k, (k + hop) % size) for k in range(size)])


def ring_gather(shard):
    return [shard] + [ring(shard, hop) for hop in range(1, lax.axis_size("mp"))]


def ring_scatter(pieces):
    total = pieces[0].astype(f32)
    for hop in range(1, len(pieces)):
        total = total + ring(pieces[hop], -hop).astype(f32)
    return total


def tie(values, filler):
    return lax.optimization_barrier((values, filler))


def line_gather(shard, fillers=()):
    size = lax.axis_size("mp")
    me = lax.axis_index("mp")
    fillers = list(fillers)
    ups, downs = [shard], [shard]
    for step in range(1, size):
        up = lax.ppermute(ups[-1], "mp", [(k, k + 1) for k in range(step - 1, size - 1)])
        down = lax.ppermute(downs[-1], "mp", [(k + 1, k) for k in range(size - step)])
        if step <= len(fillers):
            (up, down), fillers[step - 1] = tie((up, down), fillers[step - 1])
        ups.append(up)
        downs.append(down)
    pieces = [shard] + [
        jnp.where(me >= hop, ups[hop], downs[size - hop]) for hop in range(1, size)
    ]
    return jnp.concatenate(pieces), fillers


def line_scatter(parts, fillers=()):
    size = lax.axis_size("mp")
    parts = parts.reshape((size, -1) + parts.shape[1:])
    fillers = list(fillers)
    up, down = None, None
    for step in range(1, size):
        mine_up, mine_down = parts[step], parts[size - step]
        if step > 1:
            mine_up, mine_down = mine_up + up, mine_down + down
        up = lax.ppermute(mine_up, "mp", [(k, k + 1) for k in range(min(step, size - 1))])
        down = lax.ppermute(
            mine_down, "mp", [(k + 1, k) for k in range(max(size - 1 - step, 0), size - 1)]
        )
        if step <= len(fillers):
            (up, down), fillers[step - 1] = tie((up, down), fillers[step - 1])
    return parts[0].astype(f32) + up.astype(f32) + down.astype(f32), fillers


def adamw(weight, grad, mean_old, square_old, factor, rate, decay):
    clipped = grad.astype(f32) * factor
    mean_new = BETA_ONE * mean_old + (1 - BETA_ONE) * clipped
    square_new = BETA_TWO * square_old + (1 - BETA_TWO) * clipped * clipped
    ratio = (
        mean_new / (1 - BETA_ONE**STEP) / (jnp.sqrt(square_new / (1 - BETA_TWO**STEP)) + ADAM_EPS)
    )
    return (weight - rate * (ratio + decay * weight), mean_new, square_new)


def dot(a, b, dims=((1,), (0,)), out=f32):
    return lax.dot_general(a, b, (dims, ((), ())), preferred_element_type=f32).astype(out)


def body(
    tokens,
    targets,
    select,
    bucket,
    embed_table,
    query_weight,
    keyvalue_weight,
    output_weight,
    gateup_weight,
    down_weight,
    head_weight,
    norm_gains,
    embed_mean,
    query_mean,
    keyvalue_mean,
    output_mean,
    gateup_mean,
    down_mean,
    head_mean,
    gains_mean,
    embed_square,
    query_square,
    keyvalue_square,
    output_square,
    gateup_square,
    down_square,
    head_square,
    gains_square,
):
    n_dp, n_mp = lax.axis_size("dp"), lax.axis_size("mp")
    group = lax.axis_index("mp")
    rows = tokens.shape[0]
    home = rows // n_mp
    strip = home // 2
    table_rows, table_cols = embed_table.shape
    vocab_start = group * table_rows
    kv_cols = keyvalue_weight.shape[1]
    q_cols = query_weight.shape[1]
    others = (group - jnp.arange(n_mp)) % n_mp

    def by_piece(x):
        strips = x.reshape(x.shape[:-1] + (2 * n_mp, strip))
        first = strips[..., others, :]
        second = strips[..., 2 * n_mp - 1 - others, :]
        return jnp.concatenate([first, second], -1)

    def pair_heads(x):
        return x.reshape(-1, 2, KVH, HD).transpose(0, 2, 1, 3).reshape(-1, kv_cols)

    scales_int = select * bucket
    ids_scales = lax.all_gather(jnp.stack([tokens, scales_int]), "dp")
    gains_rows = lax.all_gather(norm_gains.astype(bf16), "dp", axis=1, tiled=True).astype(f32)

    def ordered(pieces, axis):
        stacked = jnp.stack(pieces)
        return jnp.concatenate([stacked[(group - k) % n_mp] for k in range(n_mp)], axis)

    query_rows = ordered(ring_gather(query_weight.astype(bf16)), 1)
    kvq_own = jnp.concatenate([pair_heads(keyvalue_weight.astype(bf16)), query_rows], 1)
    kvq_full = lax.all_gather(kvq_own, "dp", axis=0, tiled=True)
    output_rows = ordered(ring_gather(output_weight.astype(bf16)), 0)
    output_full = lax.all_gather(output_rows, "dp", axis=1, tiled=True)
    gateup_full = lax.all_gather(gateup_weight.astype(bf16), "dp", axis=1, tiled=True)
    down_full = lax.all_gather(down_weight.astype(bf16), "dp", axis=1, tiled=True)
    head_full = lax.all_gather(head_weight.astype(bf16), "dp", axis=0, tiled=True)

    positions = by_piece(jnp.arange(rows))
    cosine, sine = rotary_tables(positions[0])
    key_places = jnp.concatenate([positions[:, :strip].reshape(-1), positions[:, strip:].reshape(-1)])
    places, key_places = positions[0][:, None], key_places[None, :]

    weight_total = jnp.sum(ids_scales[:, 1]).astype(f32)
    ids_local = by_piece(ids_scales[:, 0]).transpose(1, 0, 2).reshape(-1) - vocab_start
    inside = (ids_local >= 0) & (ids_local < table_rows)
    looked = embed_table[jnp.clip(ids_local, 0, table_rows - 1)]
    looked = jnp.where(inside[:, None], looked, 0.0).astype(bf16)
    looked = line_scatter(looked)[0].astype(bf16)
    looked = lax.all_to_all(looked.reshape(n_dp, home, table_cols), "dp", 0, 0)
    start_rows = looked.transpose(1, 0, 2).reshape(home, -1).astype(f32)

    first_in = normed(start_rows, gains_rows[0]).astype(bf16)
    kvq = dot(first_in, kvq_full)
    kv_own = turn_keys(kvq, cosine, sine, 1.0, KVH)
    kv_pieces = ring_gather(kv_own)
    kv = jnp.concatenate([p[:strip] for p in kv_pieces] + [p[strip:] for p in kv_pieces])
    mixed, rope, lse = attend(kvq, kv, cosine, sine, places, key_places)
    middle_rows = start_rows + dot(mixed, output_full)

    second_in, _ = line_gather(normed(middle_rows, gains_rows[1]).astype(bf16))
    gate = dot(second_in, gateup_full[0])
    upper = dot(second_in, gateup_full[1])
    active = (jax.nn.silu(gate) * upper).astype(bf16)
    final_rows = middle_rows + line_scatter(dot(active, down_full, out=bf16))[0]

    final_in, _ = line_gather(normed(final_rows, gains_rows[2]).astype(bf16))
    head_cols = head_full.shape[1]
    goals = by_piece(targets).reshape(-1) - group * head_cols
    scales = by_piece(scales_int).reshape(-1).astype(f32)
    logits = dot(final_in, head_full)
    hits = jnp.arange(head_cols)[None, :] == goals[:, None]
    local_top = jnp.max(logits, -1)
    stats = jnp.stack(
        [
            local_top,
            jnp.sum(jnp.exp(logits - local_top[:, None]), -1),
            jnp.sum(jnp.where(hits, logits, 0.0), -1),
        ]
    ).reshape(3, n_mp, home)
    stats = lax.all_gather(stats[:, others], "mp")[:, :, others].reshape(n_mp, 3, rows)
    top = jnp.max(stats[:, 0], 0)
    expsum = jnp.sum(stats[:, 1] * jnp.exp(stats[:, 0] - top[None]), 0)
    logsum_all = top + jnp.log(expsum)
    picked = jnp.sum(stats[:, 2], 0)
    loss_part = jnp.sum(scales * (logsum_all - picked)) / n_mp
    coef = scales * (1.0 / weight_total)
    logit_grad = (
        (jnp.exp(logits - logsum_all[:, None]) - hits.astype(f32)) * coef[:, None]
    ).astype(bf16)

    def reduce_to(grad, axis):
        return lax.psum_scatter(grad, "dp", scatter_dimension=axis, tiled=True)

    final_partial = dot(logit_grad, head_full, ((1,), (1,)), bf16)
    final_grad, (head_grad,) = line_scatter(
        final_partial, [dot(final_in, logit_grad, ((0,), (0,)), bf16)]
    )
    head_part = reduce_to(head_grad, 0)
    residual, final_gain = norm_back(final_rows, gains_rows[2], final_grad)

    branch, _ = line_gather(residual.astype(bf16))
    sigmoid = jax.nn.sigmoid(gate)
    silu_gate = gate * sigmoid
    active_grad = dot(branch, down_full, ((1,), (1,)))
    gate_grad = (active_grad * upper * sigmoid * (1.0 + gate * (1.0 - sigmoid))).astype(bf16)
    upper_grad = (active_grad * silu_gate).astype(bf16)
    second_partial = (
        dot(gate_grad, gateup_full[0], ((1,), (1,)))
        + dot(upper_grad, gateup_full[1], ((1,), (1,)))
    ).astype(bf16)
    second_grad, (down_grad, gate_w, upper_w) = line_scatter(
        second_partial,
        [
            dot(active, branch, ((0,), (0,)), bf16),
            dot(second_in, gate_grad, ((0,), (0,)), bf16),
            dot(second_in, upper_grad, ((0,), (0,)), bf16),
        ],
    )
    down_part = reduce_to(down_grad, 1)
    gateup_part = reduce_to(jnp.stack([gate_w, upper_w]), 1)
    middle_extra, middle_gain = norm_back(middle_rows, gains_rows[1], second_grad)
    residual = residual + middle_extra

    branch = residual.astype(bf16)
    mixed_grad = dot(branch, output_full, ((1,), (1,)), bf16)
    query_pre, kv_grad = attend_back(rope, kv, lse, mixed_grad, cosine, sine, places, key_places)
    kv_halves = kv_grad.reshape(2, n_mp, strip, kv_cols)
    kv_grad = ring_scatter([jnp.concatenate([kv_halves[0, i], kv_halves[1, i]]) for i in range(n_mp)])
    kv_grad, output_grad = tie(kv_grad, dot(mixed, branch, ((0,), (0,)), bf16))
    pair_grad = turn_keys(kv_grad, cosine, sine, -1.0, KVH)
    kvq_grad = jnp.concatenate([pair_grad, query_pre], 1)
    first_grad = dot(kvq_grad, kvq_full, ((1,), (1,)))
    start_extra, start_gain = norm_back(start_rows, gains_rows[0], first_grad)
    start_grad = (residual + start_extra).astype(bf16)
    gains_grad = jnp.stack([start_gain, middle_gain, final_gain], 1).astype(bf16)
    kvq_w = jnp.concatenate([dot(first_in, kvq_grad, ((0,), (0,)), bf16), gains_grad], 1)
    start_grad, kvq_w = tie(start_grad, kvq_w)

    kvq_w = reduce_to(kvq_w, 0)
    output_w = reduce_to(output_grad, 1)

    def piece_of(x, hop, axis, length):
        return lax.dynamic_slice_in_dim(x, (group - hop) % n_mp * length, length, axis)

    query_part = ring_scatter(
        [piece_of(kvq_w[:, kv_cols : kv_cols + q_cols * n_mp], i, 1, q_cols) for i in range(n_mp)]
    )
    output_part = ring_scatter(
        [piece_of(output_w, i, 0, output_weight.shape[0]) for i in range(n_mp)]
    )
    shared = jnp.concatenate([kvq_w[:, :kv_cols], kvq_w[:, kv_cols + q_cols * n_mp :]], 1)
    shared = ring_scatter([shared] * n_mp)
    gains_part = shared[:, kv_cols:].T
    keyvalue_part = (
        shared[:, :kv_cols].reshape(-1, KVH, 2, HD).transpose(0, 2, 1, 3).reshape(-1, kv_cols)
    )

    moved = start_grad.reshape(home, n_dp, table_cols).transpose(1, 0, 2)
    moved = lax.all_to_all(moved, "dp", 0, 0)
    moved, _ = line_gather(moved.reshape(n_dp * home, table_cols))
    onehot = (ids_local[None, :] == jnp.arange(table_rows)[:, None]).astype(bf16)
    embed_part = dot(onehot, moved)

    leading = (group == 0).astype(f32)

    def square(piece):
        piece = piece.astype(f32)
        return jnp.sum(piece * piece)

    squared = sum(
        square(piece)
        for piece in (embed_part, query_part, output_part, gateup_part, down_part, head_part)
    )
    squared = squared + leading * (square(keyvalue_part) + square(gains_part))
    squared, loss_sum = lax.psum((squared, loss_part), ("dp", "mp"))
    grad_norm = jnp.sqrt(squared)
    factor = jnp.minimum(1.0, CLIP / (grad_norm + 1e-06))
    outs = [loss_sum, weight_total, grad_norm]
    for number, (weight, grad, mean_old, square_old) in enumerate(
        (
            (embed_table, embed_part, embed_mean, embed_square),
            (query_weight, query_part, query_mean, query_square),
            (keyvalue_weight, keyvalue_part, keyvalue_mean, keyvalue_square),
            (output_weight, output_part, output_mean, output_square),
            (gateup_weight, gateup_part, gateup_mean, gateup_square),
            (down_weight, down_part, down_mean, down_square),
            (head_weight, head_part, head_mean, head_square),
            (norm_gains, gains_part, gains_mean, gains_square),
        )
    ):
        new, mean_new, square_new = adamw(
            weight, grad, mean_old, square_old, factor, RATES[number], DECAYS[number]
        )
        outs += [new, embed_part * factor if number == 0 else mean_new, square_new]
    return tuple(outs)


def solution(mesh):
    weights = (
        P("mp", "dp"),
        P("dp", "mp"),
        P("dp", None),
        P("mp", "dp"),
        P(None, "dp", "mp"),
        P("mp", "dp"),
        P("dp", "mp"),
        P(None, "dp"),
    )
    in_specs = (P("dp"),) * 4 + weights * 3
    out_specs = (P(),) * 3 + tuple(spec for spec in weights for _ in range(3))
    return jax.shard_map(body, mesh=mesh, in_specs=in_specs, out_specs=out_specs, check_vma=False)
```

time: 1830 us -> 1720 us (0.940)
  waiting for transfers between devices: 615 us -> 711 us
  other arithmetic: 256 us -> 163 us
  local copies, waits for them, and re-layouts: 213 us -> 134 us
  blocking collectives: 150 us -> 110 us
  starting transfers between devices: 218 us -> 180 us
  Pallas kernels: 46.4 us -> 78.7 us
    reduce_scatter x5, waiting for transfers between devices: 95.9 us -> 216 us  [reduce_to(): return lax.psum_scatter(grad, 'dp', scatter_dimension=axis, tiled=True)]
    dynamic_slice x35 -> x7, local copies, waits for them, and re-layouts: 75.5 us -> 7.24 us  [the longest x5 5.32 us: ordered(): stacked[(group - k) % n_mp]]
    add x23 -> x11, other arithmetic: 57 us -> 9.2 us  [the longest x8 5.06 us: line_scatter(): mine_up, mine_down = (mine_up + up, mine_down + down)]
    concatenate x1 -> x3, local copies, waits for them, and re-layouts: 1.01 us -> 43.8 us  [the longest x1 43.8 us: body(): jnp.concatenate([dot(first_in, kvq_grad, ((0,), (0,)), bf16), gains_grad]...]
    ppermute x72 -> x69, starting transfers between devices: 213 us -> 176 us  [the longest x12 62.6 us: line_scatter(): lax.ppermute(mine_up, 'mp', [(k, k + 1) for k in range(min(step, size - 1...]
    broadcast_in_dim x17 -> x0, other arithmetic: 32.4 us -> none  [the longest x15 30.8 us: line_gather(): whole = lax.dynamic_update_index_in_dim(whole, piece, (me - hop) % size, 0)]
    pallas_call x2 -> x4, Pallas kernels: 46.4 us -> 78.7 us  [the longest x1 38.5 us: attend_back(): pl.pallas_call(functools.partial(attend_back_kernel, per_head), grid=(pai...]
    broadcast_in_dim x22 -> x0, local copies, waits for them, and re-layouts: 30.6 us -> none  [the longest x15 24.4 us: line_gather(): whole = lax.dynamic_update_index_in_dim(whole, piece, (me - hop) % size, 0)]
  transfers between devices with their start and end apart: 83 -> 80, of which waited for: 48 -> 43; matrix products, arithmetic and copies ran while one was open for 28% -> 21% of each run, Pallas kernels for 3% -> 2%
where the time goes in v2:
time: 1720 us; the launch traced here: 1710 us
  waiting for transfers between devices  711 us (41%)
  matrix products  312 us (18%)
  starting transfers between devices  180 us (10%)
  other arithmetic  163 us (9%)
  local copies, waits for them, and re-layouts  134 us (8%)
  blocking collectives  110 us (6%)
  Pallas kernels  78.7 us (5%)
  between operations  26 us (2%)
    dot_general x19, matrix products, dot(): lax.dot_general(a, b, (dims, ((), ())), preferred_element_type=f32)  312 us
    reduce_scatter x5, waiting for transfers between devices, reduce_to(): return lax.psum_scatter(grad, 'dp', scatter_dimension=axis, tiled=True)  216 us
    ppermute x12, waiting for transfers between devices, line_gather(): lax.ppermute(downs[-1], 'mp', [(k + 1, k) for k in range(size - step)])  173 us
    ppermute x12, waiting for transfers between devices, line_scatter(): lax.ppermute(mine_up, 'mp', [(k, k + 1) for k in range(min(step, size - 1...  122 us
    ppermute x21, waiting for transfers between devices, ring(): return lax.ppermute(x, 'mp', [(k, (k + hop) % size) for k in range(size)])  77.1 us
    ppermute x12, waiting for transfers between devices, line_gather(): lax.ppermute(ups[-1], 'mp', [(k, k + 1) for k in range(step - 1, size - 1)])  68.4 us
    ppermute x12, starting transfers between devices, line_scatter(): lax.ppermute(mine_up, 'mp', [(k, k + 1) for k in range(min(step, size - 1...  62.6 us
    sub x8, other arithmetic, adamw(): return (weight - rate * (ratio + decay * weight), mean_new, square_new)  60.2 us
  transfers between devices with their start and end apart: 80, of which 43 were waited for; matrix products, arithmetic and copies ran while one was open for 21% of the time, Pallas kernels for 2%

profile of v2, /device:TPU:0, one launch (start us, length us, event | category | flops | bytes accessed | tf_op | source)
XLA Modules:
  0.0 1714.3 jit_solution(5731217986287208766)
XLA Ops:
  20.2 15.6 collective-permute-done.7
  51.6 18.0 %collective-permute-done.13 = bf16[512,256]{1,0:T(8,128)(2,1)S(1)} collective-permute-done((bf16[512,256]{1,0:T(8,128)(2,1)S(1)}, bf16[512,256]{1,0:T(8,128)(2,1)S(1)}, u32[]{:S(2)}, u32[]{:S(2)}) %collective-permute-start.13) | collective-permute-done | bytes 262176 | tf_op jit(solution)/shard_map/ppermute | solution.py:258
  93.0 34.6 %gather_fusion.4 = bf16[8192,256]{1,0:T(8,128)(2,1)} fusion(f32[8000,256]{1,0:T(8,128)} %param.32, s32[8192]{0:T(1024)S(1)} %broadcast_clamp_fusion), kind=kCustom, calls=%fused_computation.4 | custom fusion | bytes 8421376 | tf_op jit(solution)/shard_map/gather | solution.py:401
  135.9 22.3 %collective-permute-done = bf16[2048,256]{1,0:T(8,128)(2,1)S(1)} collective-permute-done((bf16[2048,256]{1,0:T(8,128)(2,1)S(1)}, bf16[2048,256]{1,0:T(8,128)(2,1)S(1)}, u32[]{:S(2)}, u32[]{:S(2)}) %collective-permute-start) | collective-permute-done | bytes 1048608 | tf_op jit(solution)/shard_map/ppermute | solution.py:303
  163.5 21.6 %collective-permute-done.1 = bf16[2048,256]{1,0:T(8,128)(2,1)S(1)} collective-permute-done((bf16[2048,256]{1,0:T(8,128)(2,1)S(1)}, bf16[2048,256]{1,0:T(8,128)(2,1)S(1)}, u32[]{:S(2)}, u32[]{:S(2)}) %collective-permute-start.1) | collective-permute-done | bytes 1048608 | tf_op jit(solution)/shard_map/ppermute | solution.py:303
  195.8 18.0 %collective-permute-done.5 = bf16[2048,256]{1,0:T(8,128)(2,1)S(1)} collective-permute-done((bf16[2048,256]{1,0:T(8,128)(2,1)S(1)}, bf16[2048,256]{1,0:T(8,128)(2,1)S(1)}, u32[]{:S(2)}, u32[]{:S(2)}) %collective-permute-start.5) | collective-permute-done | bytes 1048608 | tf_op jit(solution)/shard_map/ppermute | solution.py:304
  221.6 29.9 %all_gather.32 = bf16[3,2048]{1,0:T(4,128)(2,1)S(1)} all-gather(bf16[3,256]{1,0:T(4,128)(2,1)S(1)} %convert_element_type.247), channel_id=1, replica_groups=mesh['dp'=8,'mp'=4] {'dp'}, dimensions={1}, use_global_device_ids=true | all-gather | bytes 13824 | tf_op jit(solution)/shard_map/all_gather | solution.py:378
  291.2 33.0 %attend.1 = (bf16[256,2048]{1,0:T(8,128)(2,1)}, bf16[256,2048]{1,0:T(8,128)(2,1)}, f32[16,256,128]{2,1,0:T(8,128)}) custom-call(f32[256,2560]{1,0:T(8,128)} %fusion.65.kv_ref.q_ref, bf16[1024,512]{1,0:T(8,128)(2,1)} %copy-done.20, f32[256,128]{1,0:T(8,128)} %pad_maximum_fusion.18.cos_ref, f32[256,128]{1,0:T(8,128)} %pad_maximum_fusion.19.sin_ref, ...), custom_call_target="tpu_custom_call" | custom-call | tf_op jit(solution)/shard_map/attend/pallas_call | solution.py:134
  340.6 21.3 %collective-permute-done.15 = bf16[256,2048]{1,0:T(8,128)(2,1)S(1)} collective-permute-done((bf16[256,2048]{1,0:T(8,128)(2,1)S(1)}, bf16[256,2048]{1,0:T(8,128)(2,1)S(1)}, u32[]{:S(2)}, u32[]{:S(2)}) %collective-permute-start.15) | collective-permute-done | bytes 1048608 | tf_op jit(solution)/shard_map/ppermute | solution.py:282
  369.1 23.4 %collective-permute-done.17 = bf16[256,2048]{1,0:T(8,128)(2,1)} collective-permute-done((bf16[256,2048]{1,0:T(8,128)(2,1)}, bf16[256,2048]{1,0:T(8,128)(2,1)}, u32[]{:S(2)}, u32[]{:S(2)}) %collective-permute-start.17) | collective-permute-done | bytes 1048608 | tf_op jit(solution)/shard_map/ppermute | solution.py:283
  398.7 19.2 %collective-permute-done.18 = bf16[256,2048]{1,0:T(8,128)(2,1)S(1)} collective-permute-done((bf16[256,2048]{1,0:T(8,128)(2,1)}, bf16[256,2048]{1,0:T(8,128)(2,1)S(1)}, u32[]{:S(2)}, u32[]{:S(2)}) %collective-permute-start.18) | collective-permute-done | bytes 1048608 | tf_op jit(solution)/shard_map/ppermute | solution.py:283
  457.8 19.2 %collective-permute-done.21 = bf16[256,2048]{1,0:T(8,128)(2,1)S(1)} collective-permute-done((bf16[256,2048]{1,0:T(8,128)(2,1)S(1)}, bf16[256,2048]{1,0:T(8,128)(2,1)S(1)}, u32[]{:S(2)}, u32[]{:S(2)}) %collective-permute-start.21) | collective-permute-done | bytes 1048608 | tf_op jit(solution)/shard_map/ppermute | solution.py:303
  482.4 18.2 %collective-permute-done.22 = bf16[256,2048]{1,0:T(8,128)(2,1)S(1)} collective-permute-done((bf16[256,2048]{1,0:T(8,128)(2,1)S(1)}, bf16[256,2048]{1,0:T(8,128)(2,1)S(1)}, u32[]{:S(2)}, u32[]{:S(2)}) %collective-permute-start.22) | collective-permute-done | bytes 1048608 | tf_op jit(solution)/shard_map/ppermute | solution.py:303
  509.6 16.4 collective-permute-done.26
  535.2 15.7 collective-permute-done.27
  563.2 17.2 %collective-permute-done.29 = bf16[256,2048]{1,0:T(8,128)(2,1)} collective-permute-done((bf16[256,2048]{1,0:T(8,128)(2,1)S(1)}, bf16[256,2048]{1,0:T(8,128)(2,1)}, u32[]{:S(2)}, u32[]{:S(2)}) %collective-permute-start.29) | collective-permute-done | bytes 1048608 | tf_op jit(solution)/shard_map/ppermute | solution.py:283
  601.1 41.4 %fusion.85 = (f32[1024]{0:T(1024)S(1)}, f32[1024,8000]{0,1:T(8,128)}) fusion(bf16[2048,8000]{0,1:T(8,128)(2,1)} %all-gather.17.cloned.1.call-done, bf16[256,2048]{1,0:T(8,128)(2,1)S(1)} %broadcast_select_fusion.4, bf16[256,2048]{1,0:T(8,128)(2,1)S(1)} %broadcast_select_fusion.7, bf16[256,2048]{1,0:T(8,128)(2,1)} %broadcast_select_fusion.10, ...), kind=kOutput, calls=%fused_computation.283 | convolution fusion | flops 33579401216 | bytes 69734400 | tf_op jit(solution)/shard_map/dot_general | solution.py:323
  672.4 42.9 %convolution_convert_fusion.6 = bf16[1024,2048]{1,0:T(8,128)(2,1)S(1)} fusion(bf16[2048,8000]{0,1:T(8,128)(2,1)} %all-gather.17.cloned.1.call-done, f32[1024,8000]{0,1:T(8,128)} %get-tuple-element.312, f32[1024]{0:T(1024)S(1)} %get-tuple-element.303, f32[1024]{0:T(1024)S(1)} %get-tuple-element.245, s32[1024]{0:T(1024)S(1)} %bitcast.222), kind=kOutput, calls=%fused_computation.62 | convolution fusion | flops 33605681152 | bytes 69742592 | tf_op jit(solution)/shard_map/dot_general | solution.py:323
  721.1 43.4 %convolution_convert_fusion = bf16[2048,8000]{0,1:T(8,128)(2,1)} fusion(bf16[256,2048]{1,0:T(8,128)(2,1)} %copy-done.43, bf16[256,2048]{1,0:T(8,128)(2,1)} %copy-done.42, bf16[256,2048]{1,0:T(8,128)(2,1)} %broadcast_select_fusion.10, bf16[256,2048]{1,0:T(8,128)(2,1)S(1)} %multiply_convert_fusion.4, f32[1024,8000]{0,1:T(8,128)} %get-tuple-element.312, ...), kind=kOutput, calls=%fused_computation.18 | convolution fusion | flops 33636745216 | bytes 69742592 | tf_op jit(solution)/shard_map/dot_general | solution.py:323
  854.5 22.4 %collective-permute-done.41 = bf16[256,2048]{1,0:T(8,128)(2,1)S(1)} collective-permute-done((bf16[256,2048]{1,0:T(8,128)(2,1)S(1)}, bf16[256,2048]{1,0:T(8,128)(2,1)S(1)}, u32[]{:S(2)}, u32[]{:S(2)}) %collective-permute-start.41) | collective-permute-done | bytes 1048608 | tf_op jit(solution)/shard_map/ppermute | solution.py:283
  894.6 16.3 multiply_convert_fusion.1
  1015.2 38.5 %attend_back.1 = (bf16[256,2048]{1,0:T(8,128)(2,1)}, bf16[1024,512]{1,0:T(8,128)(2,1)}) custom-call(bf16[256,2048]{1,0:T(8,128)(2,1)} %get-tuple-element.57.q_ref, bf16[1024,512]{1,0:T(8,128)(2,1)} %copy-done.20, f32[16,256,128]{2,1,0:T(8,128)} %get-tuple-element.58.lse_ref, bf16[256,2048]{1,0:T(8,128)(2,1)} %convolution_convert_fusion.8.grad_ref, ...), custom_call_target="tpu_custom_call" | custom-call | tf_op jit(solution)/shard_map/attend_back/pallas_call | solution.py:225
  1088.8 43.8 %concatenate.83 = bf16[2048,2563]{0,1:T(8,128)(2,1)} concatenate(bf16[2048,2560]{0,1:T(8,128)(2,1)} %convolution_convert_fusion.1, bf16[2048,1]{0,1:T(2,128)(2,1)S(1)} %stack.91, bf16[2048,1]{0,1:T(2,128)(2,1)S(1)} %stack.92, bf16[2048,1]{0,1:T(2,128)(2,1)S(1)} %stack.93), dimensions={1} | concatenate | bytes 20996096 | tf_op jit(solution)/shard_map/concatenate | solution.py:491
  1146.9 17.9 %all_to_all.10 = bf16[8,256,256]{2,1,0:T(8,128)(2,1)S(1)} all-to-all(bf16[8,256,256]{2,1,0:T(8,128)(2,1)S(1)} %bitcast.175), channel_id=1, replica_groups=mesh['dp'=8,'mp'=4] {'dp'}, dimensions={0} | all-to-all | bytes 2097152 | tf_op jit(solution)/shard_map/all_to_all | solution.py:514
  1171.5 20.4 %collective-permute-done.54 = bf16[2048,256]{1,0:T(8,128)(2,1)S(1)} collective-permute-done((bf16[2048,256]{1,0:T(8,128)(2,1)S(1)}, bf16[2048,256]{1,0:T(8,128)(2,1)S(1)}, u32[]{:S(2)}, u32[]{:S(2)}) %collective-permute-start.54) | collective-permute-done | bytes 1048608 | tf_op jit(solution)/shard_map/ppermute | solution.py:282
  1206.1 15.4 collective-permute-done.56
  1225.9 23.1 %collective-permute-done.57 = bf16[2048,256]{1,0:T(8,128)(2,1)S(1)} collective-permute-done((bf16[2048,256]{1,0:T(8,128)(2,1)}, bf16[2048,256]{1,0:T(8,128)(2,1)S(1)}, u32[]{:S(2)}, u32[]{:S(2)}) %collective-permute-start.57) | collective-permute-done | bytes 1048608 | tf_op jit(solution)/shard_map/ppermute | solution.py:283
  1249.9 47.7 %multiply_reduce_fusion = (f32[]{:T(128)}, f32[8000,256]{1,0:T(8,128)}) fusion(s32[8192]{0:T(1024)S(1)} %bitcast.206, bf16[8192,256]{1,0:T(8,128)(2,1)S(1)} %fusion.12.clone.5), kind=kOutput, calls=%fused_computation.34 | convolution fusion | flops 33624064000 | bytes 12419076 | tf_op jit(solution)/shard_map/dot_general | solution.py:323
  1385.1 201.4 %reduce-scatter.14.cloned.1.call-done = bf16[256,8000]{0,1:T(8,128)(2,1)} async-done(((bf16[2048,8000]{0,1:T(8,128)(2,1)}), bf16[256,8000]{0,1:T(8,128)(2,1)}) %reduce-scatter.14.cloned.1.call-update) | async-done | bytes 4096016 | tf_op jit(solution)/shard_map/reduce_scatter | solution.py:447
  1592.2 39.5 %all-reduce = (f32[]{:T(128)}, f32[]{:T(128)}) all-reduce(f32[]{:T(128)S(6)} %div.173, f32[]{:T(128)S(6)} %add.534), channel_id=1, replica_groups=mesh['dp'=8,'mp'=4] {'dp','mp'}, use_global_device_ids=true, to_apply=%region_10.11 | all-reduce | flops 2 | bytes 16 | tf_op jit(solution)/shard_map/psum | solution.py:530
  1648.7 22.7 %multiply_subtract_fusion.1 = (f32[8000,256]{1,0:T(8,128)}, f32[8000,256]{1,0:T(8,128)}, f32[8000,256]{1,0:T(8,128)}) fusion(f32[8000,256]{1,0:T(8,128)} %param.32, f32[8000,256]{1,0:T(8,128)} %param.40, f32[8000,256]{1,0:T(8,128)} %param.48, f32[8000,256]{1,0:T(8,128)} %get-tuple-element.315, f32[]{:T(128)S(6)} %min.19), kind=kLoop, calls=%fused_computation.33 | loop fusion | flops 32768000 | bytes 57344004 | tf_op jit(solution)/shard_map/sub | solution.py:319
  1684.5 20.4 %multiply_subtract_fusion = (f32[256,8000]{0,1:T(8,128)}, f32[256,8000]{0,1:T(8,128)}, f32[256,8000]{0,1:T(8,128)}) fusion(f32[256,8000]{0,1:T(8,128)} %param.38, f32[]{:T(128)S(6)} %min.19, bf16[256,8000]{0,1:T(8,128)(2,1)} %reduce-scatter.14.cloned.1.call-done, f32[256,8000]{0,1:T(8,128)} %param.46, f32[256,8000]{0,1:T(8,128)} %param.54), kind=kLoop, calls=%fused_computation.32 | loop fusion | flops 34816000 | bytes 53248004 | tf_op jit(solution)/shard_map/sub | solution.py:319
  (518 shorter events, 687.6 us)
Async XLA Ops:
  7.2 248.0 %all-gather.9.cloned.1.call-start = ((), (), s32[]{:S(2)}) async-start(), calls=%async_computation.7 | async-start | bytes 11796480 | tf_op jit(solution)/shard_map/all_gather | solution.py:386
  44.1 280.1 %all-gather.11.cloned.1.call-start = ((), (), s32[]{:S(2)}) async-start(), calls=%async_computation.8 | async-start | bytes 9437184 | tf_op jit(solution)/shard_map/all_gather | solution.py:388
  70.9 348.1 %all-gather.13.cloned.1.call-start = ((), (), s32[]{:S(2)}) async-start(), calls=%async_computation.9 | async-start | bytes 12976128 | tf_op jit(solution)/shard_map/all_gather | solution.py:389
  72.3 373.5 %all-gather.15.cloned.1.call-start = ((), (), s32[]{:S(2)}) async-start(), calls=%async_computation.10 | async-start | bytes 6488064 | tf_op jit(solution)/shard_map/all_gather | solution.py:390
  74.7 526.5 %all-gather.17.cloned.1.call-start = ((), (), s32[]{:S(2)}) async-start(), calls=%async_computation.11 | async-start | bytes 36864000 | tf_op jit(solution)/shard_map/all_gather | solution.py:391
  158.3 26.8 %collective-permute-start.1 = (bf16[2048,256]{1,0:T(8,128)(2,1)S(1)}, bf16[2048,256]{1,0:T(8,128)(2,1)S(1)}, u32[]{:S(2)}, u32[]{:S(2)}) collective-permute-start(bf16[2048,256]{1,0:T(8,128)(2,1)S(1)} %get-tuple-element.270), channel_id=1, source_target_pairs={{0,1},{1,2},{4,5},{5,6},{8,9},{9,10},{12,13},{13,14},{16,17},{17,1... | collective-permute-start | bytes 3145736 | tf_op jit(solution)/shard_map/ppermute | solution.py:303
  185.5 28.4 %collective-permute-start.5 = (bf16[2048,256]{1,0:T(8,128)(2,1)S(1)}, bf16[2048,256]{1,0:T(8,128)(2,1)S(1)}, u32[]{:S(2)}, u32[]{:S(2)}) collective-permute-start(bf16[2048,256]{1,0:T(8,128)(2,1)S(1)} %get-tuple-element.269), channel_id=1, source_target_pairs={{1,0},{2,1},{3,2},{5,4},{6,5},{7,6},{9,8},{10,9},{11,10},{13,12},{... | collective-permute-start | bytes 3145736 | tf_op jit(solution)/shard_map/ppermute | solution.py:304
  186.8 28.3 %collective-permute-start.2 = (bf16[2048,256]{1,0:T(8,128)(2,1)S(1)}, bf16[2048,256]{1,0:T(8,128)(2,1)}, u32[]{:S(2)}, u32[]{:S(2)}) collective-permute-start(bf16[2048,256]{1,0:T(8,128)(2,1)S(1)} %get-tuple-element.268), channel_id=1, source_target_pairs={{0,1},{1,2},{2,3},{4,5},{5,6},{6,7},{8,9},{9,10},{10,11},{12,13},{... | collective-permute-start | bytes 3145736 | tf_op jit(solution)/shard_map/ppermute | solution.py:303
  217.9 35.8 %all-to-all-start = ((bf16[8,256,256]{2,1,0:T(8,128)(2,1)}), bf16[8,256,256]{2,1,0:T(8,128)(2,1)S(1)}, u32[]{:S(2)}, u32[]{:S(2)}) async-start(bf16[8,256,256]{2,1,0:T(8,128)(2,1)} %bitcast.12), calls=%async_computation | async-start | bytes 2097152 | tf_op jit(solution)/shard_map/all_to_all | solution.py:404
  221.5 1076.1 %reduce-scatter.8.cloned.1.call-start = ((), (), s32[]{:S(2)}) async-start(), calls=%async_computation.13 | async-start | bytes 9437184 | tf_op jit(solution)/shard_map/reduce_scatter | solution.py:447
  331.2 30.7 %collective-permute-start.15 = (bf16[256,2048]{1,0:T(8,128)(2,1)S(1)}, bf16[256,2048]{1,0:T(8,128)(2,1)S(1)}, u32[]{:S(2)}, u32[]{:S(2)}) collective-permute-start(bf16[256,2048]{1,0:T(8,128)(2,1)S(1)} %multiply_convert_fusion.5), channel_id=1, source_target_pairs={{0,1},{1,2},{2,3},{4,5},{5,6},{6,7},{8,9},{9,10},{10,11},{12,13},{... | collective-permute-start | bytes 3145736 | tf_op jit(solution)/shard_map/ppermute | solution.py:282
  339.3 26.9 %collective-permute-start.16 = (bf16[256,2048]{1,0:T(8,128)(2,1)S(1)}, bf16[256,2048]{1,0:T(8,128)(2,1)}, u32[]{:S(2)}, u32[]{:S(2)}) collective-permute-start(bf16[256,2048]{1,0:T(8,128)(2,1)S(1)} %multiply_convert_fusion.5), channel_id=1, source_target_pairs={{1,0},{2,1},{3,2},{5,4},{6,5},{7,6},{9,8},{10,9},{11,10},{13,12},{... | collective-permute-start | bytes 3145736 | tf_op jit(solution)/shard_map/ppermute | solution.py:283
  366.2 26.4 %collective-permute-start.17 = (bf16[256,2048]{1,0:T(8,128)(2,1)}, bf16[256,2048]{1,0:T(8,128)(2,1)}, u32[]{:S(2)}, u32[]{:S(2)}) collective-permute-start(bf16[256,2048]{1,0:T(8,128)(2,1)} %collective-permute-done.16), channel_id=1, source_target_pairs={{1,0},{2,1},{5,4},{6,5},{9,8},{10,9},{13,12},{14,13},{17,16},{18,1... | collective-permute-start | bytes 3145736 | tf_op jit(solution)/shard_map/ppermute | solution.py:283
  367.5 28.9 %collective-permute-start.20 = (bf16[256,2048]{1,0:T(8,128)(2,1)}, bf16[256,2048]{1,0:T(8,128)(2,1)}, u32[]{:S(2)}, u32[]{:S(2)}) collective-permute-start(bf16[256,2048]{1,0:T(8,128)(2,1)} %collective-permute-done.19), channel_id=1, source_target_pairs={{2,3},{6,7},{10,11},{14,15},{18,19},{22,23},{26,27},{30,31}} | collective-permute-start | bytes 3145736 | tf_op jit(solution)/shard_map/ppermute | solution.py:282
  718.8 45.7 %collective-permute-start.33 = (bf16[256,2048]{1,0:T(8,128)(2,1)}, bf16[256,2048]{1,0:T(8,128)(2,1)S(1)}, u32[]{:S(2)}, u32[]{:S(2)}) collective-permute-start(bf16[256,2048]{1,0:T(8,128)(2,1)} %get-tuple-element.261), channel_id=1, source_target_pairs={{0,1},{4,5},{8,9},{12,13},{16,17},{20,21},{24,25},{28,29}} | collective-permute-start | bytes 3145736 | tf_op jit(solution)/shard_map/ppermute | solution.py:303
  720.2 44.3 %collective-permute-start.34 = (bf16[256,2048]{1,0:T(8,128)(2,1)}, bf16[256,2048]{1,0:T(8,128)(2,1)S(1)}, u32[]{:S(2)}, u32[]{:S(2)}) collective-permute-start(bf16[256,2048]{1,0:T(8,128)(2,1)} %get-tuple-element.260), channel_id=1, source_target_pairs={{3,2},{7,6},{11,10},{15,14},{19,18},{23,22},{27,26},{31,30}} | collective-permute-start | bytes 3145736 | tf_op jit(solution)/shard_map/ppermute | solution.py:304
  782.2 29.7 %collective-permute-start.38 = (bf16[256,2048]{1,0:T(8,128)(2,1)S(1)}, bf16[256,2048]{1,0:T(8,128)(2,1)S(1)}, u32[]{:S(2)}, u32[]{:S(2)}) collective-permute-start(bf16[256,2048]{1,0:T(8,128)(2,1)S(1)} %get-tuple-element.257), channel_id=1, source_target_pairs={{1,0},{2,1},{3,2},{5,4},{6,5},{7,6},{9,8},{10,9},{11,10},{13,12},{... | collective-permute-start | bytes 3145736 | tf_op jit(solution)/shard_map/ppermute | solution.py:304
  783.5 35.5 %collective-permute-start.36 = (bf16[256,2048]{1,0:T(8,128)(2,1)S(1)}, bf16[256,2048]{1,0:T(8,128)(2,1)S(1)}, u32[]{:S(2)}, u32[]{:S(2)}) collective-permute-start(bf16[256,2048]{1,0:T(8,128)(2,1)S(1)} %get-tuple-element.256), channel_id=1, source_target_pairs={{0,1},{1,2},{2,3},{4,5},{5,6},{6,7},{8,9},{9,10},{10,11},{12,13},{... | collective-permute-start | bytes 3145736 | tf_op jit(solution)/shard_map/ppermute | solution.py:303
  1069.4 233.9 %reduce-scatter.6.cloned.1.call-start = ((), (), s32[]{:S(2)}) async-start(), calls=%async_computation.12 | async-start | bytes 11833344 | tf_op jit(solution)/shard_map/reduce_scatter | solution.py:447
  1135.4 170.0 %reduce-scatter.12.cloned.1.call-start = ((), (), s32[]{:S(2)}) async-start(), calls=%async_computation.15 | async-start | bytes 6488064 | tf_op jit(solution)/shard_map/reduce_scatter | solution.py:447
  1136.2 244.9 %reduce-scatter.10.cloned.1.call-start = ((), (), s32[]{:S(2)}) async-start(), calls=%async_computation.14 | async-start | bytes 12976128 | tf_op jit(solution)/shard_map/reduce_scatter | solution.py:447
  1146.2 440.2 %reduce-scatter.14.cloned.1.call-start = ((), (), s32[]{:S(2)}) async-start(), calls=%async_computation.16 | async-start | bytes 36864000 | tf_op jit(solution)/shard_map/reduce_scatter | solution.py:447
  1164.8 27.1 %collective-permute-start.54 = (bf16[2048,256]{1,0:T(8,128)(2,1)S(1)}, bf16[2048,256]{1,0:T(8,128)(2,1)S(1)}, u32[]{:S(2)}, u32[]{:S(2)}) collective-permute-start(bf16[2048,256]{1,0:T(8,128)(2,1)S(1)} %bitcast.176), channel_id=1, source_target_pairs={{0,1},{1,2},{2,3},{4,5},{5,6},{6,7},{8,9},{9,10},{10,11},{12,13},{... | collective-permute-start | bytes 3145736 | tf_op jit(solution)/shard_map/ppermute | solution.py:282
  1197.5 27.1 %collective-permute-start.59 = (bf16[2048,256]{1,0:T(8,128)(2,1)}, bf16[2048,256]{1,0:T(8,128)(2,1)}, u32[]{:S(2)}, u32[]{:S(2)}) collective-permute-start(bf16[2048,256]{1,0:T(8,128)(2,1)} %collective-permute-done.58), channel_id=1, source_target_pairs={{2,3},{6,7},{10,11},{14,15},{18,19},{22,23},{26,27},{30,31}} | collective-permute-start | bytes 3145736 | tf_op jit(solution)/shard_map/ppermute | solution.py:282
  1221.5 27.5 %collective-permute-start.57 = (bf16[2048,256]{1,0:T(8,128)(2,1)}, bf16[2048,256]{1,0:T(8,128)(2,1)S(1)}, u32[]{:S(2)}, u32[]{:S(2)}) collective-permute-start(bf16[2048,256]{1,0:T(8,128)(2,1)} %collective-permute-done.56), channel_id=1, source_target_pairs={{1,0},{5,4},{9,8},{13,12},{17,16},{21,20},{25,24},{29,28}} | collective-permute-start | bytes 3145736 | tf_op jit(solution)/shard_map/ppermute | solution.py:283
  1299.4 26.5 %collective-permute-start.64 = (bf16[512,256]{1,0:T(8,128)(2,1)S(1)}, bf16[512,256]{1,0:T(8,128)(2,1)}, u32[]{:S(2)}, u32[]{:S(2)}) collective-permute-start(bf16[512,256]{1,0:T(8,128)(2,1)S(1)} %get-tuple-element.276), channel_id=1, source_target_pairs={{0,2},{1,3},{2,0},{3,1},{4,6},{5,7},{6,4},{7,5},{8,10},{9,11},{10,... | collective-permute-start | bytes 786440 | tf_op jit(solution)/shard_map/ppermute | solution.py:258
  1299.4 31.6 %collective-permute-start.63 = (bf16[512,256]{1,0:T(8,128)(2,1)S(1)}, bf16[512,256]{1,0:T(8,128)(2,1)}, u32[]{:S(2)}, u32[]{:S(2)}) collective-permute-start(bf16[512,256]{1,0:T(8,128)(2,1)S(1)} %get-tuple-element.274), channel_id=1, source_target_pairs={{0,3},{1,0},{2,1},{3,2},{4,7},{5,4},{6,5},{7,6},{8,11},{9,8},{10,9... | collective-permute-start | bytes 786440 | tf_op jit(solution)/shard_map/ppermute | solution.py:258
  1305.0 32.6 %collective-permute-start.62 = (bf16[256,512]{0,1:T(8,128)(2,1)S(1)}, bf16[256,512]{0,1:T(8,128)(2,1)}, u32[]{:S(2)}, u32[]{:S(2)}) collective-permute-start(bf16[256,512]{0,1:T(8,128)(2,1)S(1)} %get-tuple-element.278), channel_id=1, source_target_pairs={{0,1},{1,2},{2,3},{3,0},{4,5},{5,6},{6,7},{7,4},{8,9},{9,10},{10,1... | collective-permute-start | bytes 786440 | tf_op jit(solution)/shard_map/ppermute | solution.py:258
  1307.6 44.5 %collective-permute-start.61 = (bf16[256,512]{0,1:T(8,128)(2,1)S(1)}, bf16[256,512]{0,1:T(8,128)(2,1)S(1)}, u32[]{:S(2)}, u32[]{:S(2)}) collective-permute-start(bf16[256,512]{0,1:T(8,128)(2,1)S(1)} %get-tuple-element.279), channel_id=1, source_target_pairs={{0,2},{1,3},{2,0},{3,1},{4,6},{5,7},{6,4},{7,5},{8,10},{9,11},{10,... | collective-permute-start | bytes 786440 | tf_op jit(solution)/shard_map/ppermute | solution.py:258
  1310.9 41.2 %collective-permute-start.60 = (bf16[256,512]{0,1:T(8,128)(2,1)S(1)}, bf16[256,512]{0,1:T(8,128)(2,1)S(1)}, u32[]{:S(2)}, u32[]{:S(2)}) collective-permute-start(bf16[256,512]{0,1:T(8,128)(2,1)S(1)} %get-tuple-element.277), channel_id=1, source_target_pairs={{0,3},{1,0},{2,1},{3,2},{4,7},{5,4},{6,5},{7,6},{8,11},{9,8},{10,9... | collective-permute-start | bytes 786440 | tf_op jit(solution)/shard_map/ppermute | solution.py:258
  1325.9 30.8 %collective-permute-start.68 = (bf16[256,515]{0,1:T(8,128)(2,1)}, bf16[256,515]{0,1:T(8,128)(2,1)S(1)}, u32[]{:S(2)}, u32[]{:S(2)}) collective-permute-start(bf16[256,515]{0,1:T(8,128)(2,1)} %pad_maximum_fusion.14), channel_id=1, source_target_pairs={{0,1},{1,2},{2,3},{3,0},{4,5},{5,6},{6,7},{7,4},{8,9},{9,10},{10,1... | collective-permute-start | bytes 791048 | tf_op jit(solution)/shard_map/ppermute | solution.py:258
  1331.1 32.4 %collective-permute-start.67 = (bf16[256,515]{0,1:T(8,128)(2,1)}, bf16[256,515]{0,1:T(8,128)(2,1)S(1)}, u32[]{:S(2)}, u32[]{:S(2)}) collective-permute-start(bf16[256,515]{0,1:T(8,128)(2,1)} %pad_maximum_fusion.14), channel_id=1, source_target_pairs={{0,2},{1,3},{2,0},{3,1},{4,6},{5,7},{6,4},{7,5},{8,10},{9,11},{10,... | collective-permute-start | bytes 791048 | tf_op jit(solution)/shard_map/ppermute | solution.py:258
  (138 other events, 3990.5 us)
Sparse Core Ops, SparseCore 0:
  44.2 65.9 all-gather.8
  112.7 55.8 all-gather.10
  171.1 78.6 all-gather.12
  252.1 44.6 all-gather.14
  299.1 163.9 all-gather.16
  1069.5 70.9 reduce-scatter.7
  1144.5 82.7 reduce-scatter.5
  1231.7 59.0 reduce-scatter.11
  1294.3 86.7 reduce-scatter.9
  1384.7 201.7 reduce-scatter.13

commit v3 on v2

v3 whole, which is shorter than its diff:
```python
import functools

import jax
import jax.numpy as jnp
from jax import lax
from jax.experimental import pallas as pl
from jax.experimental.pallas import tpu as pltpu
from jax.sharding import PartitionSpec as P

HD = 64
KVH = 4
LEN = 1024
STEP = 5

EPS = 1e-05
SCALE = 0.125
CLIP = 0.01
BETA_ONE = 0.9
BETA_TWO = 0.95
ADAM_EPS = 1e-08
RATES = (0.9, 0.01, 0.01, 0.06, 0.01, 0.01, 0.08, 0.9)
DECAYS = (0.1, 0.1, 0.1, 0.1, 0.1, 0.1, 0.1, 0.0)

LANES = 128
VMEM_LIMIT = 56 * 1024 * 1024

f32 = jnp.float32
bf16 = jnp.bfloat16


def normed(hidden, gain):
    return hidden * lax.rsqrt(jnp.mean(hidden * hidden, axis=-1, keepdims=True) + EPS) * gain


def norm_back(hidden, gain, upstream):
    _, pullback = jax.vjp(normed, hidden, gain)
    return pullback(upstream)


def rotary_tables(places):
    freqs = 10000.0 ** (-(2 * jnp.arange(HD // 2)).astype(f32) / HD)
    angles = (places % LEN).astype(f32)[:, None] * freqs[None, :]
    cosine = jnp.cos(angles)
    sine = jnp.sin(angles)
    return (
        jnp.concatenate([cosine] * 4, -1),
        jnp.concatenate([-sine, sine, -sine, sine], -1),
    )


def swap_halves(x, lane):
    half = HD // 2
    return jnp.where(
        lane % HD < half, pltpu.roll(x, LANES - half, 1), pltpu.roll(x, half, 1)
    )


def lanes_of(shape):
    return lax.broadcasted_iota(jnp.int32, shape, 1)


def turn_kernel(sign, kv_ref, cos_ref, sin_ref, out_ref):
    rows = kv_ref.shape[0]
    lane = lanes_of((rows, LANES))
    x = kv_ref[...]
    turned = x * cos_ref[...] + sign * swap_halves(x, lane) * sin_ref[...]
    out_ref[...] = jnp.where(lane < HD, turned, x).astype(bf16)


def turn_keys(kv, cosine, sine, sign, n_heads):
    rows = kv.shape[0]
    column = pl.BlockSpec((rows, LANES), lambda p: (0, p))
    whole = pl.BlockSpec((rows, LANES), lambda p: (0, 0))
    return pl.pallas_call(
        functools.partial(turn_kernel, sign),
        grid=(n_heads,),
        in_specs=[column, whole, whole],
        out_specs=column,
        out_shape=jax.ShapeDtypeStruct((rows, n_heads * LANES), bf16),
        name="turn_keys",
    )(kv, cosine, sine)


def load_keys(step, per_head, kv_ref, key_ref, value_ref):
    @pl.when(step % per_head == 0)
    def _():
        pair = kv_ref[...].astype(f32)
        other = pltpu.roll(pair, HD, 1)
        lane = lanes_of(pair.shape)
        key_ref[...] = jnp.where(lane < HD, pair, other).astype(bf16)
        value_ref[...] = jnp.where(lane < HD, other, pair).astype(bf16)


def both_heads(pair, low):
    zero = jnp.zeros_like(pair)
    return jnp.concatenate([jnp.where(low, pair, zero), jnp.where(low, zero, pair)])


def contract(a, b, dims):
    return lax.dot_general(a, b, (((dims[0],), (dims[1],)), ((), ())), preferred_element_type=f32)


def attend_kernel(
    per_head, q_ref, kv_ref, cos_ref, sin_ref, place_ref, key_place_ref,
    mixed_ref, rope_ref, lse_ref, key_ref, value_ref,
):
    rows = q_ref.shape[0]
    half_rows, n_keys = rows // 2, kv_ref.shape[0]
    load_keys(pl.program_id(0), per_head, kv_ref, key_ref, value_ref)
    q = q_ref[...]
    rope_ref[...] = (q * cos_ref[...] + swap_halves(q, lanes_of(q.shape)) * sin_ref[...]).astype(bf16)
    low = lanes_of((half_rows, LANES)) < HD
    for block in range(2):
        at, width = block * half_rows, (block + 1) * n_keys // 2
        chosen = both_heads(rope_ref[at : at + half_rows, :], low)
        scores = SCALE * contract(key_ref[:width, :], chosen, (1, 1))
        causal = key_place_ref[:width, :] <= place_ref[block : block + 1, :]
        scores = jnp.where(causal, scores, -1e30)
        peak = jnp.max(scores, 0, keepdims=True)
        expo = jnp.exp(scores - peak)
        total = jnp.sum(expo, 0, keepdims=True)
        probs = (expo * (1.0 / total)).astype(bf16)
        out = contract(probs, value_ref[:width, :], (0, 0))
        mixed_ref[at : at + half_rows, :] = jnp.where(
            low, out[:half_rows], out[half_rows:]
        ).astype(bf16)
        lse_ref[0, block : block + 1, :] = peak + jnp.log(total)


def attend(q, kv, cosine, sine, places, key_places):
    rows, cols = q.shape
    n_keys, kv_cols = kv.shape
    pairs, kv_heads = cols // LANES, kv_cols // LANES
    per_head = pairs // kv_heads
    whole = pl.BlockSpec((rows, LANES), lambda p: (0, 0))
    column = pl.BlockSpec((rows, LANES), lambda p: (0, p))
    return pl.pallas_call(
        functools.partial(attend_kernel, per_head),
        grid=(pairs,),
        in_specs=[
            column,
            pl.BlockSpec((n_keys, LANES), lambda p: (0, p // per_head)),
            whole,
            whole,
            pl.BlockSpec((2, rows), lambda p: (0, 0)),
            pl.BlockSpec((n_keys, 1), lambda p: (0, 0)),
        ],
        out_specs=[column, column, pl.BlockSpec((1, 2, rows), lambda p: (p, 0, 0))],
        out_shape=[
            jax.ShapeDtypeStruct((rows, cols), bf16),
            jax.ShapeDtypeStruct((rows, cols), bf16),
            jax.ShapeDtypeStruct((pairs, 2, rows), f32),
        ],
        scratch_shapes=[pltpu.VMEM((n_keys, LANES), bf16), pltpu.VMEM((n_keys, LANES), bf16)],
        compiler_params=pltpu.CompilerParams(
            dimension_semantics=("arbitrary",), vmem_limit_bytes=VMEM_LIMIT
        ),
        name="attend",
    )(q, kv, cosine, sine, places, key_places)


def attend_back_kernel(
    per_head, q_ref, kv_ref, lse_ref, grad_ref, cos_ref, sin_ref, place_ref, key_place_ref,
    dq_ref, dkv_ref, key_ref, value_ref, dk_acc, dv_acc,
):
    rows = q_ref.shape[0]
    half_rows, n_keys = rows // 2, kv_ref.shape[0]
    step = pl.program_id(0)
    load_keys(step, per_head, kv_ref, key_ref, value_ref)

    @pl.when(step % per_head == 0)
    def _():
        dk_acc[...] = jnp.zeros_like(dk_acc)
        dv_acc[...] = jnp.zeros_like(dv_acc)

    lane = lanes_of((half_rows, LANES))
    low = lane < HD
    for block in range(2):
        at, width = block * half_rows, (block + 1) * n_keys // 2
        chosen = both_heads(q_ref[at : at + half_rows, :], low)
        grad = both_heads(grad_ref[at : at + half_rows, :], low)
        keys, values = key_ref[:width, :], value_ref[:width, :]
        scores = SCALE * contract(keys, chosen, (1, 1))
        causal = key_place_ref[:width, :] <= place_ref[block : block + 1, :]
        probs = jnp.where(causal, jnp.exp(scores - lse_ref[0, block : block + 1, :]), 0.0)
        prob_grad = contract(values, grad, (1, 1))
        inner = jnp.sum(probs * prob_grad, 0, keepdims=True)
        score_grad = (probs * (prob_grad - inner)).astype(bf16)
        dk_acc[:width, :] += SCALE * contract(score_grad, chosen, (1, 0))
        dv_acc[:width, :] += contract(probs.astype(bf16), grad, (1, 0))
        out = SCALE * contract(score_grad, keys, (0, 0))
        total = jnp.where(low, out[:half_rows], out[half_rows:])
        dq_ref[at : at + half_rows, :] = (
            total * cos_ref[at : at + half_rows, :]
            - swap_halves(total, lane) * sin_ref[at : at + half_rows, :]
        ).astype(bf16)

    @pl.when(step % per_head == per_head - 1)
    def _():
        dk, dv = dk_acc[...], dv_acc[...]
        dk = dk + pltpu.roll(dk, HD, 1)
        dv = dv + pltpu.roll(dv, HD, 1)
        dkv_ref[...] = jnp.where(lanes_of(dk.shape) < HD, dk, dv).astype(bf16)


def attend_back(rope, kv, lse, grad, cosine, sine, places, key_places):
    rows, cols = rope.shape
    n_keys, kv_cols = kv.shape
    pairs, kv_heads = cols // LANES, kv_cols // LANES
    per_head = pairs // kv_heads
    whole = pl.BlockSpec((rows, LANES), lambda p: (0, 0))
    column = pl.BlockSpec((rows, LANES), lambda p: (0, p))
    keys = pl.BlockSpec((n_keys, LANES), lambda p: (0, p // per_head))
    return pl.pallas_call(
        functools.partial(attend_back_kernel, per_head),
        grid=(pairs,),
        in_specs=[
            column,
            keys,
            pl.BlockSpec((1, 2, rows), lambda p: (p, 0, 0)),
            column,
            whole,
            whole,
            pl.BlockSpec((2, rows), lambda p: (0, 0)),
            pl.BlockSpec((n_keys, 1), lambda p: (0, 0)),
        ],
        out_specs=[column, keys],
        out_shape=[
            jax.ShapeDtypeStruct((rows, cols), bf16),
            jax.ShapeDtypeStruct((n_keys, kv_cols), bf16),
        ],
        scratch_shapes=[
            pltpu.VMEM((n_keys, LANES), bf16),
            pltpu.VMEM((n_keys, LANES), bf16),
            pltpu.VMEM((n_keys, LANES), f32),
            pltpu.VMEM((n_keys, LANES), f32),
        ],
        compiler_params=pltpu.CompilerParams(
            dimension_semantics=("arbitrary",), vmem_limit_bytes=VMEM_LIMIT
        ),
        name="attend_back",
    )(rope, kv, lse, grad, cosine, sine, places, key_places)


def ring(x, hop):
    size = lax.axis_size("mp")
    return lax.ppermute(x, "mp", [(k, (k + hop) % size) for k in range(size)])


def ring_gather(shard):
    return [shard] + [ring(shard, hop) for hop in range(1, lax.axis_size("mp"))]


def ring_scatter(pieces):
    total = pieces[0].astype(f32)
    for hop in range(1, len(pieces)):
        total = total + ring(pieces[hop], -hop).astype(f32)
    return total


def tie(values, filler):
    return lax.optimization_barrier((values, filler))


def piece_order():
    size = lax.axis_size("mp")
    order = []
    for step in range(1, size // 2 + 1):
        order += [step, size - step] if 2 * step < size else [step]
    return order + [0]


def line_gather(shard):
    size = lax.axis_size("mp")
    me = lax.axis_index("mp")
    ups, downs = [shard], [shard]
    for step in range(1, size):
        ups.append(lax.ppermute(ups[-1], "mp", [(k, k + 1) for k in range(step - 1, size - 1)]))
        downs.append(lax.ppermute(downs[-1], "mp", [(k + 1, k) for k in range(size - step)]))
    pieces = [shard] + [
        jnp.where(me >= hop, ups[hop], downs[size - hop]) for hop in range(1, size)
    ]
    return jnp.concatenate([pieces[i] for i in piece_order()])


def arrivals(shard):
    size = lax.axis_size("mp")
    me = lax.axis_index("mp")
    yield me, shard
    up, downs = shard, [shard]
    for step in range(1, size):
        up = lax.ppermute(up, "mp", [(k, k + 1) for k in range(step - 1, size - 1)])
        downs.append(lax.ppermute(downs[-1], "mp", [(k + 1, k) for k in range(size - step)]))
        piece = up
        for place in range(step):
            piece = jnp.where(me == place, downs[step - place], piece)
        yield jnp.where(me >= step, me - step, step), piece


def line_scatter(parts, fillers=()):
    size = lax.axis_size("mp")
    split = []
    for part in parts:
        split += list(part.reshape((size // len(parts), -1) + part.shape[1:]))
    piece = dict(zip(piece_order(), split))
    fillers = list(fillers)
    up, down = None, None
    for step in range(1, size):
        mine_up, mine_down = piece[step], piece[size - step]
        if step > 1:
            mine_up, mine_down = mine_up + up, mine_down + down
        up = lax.ppermute(mine_up, "mp", [(k, k + 1) for k in range(min(step, size - 1))])
        down = lax.ppermute(
            mine_down, "mp", [(k + 1, k) for k in range(max(size - 1 - step, 0), size - 1)]
        )
        if step <= len(fillers):
            (up, down), fillers[step - 1] = tie((up, down), fillers[step - 1])
        if step == 2:
            (up, down), piece[0] = tie((up, down), piece[0])
    return piece[0].astype(f32) + up.astype(f32) + down.astype(f32), fillers


def halves(x):
    n = x.shape[0] // 2
    return [x[:n], x[n:]]


def adamw(weight, grad, mean_old, square_old, factor, rate, decay):
    clipped = grad.astype(f32) * factor
    mean_new = BETA_ONE * mean_old + (1 - BETA_ONE) * clipped
    square_new = BETA_TWO * square_old + (1 - BETA_TWO) * clipped * clipped
    ratio = (
        mean_new / (1 - BETA_ONE**STEP) / (jnp.sqrt(square_new / (1 - BETA_TWO**STEP)) + ADAM_EPS)
    )
    return (weight - rate * (ratio + decay * weight), mean_new, square_new)


def dot(a, b, dims=((1,), (0,)), out=f32):
    return lax.dot_general(a, b, (dims, ((), ())), preferred_element_type=f32).astype(out)


def body(
    tokens,
    targets,
    select,
    bucket,
    embed_table,
    query_weight,
    keyvalue_weight,
    output_weight,
    gateup_weight,
    down_weight,
    head_weight,
    norm_gains,
    embed_mean,
    query_mean,
    keyvalue_mean,
    output_mean,
    gateup_mean,
    down_mean,
    head_mean,
    gains_mean,
    embed_square,
    query_square,
    keyvalue_square,
    output_square,
    gateup_square,
    down_square,
    head_square,
    gains_square,
):
    n_dp, n_mp = lax.axis_size("dp"), lax.axis_size("mp")
    group = lax.axis_index("mp")
    rows = tokens.shape[0]
    home = rows // n_mp
    strip = home // 2
    table_rows, table_cols = embed_table.shape
    vocab_start = group * table_rows
    kv_cols = keyvalue_weight.shape[1]
    q_cols = query_weight.shape[1]
    ring_order = (group - jnp.arange(n_mp)) % n_mp
    line_order = (group - jnp.array(piece_order())) % n_mp

    def by_piece(x, order):
        strips = x.reshape(x.shape[:-1] + (2 * n_mp, strip))
        first = strips[..., order, :]
        second = strips[..., 2 * n_mp - 1 - order, :]
        return jnp.concatenate([first, second], -1)

    def pair_heads(x):
        return x.reshape(-1, 2, KVH, HD).transpose(0, 2, 1, 3).reshape(-1, kv_cols)

    scales_int = select * bucket
    meta = jnp.concatenate(
        [tokens.astype(f32), scales_int.astype(f32), norm_gains.astype(bf16).astype(f32).reshape(-1)]
    )
    meta = lax.all_gather(meta, "dp")
    ids = meta[:, :rows].astype(jnp.int32)
    gains_rows = meta[:, 2 * rows :].reshape(n_dp, 3, -1).transpose(1, 0, 2).reshape(3, -1)

    def ordered(pieces, axis):
        stacked = jnp.stack(pieces)
        return jnp.concatenate([stacked[(group - k) % n_mp] for k in range(n_mp)], axis)

    weight_total = jnp.sum(meta[:, rows : 2 * rows])
    ids_local = by_piece(ids, line_order).transpose(1, 0, 2) - vocab_start

    def look_up(piece_ids):
        inside = (piece_ids >= 0) & (piece_ids < table_rows)
        found = embed_table[jnp.clip(piece_ids, 0, table_rows - 1)]
        return jnp.where(inside[:, None], found, 0.0).astype(bf16)

    looked = [look_up(ids_local[i].reshape(-1)) for i in range(n_mp)]
    ids_local = ids_local.reshape(-1)

    query_pieces = ring_gather(query_weight.astype(bf16))
    output_pieces = ring_gather(output_weight.astype(bf16))
    looked[: n_mp // 2], (query_pieces, output_pieces) = tie(
        looked[: n_mp // 2], (query_pieces, output_pieces)
    )
    kvq_own = jnp.concatenate(
        [pair_heads(keyvalue_weight.astype(bf16)), ordered(query_pieces, 1)], 1
    )
    kvq_full = lax.all_gather(kvq_own, "dp", axis=0, tiled=True)
    looked, (gateup_own, down_own, head_own) = line_scatter(
        looked,
        [
            gateup_weight.astype(bf16).transpose(1, 0, 2).reshape(table_cols, -1),
            down_weight.astype(bf16),
            head_weight.astype(bf16),
        ],
    )
    output_own = ordered(output_pieces, 0)
    gateup_full = lax.all_gather(gateup_own, "dp", axis=0, tiled=True)
    output_full = lax.all_gather(output_own, "dp", axis=1, tiled=True)
    down_full = lax.all_gather(down_own, "dp", axis=1, tiled=True)
    head_full = lax.all_gather(head_own, "dp", axis=0, tiled=True)

    positions = by_piece(jnp.arange(rows), ring_order)
    cosine, sine = rotary_tables(positions[0])
    key_places = jnp.concatenate([positions[:, :strip].reshape(-1), positions[:, strip:].reshape(-1)])
    places, key_places = jnp.tile(positions[0].reshape(2, strip), (1, 2)), key_places[:, None]

    looked = looked.astype(bf16)
    looked = lax.all_to_all(looked.reshape(n_dp, home, table_cols), "dp", 0, 0)
    start_rows = looked.transpose(1, 0, 2).reshape(home, -1).astype(f32)

    first_in = normed(start_rows, gains_rows[0]).astype(bf16)
    kv_own = turn_keys(dot(first_in, kvq_full[:, :kv_cols]), cosine, sine, 1.0, KVH)
    queries = dot(first_in, kvq_full[:, kv_cols:])
    kv_pieces = ring_gather(kv_own)
    kv = jnp.concatenate([p[:strip] for p in kv_pieces] + [p[strip:] for p in kv_pieces])
    mixed, rope, lse = attend(queries, kv, cosine, sine, places, key_places)
    middle_rows = start_rows + dot(mixed, output_full)

    second_in = line_gather(normed(middle_rows, gains_rows[1]).astype(bf16))
    gate_upper = dot(second_in, gateup_full)
    half = gate_upper.shape[1] // 2
    gate, upper = gate_upper[:, :half], gate_upper[:, half:]
    active = (jax.nn.silu(gate) * upper).astype(bf16)
    final_rows = middle_rows + line_scatter([dot(a, down_full, out=bf16) for a in halves(active)])[0]

    final_in = line_gather(normed(final_rows, gains_rows[2]).astype(bf16))
    head_cols = head_full.shape[1]
    goals = by_piece(targets, line_order).reshape(-1) - group * head_cols
    scales = by_piece(scales_int, line_order).reshape(-1).astype(f32)
    logits = dot(final_in, head_full)
    hits = jnp.arange(head_cols)[None, :] == goals[:, None]
    local_top = jnp.max(logits, -1)
    stats = jnp.stack(
        [
            local_top,
            jnp.sum(jnp.exp(logits - local_top[:, None]), -1),
            jnp.sum(jnp.where(hits, logits, 0.0), -1),
        ]
    ).reshape(3, n_mp, home)
    back = [piece_order().index(i) for i in range(n_mp)]
    stats = stats[:, jnp.array(back)[ring_order]]
    stats = jnp.stack(ring_gather(stats))[:, :, line_order].reshape(n_mp, 3, rows)
    top = jnp.max(stats[:, 0], 0)
    expsum = jnp.sum(stats[:, 1] * jnp.exp(stats[:, 0] - top[None]), 0)
    logsum_all = top + jnp.log(expsum)
    picked = jnp.sum(stats[:, 2], 0)
    loss_part = jnp.sum(scales * (logsum_all - picked)) / n_mp
    coef = scales * (1.0 / weight_total)
    logit_grad = (
        (jnp.exp(logits - logsum_all[:, None]) - hits.astype(f32)) * coef[:, None]
    ).astype(bf16)

    def reduce_to(grad, axis):
        return lax.psum_scatter(grad, "dp", scatter_dimension=axis, tiled=True)

    final_partial = [dot(logit_grad, head_full, ((1,), (1,)), bf16)]
    final_grad, (head_grad,) = line_scatter(
        final_partial, [dot(final_in, logit_grad, ((0,), (0,)), bf16)]
    )
    head_part = reduce_to(head_grad, 0)
    residual, final_gain = norm_back(final_rows, gains_rows[2], final_grad)

    branch = line_gather(residual.astype(bf16))
    sigmoid = jax.nn.sigmoid(gate)
    silu_gate = gate * sigmoid
    active_grad = dot(branch, down_full, ((1,), (1,)))
    gate_grad = (active_grad * upper * sigmoid * (1.0 + gate * (1.0 - sigmoid))).astype(bf16)
    upper_grad = (active_grad * silu_gate).astype(bf16)
    gateup_grad = jnp.concatenate([gate_grad, upper_grad], 1)
    second_partial = [dot(g, gateup_full, ((1,), (1,)), bf16) for g in halves(gateup_grad)]
    second_grad, (down_grad, gateup_w) = line_scatter(
        second_partial,
        [
            dot(active, branch, ((0,), (0,)), bf16),
            dot(second_in, gateup_grad, ((0,), (0,)), bf16),
        ],
    )
    (down_grad, gateup_w), head_part = tie((down_grad, gateup_w), head_part)
    down_part = reduce_to(down_grad, 1)
    gateup_part = reduce_to(gateup_w, 0)
    middle_extra, middle_gain = norm_back(middle_rows, gains_rows[1], second_grad)
    residual = residual + middle_extra

    branch = residual.astype(bf16)
    branch, output_w = tie(branch, dot(mixed, branch, ((0,), (0,)), bf16))
    output_w, down_part = tie(output_w, down_part)
    output_w = reduce_to(output_w, 1)
    mixed_grad = dot(branch, output_full, ((1,), (1,)), bf16)
    query_pre, kv_grad = attend_back(rope, kv, lse, mixed_grad, cosine, sine, places, key_places)
    kv_halves = kv_grad.reshape(2, n_mp, strip, kv_cols)
    kv_grad = ring_scatter([jnp.concatenate([kv_halves[0, i], kv_halves[1, i]]) for i in range(n_mp)])
    pair_grad = turn_keys(kv_grad, cosine, sine, -1.0, KVH)
    kvq_grad = jnp.concatenate([pair_grad, query_pre], 1)
    kvq_grad, kvq_w = tie(kvq_grad, dot(first_in, kvq_grad, ((0,), (0,)), bf16))
    first_grad = dot(kvq_grad, kvq_full, ((1,), (1,)))
    start_extra, start_gain = norm_back(start_rows, gains_rows[0], first_grad)
    start_grad = (residual + start_extra).astype(bf16)
    gains_grad = jnp.stack([start_gain, middle_gain, final_gain]).astype(bf16)

    def piece_of(x, hop, axis, length):
        return lax.dynamic_slice_in_dim(x, (group - hop) % n_mp * length, length, axis)

    moved = jnp.concatenate([start_grad, gains_grad, jnp.zeros((13, start_grad.shape[1]), bf16)])
    moved = moved.reshape(-1, n_dp, table_cols).transpose(1, 0, 2)
    moved = lax.all_to_all(moved, "dp", 0, 0)
    kvq_w, (gateup_part, _) = tie(kvq_w, (gateup_part, moved[0, :16]))
    gateup_part = gateup_part.reshape(table_cols, 2, -1).transpose(1, 0, 2)
    gains_part = ring_scatter([jnp.sum(moved[:, home : home + 3].astype(f32), 0)] * n_mp)
    embed_part = None
    ids_home = by_piece(ids, jnp.arange(n_mp)).transpose(1, 0, 2).reshape(n_mp, -1) - vocab_start
    for device, shard in arrivals(moved[:, :home].reshape(n_dp * home, table_cols)):
        onehot = (ids_home[device][None, :] == jnp.arange(table_rows)[:, None]).astype(bf16)
        part = dot(onehot, shard)
        embed_part = part if embed_part is None else embed_part + part

    kvq_w = reduce_to(kvq_w, 0)
    output_w, embed_part = tie(output_w, embed_part)
    query_part = ring_scatter(
        [piece_of(kvq_w[:, kv_cols:], i, 1, q_cols) for i in range(n_mp)]
    )
    keyvalue_part = ring_scatter([kvq_w[:, :kv_cols]] * n_mp)
    keyvalue_part = keyvalue_part.reshape(-1, KVH, 2, HD).transpose(0, 2, 1, 3).reshape(-1, kv_cols)
    output_part = ring_scatter(
        [piece_of(output_w, i, 0, output_weight.shape[0]) for i in range(n_mp)]
    )

    leading = (group == 0).astype(f32)

    def square(piece):
        piece = piece.astype(f32)
        return jnp.sum(piece * piece)

    squared = sum(
        square(piece)
        for piece in (embed_part, query_part, output_part, gateup_part, down_part, head_part)
    )
    squared = squared + leading * (square(keyvalue_part) + square(gains_part))
    totals = jnp.stack([squared, loss_part])[:, None]
    totals = sum(ring_gather(totals))
    hop = 1
    while hop < n_dp:
        totals = totals + lax.ppermute(totals, "dp", [(k, k ^ hop) for k in range(n_dp)])
        hop *= 2
    grad_norm, loss_sum = jnp.sqrt(totals[0, 0]), totals[1, 0]
    factor = jnp.minimum(1.0, CLIP / (grad_norm + 1e-06))
    outs = [loss_sum, weight_total, grad_norm]
    for number, (weight, grad, mean_old, square_old) in enumerate(
        (
            (embed_table, embed_part, embed_mean, embed_square),
            (query_weight, query_part, query_mean, query_square),
            (keyvalue_weight, keyvalue_part, keyvalue_mean, keyvalue_square),
            (output_weight, output_part, output_mean, output_square),
            (gateup_weight, gateup_part, gateup_mean, gateup_square),
            (down_weight, down_part, down_mean, down_square),
            (head_weight, head_part, head_mean, head_square),
            (norm_gains, gains_part, gains_mean, gains_square),
        )
    ):
        new, mean_new, square_new = adamw(
            weight, grad, mean_old, square_old, factor, RATES[number], DECAYS[number]
        )
        outs += [new, embed_part * factor if number == 0 else mean_new, square_new]
    return tuple(outs)


def solution(mesh):
    weights = (
        P("mp", "dp"),
        P("dp", "mp"),
        P("dp", None),
        P("mp", "dp"),
        P(None, "dp", "mp"),
        P("mp", "dp"),
        P("dp", "mp"),
        P(None, "dp"),
    )
    in_specs = (P("dp"),) * 4 + weights * 3
    out_specs = (P(),) * 3 + tuple(spec for spec in weights for _ in range(3))
    return jax.shard_map(body, mesh=mesh, in_specs=in_specs, out_specs=out_specs, check_vma=False)
```

time: 1720 us -> 1380 us (0.80)
  waiting for transfers between devices: 711 us -> 530 us
  blocking collectives: 110 us -> 27.9 us
  local copies, waits for them, and re-layouts: 134 us -> 74.8 us
  starting transfers between devices: 180 us -> 156 us
    reduce_scatter x5, waiting for transfers between devices: 216 us -> 41.5 us  [reduce_to(): return lax.psum_scatter(grad, 'dp', scatter_dimension=axis, tiled=True)]
    ppermute x12 -> x9, waiting for transfers between devices: 68.4 us -> 0.02 us  [line_gather(): lax.ppermute(ups[-1], 'mp', [(k, k + 1) for k in range(step - 1, size - 1)])]
    concatenate x2, local copies, waits for them, and re-layouts: 43.8 us -> 0.53 us  [the longest x1 0.51 us: body(): jnp.concatenate([start_grad, gains_grad, jnp.zeros((13, start_grad.shape[...]
    all_gather x3 -> x1, blocking collectives: 52.2 us -> 9.27 us  [body(): meta = lax.all_gather(meta, 'dp')]
    ppermute x0 -> x9, waiting for transfers between devices: none -> 40.1 us  [the longest x3 21.6 us: arrivals(): lax.ppermute(downs[-1], 'mp', [(k + 1, k) for k in range(size - step)])]
    psum x1 -> x0, blocking collectives: 39.5 us -> none  [body(): squared, loss_sum = lax.psum((squared, loss_part), ('dp', 'mp'))]
    ppermute x12, waiting for transfers between devices: 122 us -> 156 us  [line_scatter(): lax.ppermute(mine_up, 'mp', [(k, k + 1) for k in range(min(step, size - 1...]
    ppermute x12, waiting for transfers between devices: 53.2 us -> 24.4 us  [line_scatter(): lax.ppermute(mine_down, 'mp', [(k + 1, k) for k in range(max(size - 1 - s...]
  transfers between devices with their start and end apart: 80 -> 92, of which waited for: 43 -> 47; matrix products, arithmetic and copies ran while one was open for 21% -> 28% of each run, Pallas kernels for 2% -> 5%
where the time goes in v3:
time: 1380 us; the launch traced here: 1370 us
  waiting for transfers between devices  530 us (38%)
  matrix products  324 us (23%)
  other arithmetic  162 us (12%)
  starting transfers between devices  156 us (11%)
  local copies, waits for them, and re-layouts  74.8 us (5%)
  Pallas kernels  72.1 us (5%)
  blocking collectives  27.9 us (2%)
  between operations  25.6 us (2%)
    dot_general x22, matrix products, dot(): lax.dot_general(a, b, (dims, ((), ())), preferred_element_type=f32)  324 us
    ppermute x9, waiting for transfers between devices, line_gather(): lax.ppermute(downs[-1], 'mp', [(k + 1, k) for k in range(size - step)])  177 us
    ppermute x12, waiting for transfers between devices, line_scatter(): lax.ppermute(mine_up, 'mp', [(k, k + 1) for k in range(min(step, size - 1...  156 us
    ppermute x30, waiting for transfers between devices, ring(): return lax.ppermute(x, 'mp', [(k, (k + hop) % size) for k in range(size)])  76.5 us
    sub x8, other arithmetic, adamw(): return (weight - rate * (ratio + decay * weight), mean_new, square_new)  59.5 us
    ppermute x30, starting transfers between devices, ring(): return lax.ppermute(x, 'mp', [(k, (k + hop) % size) for k in range(size)])  46.8 us
    ppermute x12, starting transfers between devices, line_scatter(): lax.ppermute(mine_up, 'mp', [(k, k + 1) for k in range(min(step, size - 1...  45.4 us
    reduce_scatter x5, waiting for transfers between devices, reduce_to(): return lax.psum_scatter(grad, 'dp', scatter_dimension=axis, tiled=True)  41.5 us
  transfers between devices with their start and end apart: 92, of which 47 were waited for; matrix products, arithmetic and copies ran while one was open for 28% of the time, Pallas kernels for 5%

profile of v3, /device:TPU:0, one launch (start us, length us, event | category | flops | bytes accessed | tf_op | source)
XLA Modules:
  0.0 1372.5 jit_solution(10452683273001676914)
XLA Ops:
  76.3 18.4 %collective-permute-done.6 = bf16[2048,256]{1,0:T(8,128)(2,1)} collective-permute-done((bf16[2048,256]{1,0:T(8,128)(2,1)}, bf16[2048,256]{1,0:T(8,128)(2,1)}, u32[]{:S(2)}, u32[]{:S(2)}) %collective-permute-start.6) | collective-permute-done | bytes 1048608 | tf_op jit(solution)/shard_map/ppermute | solution.py:312
  115.6 20.1 %collective-permute-done.8 = bf16[2048,256]{1,0:T(8,128)(2,1)S(1)} collective-permute-done((bf16[2048,256]{1,0:T(8,128)(2,1)S(1)}, bf16[2048,256]{1,0:T(8,128)(2,1)S(1)}, u32[]{:S(2)}, u32[]{:S(2)}) %collective-permute-start.8) | collective-permute-done | bytes 1048608 | tf_op jit(solution)/shard_map/ppermute | solution.py:312
  240.2 31.3 %attend.1 = (bf16[256,2048]{1,0:T(8,128)(2,1)}, bf16[256,2048]{1,0:T(8,128)(2,1)}, f32[16,2,256]{2,1,0:T(2,128)}) custom-call(f32[256,2048]{1,0:T(8,128)} %fusion.12.q_ref, bf16[1024,512]{1,0:T(8,128)(2,1)} %copy-done.25, f32[256,128]{1,0:T(8,128)} %pad_maximum_fusion.18.cos_ref, f32[256,128]{1,0:T(8,128)} %pad_maximum_fusion.19.sin_ref, ...), custom_call_target="tpu_custom_call" | custom-call | tf_op jit(solution)/shard_map/attend/pallas_call | solution.py:137
  285.7 18.3 %collective-permute-done.16 = bf16[256,2048]{1,0:T(8,128)(2,1)S(1)} collective-permute-done((bf16[256,2048]{1,0:T(8,128)(2,1)S(1)}, bf16[256,2048]{1,0:T(8,128)(2,1)S(1)}, u32[]{:S(2)}, u32[]{:S(2)}) %collective-permute-start.16) | collective-permute-done | bytes 1048608 | tf_op jit(solution)/shard_map/ppermute | solution.py:279
  307.0 23.2 %collective-permute-done.17 = bf16[256,2048]{1,0:T(8,128)(2,1)} collective-permute-done((bf16[256,2048]{1,0:T(8,128)(2,1)S(1)}, bf16[256,2048]{1,0:T(8,128)(2,1)}, u32[]{:S(2)}, u32[]{:S(2)}) %collective-permute-start.17) | collective-permute-done | bytes 1048608 | tf_op jit(solution)/shard_map/ppermute | solution.py:279
  335.1 20.5 %collective-permute-done.18 = bf16[256,2048]{1,0:T(8,128)(2,1)} collective-permute-done((bf16[256,2048]{1,0:T(8,128)(2,1)}, bf16[256,2048]{1,0:T(8,128)(2,1)}, u32[]{:S(2)}, u32[]{:S(2)}) %collective-permute-start.18) | collective-permute-done | bytes 1048608 | tf_op jit(solution)/shard_map/ppermute | solution.py:279
  359.1 18.9 %fusion.53 = f32[1024,2816]{1,0:T(8,128)} fusion(bf16[2048,2816]{0,1:T(8,128)(2,1)} %all-gather.12.cloned.1.call-done, bf16[256,2048]{1,0:T(8,128)(2,1)S(1)} %multiply_convert_fusion.5, bf16[256,2048]{1,0:T(8,128)(2,1)} %broadcast_select_fusion.2, bf16[256,2048]{1,0:T(8,128)(2,1)} %broadcast_select_fusion.5, bf16[256,2048]{1,0:T(8,128)(2,1)} %broadcast_select_fusion.8), kind=kOutput, calls=%fused_computation.164 | convolution fusion | flops 11827937280 | bytes 27262976 | tf_op jit(solution)/shard_map/dot_general | solution.py:339
  400.4 16.2 %collective-permute-done.21 = bf16[256,2048]{1,0:T(8,128)(2,1)S(1)} collective-permute-done((bf16[256,2048]{1,0:T(8,128)(2,1)S(1)}, bf16[256,2048]{1,0:T(8,128)(2,1)S(1)}, u32[]{:S(2)}, u32[]{:S(2)}) %collective-permute-start.21) | collective-permute-done | bytes 1048608 | tf_op jit(solution)/shard_map/ppermute | solution.py:312
  422.6 19.0 %collective-permute-done.22 = bf16[256,2048]{1,0:T(8,128)(2,1)S(1)} collective-permute-done((bf16[256,2048]{1,0:T(8,128)(2,1)S(1)}, bf16[256,2048]{1,0:T(8,128)(2,1)S(1)}, u32[]{:S(2)}, u32[]{:S(2)}) %collective-permute-start.22) | collective-permute-done | bytes 1048608 | tf_op jit(solution)/shard_map/ppermute | solution.py:312
  448.3 17.3 %collective-permute-done.25 = bf16[256,2048]{1,0:T(8,128)(2,1)S(1)} collective-permute-done((bf16[256,2048]{1,0:T(8,128)(2,1)S(1)}, bf16[256,2048]{1,0:T(8,128)(2,1)S(1)}, u32[]{:S(2)}, u32[]{:S(2)}) %collective-permute-start.25) | collective-permute-done | bytes 1048608 | tf_op jit(solution)/shard_map/ppermute | solution.py:312
  478.8 17.4 %collective-permute-done.28 = bf16[256,2048]{1,0:T(8,128)(2,1)S(1)} collective-permute-done((bf16[256,2048]{1,0:T(8,128)(2,1)S(1)}, bf16[256,2048]{1,0:T(8,128)(2,1)S(1)}, u32[]{:S(2)}, u32[]{:S(2)}) %collective-permute-start.28) | collective-permute-done | bytes 1048608 | tf_op jit(solution)/shard_map/ppermute | solution.py:279
  499.2 20.4 %collective-permute-done.29 = bf16[256,2048]{1,0:T(8,128)(2,1)S(1)} collective-permute-done((bf16[256,2048]{1,0:T(8,128)(2,1)S(1)}, bf16[256,2048]{1,0:T(8,128)(2,1)S(1)}, u32[]{:S(2)}, u32[]{:S(2)}) %collective-permute-start.29) | collective-permute-done | bytes 1048608 | tf_op jit(solution)/shard_map/ppermute | solution.py:279
  524.4 15.9 %collective-permute-done.30 = bf16[256,2048]{1,0:T(8,128)(2,1)} collective-permute-done((bf16[256,2048]{1,0:T(8,128)(2,1)S(1)}, bf16[256,2048]{1,0:T(8,128)(2,1)}, u32[]{:S(2)}, u32[]{:S(2)}) %collective-permute-start.30) | collective-permute-done | bytes 1048608 | tf_op jit(solution)/shard_map/ppermute | solution.py:279
  542.9 41.5 %fusion.110 = (f32[1024]{0:T(1024)S(1)}, f32[1024,8000]{0,1:T(8,128)}) fusion(bf16[2048,8000]{0,1:T(8,128)(2,1)} %all-gather.16.cloned.1.call-done, bf16[256,2048]{1,0:T(8,128)(2,1)S(1)} %multiply_convert_fusion.4, bf16[256,2048]{1,0:T(8,128)(2,1)S(1)} %broadcast_select_fusion.1, bf16[256,2048]{1,0:T(8,128)(2,1)} %broadcast_select_fusion.4, ...), kind=kOutput, calls=%fused_computation.362 | convolution fusion | flops 33579401216 | bytes 69734400 | tf_op jit(solution)/shard_map/dot_general | solution.py:339
  584.4 14.8 %exponential_reduce_fusion = (f32[1024]{0:T(1024)S(1)}, f32[1024]{0:T(1024)S(1)}) fusion(f32[1024,8000]{0,1:T(8,128)} %get-tuple-element.268, f32[1024]{0:T(1024)S(1)} %get-tuple-element.267, s32[1024]{0:T(1024)S(1)} %bitcast.284), kind=kLoop, calls=%fused_computation.32 | loop fusion | flops 40957952 | bytes 32784384 | tf_op jit(solution)/shard_map/reduce_sum | solution.py:473
  608.8 43.0 %convolution_convert_fusion.5 = bf16[1024,2048]{1,0:T(8,128)(2,1)S(1)} fusion(bf16[2048,8000]{0,1:T(8,128)(2,1)} %all-gather.16.cloned.1.call-done, f32[1024,8000]{0,1:T(8,128)} %get-tuple-element.268, f32[1024]{0:T(1024)S(1)} %get-tuple-element.257, f32[1024]{0:T(1024)S(1)} %get-tuple-element.186, s32[1024]{0:T(1024)S(1)} %bitcast.285), kind=kOutput, calls=%fused_computation.70 | convolution fusion | flops 33605681152 | bytes 69742592 | tf_op jit(solution)/shard_map/dot_general | solution.py:339
  658.9 43.3 %convolution_convert_fusion = bf16[2048,8000]{0,1:T(8,128)(2,1)} fusion(bf16[256,2048]{1,0:T(8,128)(2,1)S(1)} %multiply_convert_fusion.4, bf16[256,2048]{1,0:T(8,128)(2,1)} %copy-done.50, bf16[256,2048]{1,0:T(8,128)(2,1)} %broadcast_select_fusion.4, bf16[256,2048]{1,0:T(8,128)(2,1)} %copy-done.51, f32[1024,8000]{0,1:T(8,128)} %get-tuple-element.268, ...), kind=kOutput, calls=%fused_computation.33 | convolution fusion | flops 33636745216 | bytes 69742592 | tf_op jit(solution)/shard_map/dot_general | solution.py:339
  707.6 18.5 %collective-permute-done.38 = bf16[256,2048]{1,0:T(8,128)(2,1)S(1)} collective-permute-done((bf16[256,2048]{1,0:T(8,128)(2,1)S(1)}, bf16[256,2048]{1,0:T(8,128)(2,1)S(1)}, u32[]{:S(2)}, u32[]{:S(2)}) %collective-permute-start.38) | collective-permute-done | bytes 1048608 | tf_op jit(solution)/shard_map/ppermute | solution.py:312
  764.2 21.8 %collective-permute-done.43 = bf16[256,2048]{1,0:T(8,128)(2,1)S(1)} collective-permute-done((bf16[256,2048]{1,0:T(8,128)(2,1)S(1)}, bf16[256,2048]{1,0:T(8,128)(2,1)S(1)}, u32[]{:S(2)}, u32[]{:S(2)}) %collective-permute-start.43) | collective-permute-done | bytes 1048608 | tf_op jit(solution)/shard_map/ppermute | solution.py:279
  788.0 25.4 %collective-permute-done.44 = bf16[256,2048]{1,0:T(8,128)(2,1)S(1)} collective-permute-done((bf16[256,2048]{1,0:T(8,128)(2,1)S(1)}, bf16[256,2048]{1,0:T(8,128)(2,1)S(1)}, u32[]{:S(2)}, u32[]{:S(2)}) %collective-permute-start.44) | collective-permute-done | bytes 1048608 | tf_op jit(solution)/shard_map/ppermute | solution.py:279
  815.6 14.5 %collective-permute-done.45 = bf16[256,2048]{1,0:T(8,128)(2,1)S(1)} collective-permute-done((bf16[256,2048]{1,0:T(8,128)(2,1)S(1)}, bf16[256,2048]{1,0:T(8,128)(2,1)S(1)}, u32[]{:S(2)}, u32[]{:S(2)}) %collective-permute-start.45) | collective-permute-done | bytes 1048608 | tf_op jit(solution)/shard_map/ppermute | solution.py:279
  832.3 16.6 %multiply_convert_fusion.1 = (bf16[1024,1408]{1,0:T(8,128)(2,1)}, bf16[1024,1408]{1,0:T(8,128)(2,1)}) fusion(f32[1024,2816]{1,0:T(8,128)} %fusion.53, bf16[1408,2048]{1,0:T(8,128)(2,1)} %all-gather.14.cloned.1.call-done, bf16[256,2048]{1,0:T(8,128)(2,1)} %copy-done.60, bf16[256,2048]{1,0:T(8,128)(2,1)S(1)} %broadcast_select_fusion, ...), kind=kOutput, calls=%fused_computation.60 | convolution fusion | flops 5941100544 | bytes 27262976 | tf_op jit(solution)/shard_map/dot_general | solution.py:339
  892.0 18.3 %convolution_convert_fusion.2 = bf16[2048,2816]{1,0:T(8,128)(2,1)} fusion(bf16[1024,1408]{1,0:T(8,128)(2,1)} %get-tuple-element.191, bf16[1024,1408]{1,0:T(8,128)(2,1)} %get-tuple-element.192, bf16[256,2048]{1,0:T(8,128)(2,1)S(1)} %copy-done.47, bf16[256,2048]{1,0:T(8,128)(2,1)S(1)} %copy-done.48, bf16[256,2048]{1,0:T(8,128)(2,1)} %broadcast_select_fusion.5, ...), kind=kOutput, calls=%fused_computation.37 | convolution fusion | flops 11845238784 | bytes 21495808 | tf_op jit(solution)/shard_map/dot_general | solution.py:339
  918.6 20.3 %collective-permute-done.52 = bf16[256,2048]{1,0:T(8,128)(2,1)S(1)} collective-permute-done((bf16[256,2048]{1,0:T(8,128)(2,1)S(1)}, bf16[256,2048]{1,0:T(8,128)(2,1)S(1)}, u32[]{:S(2)}, u32[]{:S(2)}) %collective-permute-start.52) | collective-permute-done | bytes 1048608 | tf_op jit(solution)/shard_map/ppermute | solution.py:312
  953.6 18.8 %reduce-scatter.8.cloned.1.call-done = bf16[1408,256]{1,0:T(8,128)(2,1)} async-done(((bf16[1408,2048]{1,0:T(8,128)(2,1)}), bf16[1408,256]{1,0:T(8,128)(2,1)}) %reduce-scatter.8.cloned.1.call-update) | async-done | bytes 720912 | tf_op jit(solution)/shard_map/reduce_scatter | solution.py:491
  979.2 33.8 %attend_back.1 = (bf16[256,2048]{1,0:T(8,128)(2,1)}, bf16[1024,512]{1,0:T(8,128)(2,1)}) custom-call(bf16[256,2048]{1,0:T(8,128)(2,1)} %get-tuple-element.129.q_ref, bf16[1024,512]{1,0:T(8,128)(2,1)} %copy-done.25, f32[16,2,256]{2,1,0:T(2,128)} %get-tuple-element.130.lse_ref, bf16[256,2048]{1,0:T(8,128)(2,1)} %convolution_convert_fusion.10.grad_ref, ...), custom_call_target="tpu_custom_call" | custom-call | tf_op jit(solution)/shard_map/attend_back/pallas_call | solution.py:214
  1024.7 15.7 %collective-permute-done.55 = bf16[256,512]{1,0:T(8,128)(2,1)S(1)} collective-permute-done((bf16[256,512]{1,0:T(8,128)(2,1)S(1)}, bf16[256,512]{1,0:T(8,128)(2,1)S(1)}, u32[]{:S(2)}, u32[]{:S(2)}) %collective-permute-start.55) | collective-permute-done | bytes 262176 | tf_op jit(solution)/shard_map/ppermute | solution.py:247
  1070.7 18.6 %all_to_all.10 = bf16[8,272,256]{2,1,0:T(8,128)(2,1)S(1)} all-to-all(bf16[8,272,256]{2,1,0:T(8,128)(2,1)S(1)} %bitcast.231), channel_id=1, replica_groups=mesh['dp'=8,'mp'=4] {'dp'}, dimensions={0} | all-to-all | bytes 2228224 | tf_op jit(solution)/shard_map/all_to_all | solution.py:542
  1147.6 16.4 %fusion.10 = f32[8000,256]{1,0:T(8,128)} fusion(f32[8000,256]{1,0:T(8,128)S(1)} %fusion, s32[2048]{0:T(1024)S(1)} %bitcast.296, bf16[2048,256]{1,0:T(8,128)(2,1)} %collective-permute-done.57, bf16[2048,256]{1,0:T(8,128)(2,1)} %collective-permute-done.58, pred[]{:T(512)S(6)} %eq.119), kind=kOutput, calls=%fused_computation.40 | convolution fusion | flops 8407564288 | bytes 18489344 | tf_op jit(solution)/shard_map/dot_general | solution.py:339
  1184.9 18.0 %fusion.9 = f32[8000,256]{1,0:T(8,128)} fusion(f32[8000,256]{1,0:T(8,128)} %fusion.3, f32[8000,256]{1,0:T(8,128)} %fusion.10, s32[2048]{0:T(1024)S(1)} %bitcast.294, bf16[2048,256]{1,0:T(8,128)(2,1)} %collective-permute-done.57, bf16[2048,256]{1,0:T(8,128)(2,1)S(1)} %collective-permute-done.59, bf16[2048,256]{1,0:T(8,128)(2,1)S(1)} %collective-permute-done.60, ...), kind=kOutput, calls=%fused_computation.39 | convolution fusion | flops 8410136576 | bytes 27729922 | tf_op jit(solution)/shard_map/dot_general | solution.py:339
  1309.7 21.7 %multiply_subtract_fusion.1 = (f32[8000,256]{1,0:T(8,128)}, f32[8000,256]{1,0:T(8,128)}, f32[8000,256]{1,0:T(8,128)}) fusion(f32[8000,256]{1,0:T(8,128)} %param.34, f32[8000,256]{1,0:T(8,128)} %param.42, f32[8000,256]{1,0:T(8,128)} %param.50, f32[8000,256]{1,0:T(8,128)} %fusion.9, f32[]{:T(128)S(6)} %min.40), kind=kLoop, calls=%fused_computation.51 | loop fusion | flops 32768000 | bytes 57344004 | tf_op jit(solution)/shard_map/sub | solution.py:335
  1331.4 20.3 %multiply_subtract_fusion = (f32[256,8000]{0,1:T(8,128)}, f32[256,8000]{0,1:T(8,128)}, f32[256,8000]{0,1:T(8,128)}) fusion(f32[256,8000]{0,1:T(8,128)} %param.40, f32[]{:T(128)S(6)} %min.40, bf16[256,8000]{0,1:T(8,128)(2,1)} %reduce-scatter.6.cloned.1.call-done, f32[256,8000]{0,1:T(8,128)} %param.48, f32[256,8000]{0,1:T(8,128)} %param.56), kind=kLoop, calls=%fused_computation.50 | loop fusion | flops 34816000 | bytes 53248004 | tf_op jit(solution)/shard_map/sub | solution.py:335
  (582 shorter events, 648.7 us)
Async XLA Ops:
  7.2 202.0 %all-gather.8.cloned.1.call-start = ((), (), s32[]{:S(2)}) async-start(), calls=%async_computation.7 | async-start | bytes 11796480 | tf_op jit(solution)/shard_map/all_gather | solution.py:424
  8.3 46.4 %collective-permute-start.5 = (bf16[512,256]{1,0:T(8,128)(2,1)S(1)}, bf16[512,256]{1,0:T(8,128)(2,1)S(1)}, u32[]{:S(2)}, u32[]{:S(2)}) collective-permute-start(bf16[512,256]{1,0:T(8,128)(2,1)S(1)} %convert_element_type.268), channel_id=1, source_target_pairs={{0,3},{1,0},{2,1},{3,2},{4,7},{5,4},{6,5},{7,6},{8,11},{9,8},{10,9... | collective-permute-start | bytes 786440 | tf_op jit(solution)/shard_map/ppermute | solution.py:247
  13.4 42.8 %collective-permute-start.4 = (bf16[512,256]{1,0:T(8,128)(2,1)S(1)}, bf16[512,256]{1,0:T(8,128)(2,1)}, u32[]{:S(2)}, u32[]{:S(2)}) collective-permute-start(bf16[512,256]{1,0:T(8,128)(2,1)S(1)} %convert_element_type.268), channel_id=1, source_target_pairs={{0,2},{1,3},{2,0},{3,1},{4,6},{5,7},{6,4},{7,5},{8,10},{9,11},{10,... | collective-permute-start | bytes 786440 | tf_op jit(solution)/shard_map/ppermute | solution.py:247
  13.4 42.8 %collective-permute-start.3 = (bf16[512,256]{1,0:T(8,128)(2,1)S(1)}, bf16[512,256]{1,0:T(8,128)(2,1)}, u32[]{:S(2)}, u32[]{:S(2)}) collective-permute-start(bf16[512,256]{1,0:T(8,128)(2,1)S(1)} %convert_element_type.268), channel_id=1, source_target_pairs={{0,1},{1,2},{2,3},{3,0},{4,5},{5,6},{6,7},{7,4},{8,9},{9,10},{10,1... | collective-permute-start | bytes 786440 | tf_op jit(solution)/shard_map/ppermute | solution.py:247
  15.5 40.7 %collective-permute-start.2 = (bf16[256,512]{1,0:T(8,128)(2,1)S(1)}, bf16[256,512]{1,0:T(8,128)(2,1)}, u32[]{:S(2)}, u32[]{:S(2)}) collective-permute-start(bf16[256,512]{1,0:T(8,128)(2,1)S(1)} %convert_element_type.267), channel_id=1, source_target_pairs={{0,3},{1,0},{2,1},{3,2},{4,7},{5,4},{6,5},{7,6},{8,11},{9,8},{10,9... | collective-permute-start | bytes 786440 | tf_op jit(solution)/shard_map/ppermute | solution.py:247
  18.4 37.8 %collective-permute-start.1 = (bf16[256,512]{1,0:T(8,128)(2,1)S(1)}, bf16[256,512]{1,0:T(8,128)(2,1)}, u32[]{:S(2)}, u32[]{:S(2)}) collective-permute-start(bf16[256,512]{1,0:T(8,128)(2,1)S(1)} %convert_element_type.267), channel_id=1, source_target_pairs={{0,2},{1,3},{2,0},{3,1},{4,6},{5,7},{6,4},{7,5},{8,10},{9,11},{10,... | collective-permute-start | bytes 786440 | tf_op jit(solution)/shard_map/ppermute | solution.py:247
  68.1 203.4 %all-gather.10.cloned.1.call-start = ((), (), s32[]{:S(2)}) async-start(), calls=%async_computation.8 | async-start | bytes 9437184 | tf_op jit(solution)/shard_map/all_gather | solution.py:435
  70.6 288.4 %all-gather.12.cloned.1.call-start = ((), (), s32[]{:S(2)}) async-start(), calls=%async_computation.9 | async-start | bytes 12976128 | tf_op jit(solution)/shard_map/all_gather | solution.py:434
  94.7 290.4 %all-gather.14.cloned.1.call-start = ((), (), s32[]{:S(2)}) async-start(), calls=%async_computation.10 | async-start | bytes 6488064 | tf_op jit(solution)/shard_map/all_gather | solution.py:436
  109.5 26.2 %collective-permute-start.8 = (bf16[2048,256]{1,0:T(8,128)(2,1)S(1)}, bf16[2048,256]{1,0:T(8,128)(2,1)S(1)}, u32[]{:S(2)}, u32[]{:S(2)}) collective-permute-start(bf16[2048,256]{1,0:T(8,128)(2,1)S(1)} %get-tuple-element.215), channel_id=1, source_target_pairs={{0,1},{1,2},{4,5},{5,6},{8,9},{9,10},{12,13},{13,14},{16,17},{17,1... | collective-permute-start | bytes 3145736 | tf_op jit(solution)/shard_map/ppermute | solution.py:312
  135.7 407.2 %all-gather.16.cloned.1.call-start = ((), (), s32[]{:S(2)}) async-start(), calls=%async_computation.11 | async-start | bytes 36864000 | tf_op jit(solution)/shard_map/all_gather | solution.py:437
  190.0 720.4 %reduce-scatter.6.cloned.1.call-start = ((), (), s32[]{:S(2)}) async-start(), calls=%async_computation.12 | async-start | bytes 36864000 | tf_op jit(solution)/shard_map/reduce_scatter | solution.py:491
  304.1 26.1 %collective-permute-start.17 = (bf16[256,2048]{1,0:T(8,128)(2,1)S(1)}, bf16[256,2048]{1,0:T(8,128)(2,1)}, u32[]{:S(2)}, u32[]{:S(2)}) collective-permute-start(bf16[256,2048]{1,0:T(8,128)(2,1)S(1)} %collective-permute-done.16), channel_id=1, source_target_pairs={{1,0},{2,1},{5,4},{6,5},{9,8},{10,9},{13,12},{14,13},{17,16},{18,1... | collective-permute-start | bytes 3145736 | tf_op jit(solution)/shard_map/ppermute | solution.py:279
  305.4 26.1 %collective-permute-start.19 = (bf16[256,2048]{1,0:T(8,128)(2,1)}, bf16[256,2048]{1,0:T(8,128)(2,1)}, u32[]{:S(2)}, u32[]{:S(2)}) collective-permute-start(bf16[256,2048]{1,0:T(8,128)(2,1)} %collective-permute-done.15), channel_id=1, source_target_pairs={{1,2},{2,3},{5,6},{6,7},{9,10},{10,11},{13,14},{14,15},{17,18},{18... | collective-permute-start | bytes 3145736 | tf_op jit(solution)/shard_map/ppermute | solution.py:278
  331.5 26.4 %collective-permute-start.20 = (bf16[256,2048]{1,0:T(8,128)(2,1)}, bf16[256,2048]{1,0:T(8,128)(2,1)S(1)}, u32[]{:S(2)}, u32[]{:S(2)}) collective-permute-start(bf16[256,2048]{1,0:T(8,128)(2,1)} %collective-permute-done.19), channel_id=1, source_target_pairs={{2,3},{6,7},{10,11},{14,15},{18,19},{22,23},{26,27},{30,31}} | collective-permute-start | bytes 3145736 | tf_op jit(solution)/shard_map/ppermute | solution.py:278
  655.4 46.8 %collective-permute-start.37 = (bf16[256,2048]{1,0:T(8,128)(2,1)}, bf16[256,2048]{1,0:T(8,128)(2,1)S(1)}, u32[]{:S(2)}, u32[]{:S(2)}) collective-permute-start(bf16[256,2048]{1,0:T(8,128)(2,1)} %get-tuple-element.198), channel_id=1, source_target_pairs={{3,2},{7,6},{11,10},{15,14},{19,18},{23,22},{27,26},{31,30}} | collective-permute-start | bytes 3145736 | tf_op jit(solution)/shard_map/ppermute | solution.py:313
  656.1 46.1 %collective-permute-start.36 = (bf16[256,2048]{1,0:T(8,128)(2,1)}, bf16[256,2048]{1,0:T(8,128)(2,1)S(1)}, u32[]{:S(2)}, u32[]{:S(2)}) collective-permute-start(bf16[256,2048]{1,0:T(8,128)(2,1)} %get-tuple-element.199), channel_id=1, source_target_pairs={{0,1},{4,5},{8,9},{12,13},{16,17},{20,21},{24,25},{28,29}} | collective-permute-start | bytes 3145736 | tf_op jit(solution)/shard_map/ppermute | solution.py:312
  702.2 270.2 %reduce-scatter.8.cloned.1.call-start = ((), (), s32[]{:S(2)}) async-start(), calls=%async_computation.13 | async-start | bytes 6488064 | tf_op jit(solution)/shard_map/reduce_scatter | solution.py:491
  758.3 27.7 %collective-permute-start.43 = (bf16[256,2048]{1,0:T(8,128)(2,1)S(1)}, bf16[256,2048]{1,0:T(8,128)(2,1)S(1)}, u32[]{:S(2)}, u32[]{:S(2)}) collective-permute-start(bf16[256,2048]{1,0:T(8,128)(2,1)S(1)} %fusion.89), channel_id=1, source_target_pairs={{1,0},{2,1},{3,2},{5,4},{6,5},{7,6},{9,8},{10,9},{11,10},{13,12},{... | collective-permute-start | bytes 3145736 | tf_op jit(solution)/shard_map/ppermute | solution.py:279
  759.6 27.7 %collective-permute-start.42 = (bf16[256,2048]{1,0:T(8,128)(2,1)S(1)}, bf16[256,2048]{1,0:T(8,128)(2,1)S(1)}, u32[]{:S(2)}, u32[]{:S(2)}) collective-permute-start(bf16[256,2048]{1,0:T(8,128)(2,1)S(1)} %fusion.89), channel_id=1, source_target_pairs={{0,1},{1,2},{2,3},{4,5},{5,6},{6,7},{8,9},{9,10},{10,11},{12,13},{... | collective-permute-start | bytes 3145736 | tf_op jit(solution)/shard_map/ppermute | solution.py:278
  786.0 27.4 %collective-permute-start.44 = (bf16[256,2048]{1,0:T(8,128)(2,1)S(1)}, bf16[256,2048]{1,0:T(8,128)(2,1)S(1)}, u32[]{:S(2)}, u32[]{:S(2)}) collective-permute-start(bf16[256,2048]{1,0:T(8,128)(2,1)S(1)} %collective-permute-done.43), channel_id=1, source_target_pairs={{1,0},{2,1},{5,4},{6,5},{9,8},{10,9},{13,12},{14,13},{17,16},{18,1... | collective-permute-start | bytes 3145736 | tf_op jit(solution)/shard_map/ppermute | solution.py:279
  787.3 27.4 %collective-permute-start.46 = (bf16[256,2048]{1,0:T(8,128)(2,1)S(1)}, bf16[256,2048]{1,0:T(8,128)(2,1)S(1)}, u32[]{:S(2)}, u32[]{:S(2)}) collective-permute-start(bf16[256,2048]{1,0:T(8,128)(2,1)S(1)} %collective-permute-done.42), channel_id=1, source_target_pairs={{1,2},{2,3},{5,6},{6,7},{9,10},{10,11},{13,14},{14,15},{17,18},{18... | collective-permute-start | bytes 3145736 | tf_op jit(solution)/shard_map/ppermute | solution.py:278
  910.4 152.7 %reduce-scatter.12.cloned.1.call-start = ((), (), s32[]{:S(2)}) async-start(), calls=%async_computation.15 | async-start | bytes 12976128 | tf_op jit(solution)/shard_map/reduce_scatter | solution.py:491
  911.2 296.7 %reduce-scatter.10.cloned.1.call-start = ((), (), s32[]{:S(2)}) async-start(), calls=%async_computation.14 | async-start | bytes 9437184 | tf_op jit(solution)/shard_map/reduce_scatter | solution.py:491
  972.5 250.8 %reduce-scatter.14.cloned.1.call-start = ((), (), s32[]{:S(2)}) async-start(), calls=%async_computation.16 | async-start | bytes 11796480 | tf_op jit(solution)/shard_map/reduce_scatter | solution.py:491
  1093.8 26.7 %collective-permute-start.57 = (bf16[2048,256]{1,0:T(8,128)(2,1)S(1)}, bf16[2048,256]{1,0:T(8,128)(2,1)}, u32[]{:S(2)}, u32[]{:S(2)}) collective-permute-start(bf16[2048,256]{1,0:T(8,128)(2,1)S(1)} %bitcast.236), channel_id=1, source_target_pairs={{1,0},{2,1},{3,2},{5,4},{6,5},{7,6},{9,8},{10,9},{11,10},{13,12},{... | collective-permute-start | bytes 3145736 | tf_op jit(solution)/shard_map/ppermute | solution.py:293
  1097.1 37.2 %collective-permute-start.74 = (f32[3,256]{1,0:T(4,128)S(1)}, f32[3,256]{1,0:T(4,128)S(1)}, u32[]{:S(2)}, u32[]{:S(2)}) collective-permute-start(f32[3,256]{1,0:T(4,128)S(1)} %convert_reduce_fusion), channel_id=1, source_target_pairs={{0,1},{1,2},{2,3},{3,0},{4,5},{5,6},{6,7},{7,4},{8,9},{9,10},{10,1... | collective-permute-start | bytes 9224 | tf_op jit(solution)/shard_map/ppermute | solution.py:247
  1099.8 34.5 %collective-permute-start.73 = (f32[3,256]{1,0:T(4,128)S(1)}, f32[3,256]{1,0:T(4,128)S(1)}, u32[]{:S(2)}, u32[]{:S(2)}) collective-permute-start(f32[3,256]{1,0:T(4,128)S(1)} %convert_reduce_fusion), channel_id=1, source_target_pairs={{0,2},{1,3},{2,0},{3,1},{4,6},{5,7},{6,4},{7,5},{8,10},{9,11},{10,... | collective-permute-start | bytes 9224 | tf_op jit(solution)/shard_map/ppermute | solution.py:247
  1102.2 32.2 %collective-permute-start.72 = (f32[3,256]{1,0:T(4,128)S(1)}, f32[3,256]{1,0:T(4,128)S(1)}, u32[]{:S(2)}, u32[]{:S(2)}) collective-permute-start(f32[3,256]{1,0:T(4,128)S(1)} %convert_reduce_fusion), channel_id=1, source_target_pairs={{0,3},{1,0},{2,1},{3,2},{4,7},{5,4},{6,5},{7,6},{8,11},{9,8},{10,9... | collective-permute-start | bytes 9224 | tf_op jit(solution)/shard_map/ppermute | solution.py:247
  1135.0 29.0 %collective-permute-start.62 = (bf16[2048,256]{1,0:T(8,128)(2,1)S(1)}, bf16[2048,256]{1,0:T(8,128)(2,1)S(1)}, u32[]{:S(2)}, u32[]{:S(2)}) collective-permute-start(bf16[2048,256]{1,0:T(8,128)(2,1)S(1)} %collective-permute-done.60), channel_id=1, source_target_pairs={{2,3},{6,7},{10,11},{14,15},{18,19},{22,23},{26,27},{30,31}} | collective-permute-start | bytes 3145736 | tf_op jit(solution)/shard_map/ppermute | solution.py:292
  1211.1 27.2 %collective-permute-start.67 = (bf16[512,256]{1,0:T(8,128)(2,1)S(1)}, bf16[512,256]{1,0:T(8,128)(2,1)S(1)}, u32[]{:S(2)}, u32[]{:S(2)}) collective-permute-start(bf16[512,256]{1,0:T(8,128)(2,1)S(1)} %get-tuple-element.218), channel_id=1, source_target_pairs={{0,2},{1,3},{2,0},{3,1},{4,6},{5,7},{6,4},{7,5},{8,10},{9,11},{10,... | collective-permute-start | bytes 786440 | tf_op jit(solution)/shard_map/ppermute | solution.py:247
  1235.0 28.6 %collective-permute-start.63 = (bf16[256,512]{1,0:T(8,128)(2,1)S(1)}, bf16[256,512]{1,0:T(8,128)(2,1)S(1)}, u32[]{:S(2)}, u32[]{:S(2)}) collective-permute-start(bf16[256,512]{1,0:T(8,128)(2,1)S(1)} %get-tuple-element.219), channel_id=1, source_target_pairs={{0,3},{1,0},{2,1},{3,2},{4,7},{5,4},{6,5},{7,6},{8,11},{9,8},{10,9... | collective-permute-start | bytes 786440 | tf_op jit(solution)/shard_map/ppermute | solution.py:247
  (154 other events, 3569.6 us)
Sparse Core Ops, SparseCore 0:
  68.2 62.4 all-gather.7
  133.2 55.9 all-gather.9
  191.7 70.0 all-gather.11
  264.1 44.3 all-gather.13
  310.8 163.9 all-gather.15
  702.3 207.0 reduce-scatter.5
  913.4 58.9 reduce-scatter.7
  976.3 86.7 reduce-scatter.11
  1067.0 71.2 reduce-scatter.9
  1141.6 81.5 reduce-scatter.13

commit v4 on v3

--- a/solution.py
+++ b/solution.py
@@ -81,14 +81,18 @@
     )(kv, cosine, sine)
 
 
-def load_keys(step, per_head, kv_ref, key_ref, value_ref):
+def load_keys(step, per_head, kv_ref, key_ref, value_ref, turned_ref, turn_key):
     @pl.when(step % per_head == 0)
     def _():
         pair = kv_ref[...].astype(f32)
         other = pltpu.roll(pair, HD, 1)
         lane = lanes_of(pair.shape)
-        key_ref[...] = jnp.where(lane < HD, pair, other).astype(bf16)
-        value_ref[...] = jnp.where(lane < HD, other, pair).astype(bf16)
+        key = jnp.where(lane < HD, pair, other)
+        value = jnp.where(lane < HD, other, pair)
+        key_ref[...] = key.astype(bf16)
+        if value_ref is not None:
+            value_ref[...] = value.astype(bf16)
+        turned_ref[...] = (key if turn_key else value).T.astype(bf16)
 
 
 def both_heads(pair, low):
@@ -102,25 +106,26 @@
 
 def attend_kernel(
     per_head, q_ref, kv_ref, cos_ref, sin_ref, place_ref, key_place_ref,
-    mixed_ref, rope_ref, lse_ref, key_ref, value_ref,
+    mixed_ref, rope_ref, lse_ref, key_ref, turned_ref,
 ):
     rows = q_ref.shape[0]
     half_rows, n_keys = rows // 2, kv_ref.shape[0]
-    load_keys(pl.program_id(0), per_head, kv_ref, key_ref, value_ref)
+    load_keys(pl.program_id(0), per_head, kv_ref, key_ref, None, turned_ref, False)
     q = q_ref[...]
-    rope_ref[...] = (q * cos_ref[...] + swap_halves(q, lanes_of(q.shape)) * sin_ref[...]).astype(bf16)
+    q = (q * cos_ref[...] + swap_halves(q, lanes_of(q.shape)) * sin_ref[...]).astype(bf16)
+    rope_ref[...] = q * SCALE
     low = lanes_of((half_rows, LANES)) < HD
     for block in range(2):
         at, width = block * half_rows, (block + 1) * n_keys // 2
         chosen = both_heads(rope_ref[at : at + half_rows, :], low)
-        scores = SCALE * contract(key_ref[:width, :], chosen, (1, 1))
+        scores = contract(key_ref[:width, :], chosen, (1, 1))
         causal = key_place_ref[:width, :] <= place_ref[block : block + 1, :]
         scores = jnp.where(causal, scores, -1e30)
         peak = jnp.max(scores, 0, keepdims=True)
         expo = jnp.exp(scores - peak)
         total = jnp.sum(expo, 0, keepdims=True)
         probs = (expo * (1.0 / total)).astype(bf16)
-        out = contract(probs, value_ref[:width, :], (0, 0))
+        out = contract(turned_ref[:, :width], probs, (1, 0)).T
         mixed_ref[at : at + half_rows, :] = jnp.where(
             low, out[:half_rows], out[half_rows:]
         ).astype(bf16)
@@ -151,7 +156,7 @@
             jax.ShapeDtypeStruct((rows, cols), bf16),
             jax.ShapeDtypeStruct((pairs, 2, rows), f32),
         ],
-        scratch_shapes=[pltpu.VMEM((n_keys, LANES), bf16), pltpu.VMEM((n_keys, LANES), bf16)],
+        scratch_shapes=[pltpu.VMEM((n_keys, LANES), bf16), pltpu.VMEM((LANES, n_keys), bf16)],
         compiler_params=pltpu.CompilerParams(
             dimension_semantics=("arbitrary",), vmem_limit_bytes=VMEM_LIMIT
         ),
@@ -161,12 +166,12 @@
 
 def attend_back_kernel(
     per_head, q_ref, kv_ref, lse_ref, grad_ref, cos_ref, sin_ref, place_ref, key_place_ref,
-    dq_ref, dkv_ref, key_ref, value_ref, dk_acc, dv_acc,
+    dq_ref, dkv_ref, key_ref, value_ref, turned_ref, dk_acc, dv_acc,
 ):
     rows = q_ref.shape[0]
     half_rows, n_keys = rows // 2, kv_ref.shape[0]
     step = pl.program_id(0)
-    load_keys(step, per_head, kv_ref, key_ref, value_ref)
+    load_keys(step, per_head, kv_ref, key_ref, value_ref, turned_ref, True)
 
     @pl.when(step % per_head == 0)
     def _():
@@ -180,15 +185,15 @@
         chosen = both_heads(q_ref[at : at + half_rows, :], low)
         grad = both_heads(grad_ref[at : at + half_rows, :], low)
         keys, values = key_ref[:width, :], value_ref[:width, :]
-        scores = SCALE * contract(keys, chosen, (1, 1))
+        scores = contract(keys, chosen, (1, 1))
         causal = key_place_ref[:width, :] <= place_ref[block : block + 1, :]
         probs = jnp.where(causal, jnp.exp(scores - lse_ref[0, block : block + 1, :]), 0.0)
         prob_grad = contract(values, grad, (1, 1))
         inner = jnp.sum(probs * prob_grad, 0, keepdims=True)
         score_grad = (probs * (prob_grad - inner)).astype(bf16)
-        dk_acc[:width, :] += SCALE * contract(score_grad, chosen, (1, 0))
+        dk_acc[:width, :] += contract(score_grad, chosen, (1, 0))
         dv_acc[:width, :] += contract(probs.astype(bf16), grad, (1, 0))
-        out = SCALE * contract(score_grad, keys, (0, 0))
+        out = SCALE * contract(turned_ref[:, :width], score_grad, (1, 0)).T
         total = jnp.where(low, out[:half_rows], out[half_rows:])
         dq_ref[at : at + half_rows, :] = (
             total * cos_ref[at : at + half_rows, :]
@@ -232,6 +237,7 @@
         scratch_shapes=[
             pltpu.VMEM((n_keys, LANES), bf16),
             pltpu.VMEM((n_keys, LANES), bf16),
+            pltpu.VMEM((LANES, n_keys), bf16),
             pltpu.VMEM((n_keys, LANES), f32),
             pltpu.VMEM((n_keys, LANES), f32),
         ],
@@ -315,8 +321,6 @@
         )
         if step <= len(fillers):
             (up, down), fillers[step - 1] = tie((up, down), fillers[step - 1])
-        if step == 2:
-            (up, down), piece[0] = tie((up, down), piece[0])
     return piece[0].astype(f32) + up.astype(f32) + down.astype(f32), fillers
 
 
@@ -410,20 +414,19 @@
         found = embed_table[jnp.clip(piece_ids, 0, table_rows - 1)]
         return jnp.where(inside[:, None], found, 0.0).astype(bf16)
 
-    looked = [look_up(ids_local[i].reshape(-1)) for i in range(n_mp)]
-    ids_local = ids_local.reshape(-1)
-
-    query_pieces = ring_gather(query_weight.astype(bf16))
-    output_pieces = ring_gather(output_weight.astype(bf16))
-    looked[: n_mp // 2], (query_pieces, output_pieces) = tie(
-        looked[: n_mp // 2], (query_pieces, output_pieces)
-    )
+    looked = look_up(ids_local.reshape(-1))
+
+    (query_own, output_own), meta = tie(
+        (query_weight.astype(bf16), output_weight.astype(bf16)), meta
+    )
+    query_pieces, output_pieces = ring_gather(query_own), ring_gather(output_own)
+    looked, (query_pieces, output_pieces) = tie(looked, (query_pieces, output_pieces))
     kvq_own = jnp.concatenate(
         [pair_heads(keyvalue_weight.astype(bf16)), ordered(query_pieces, 1)], 1
     )
     kvq_full = lax.all_gather(kvq_own, "dp", axis=0, tiled=True)
     looked, (gateup_own, down_own, head_own) = line_scatter(
-        looked,
+        [looked],
         [
             gateup_weight.astype(bf16).transpose(1, 0, 2).reshape(table_cols, -1),
             down_weight.astype(bf16),
@@ -490,10 +493,8 @@
     def reduce_to(grad, axis):
         return lax.psum_scatter(grad, "dp", scatter_dimension=axis, tiled=True)
 
-    final_partial = [dot(logit_grad, head_full, ((1,), (1,)), bf16)]
-    final_grad, (head_grad,) = line_scatter(
-        final_partial, [dot(final_in, logit_grad, ((0,), (0,)), bf16)]
-    )
+    head_full, head_grad = tie(head_full, dot(final_in, logit_grad, ((0,), (0,)), bf16))
+    final_grad, _ = line_scatter([dot(logit_grad, head_full, ((1,), (1,)), bf16)])
     head_part = reduce_to(head_grad, 0)
     residual, final_gain = norm_back(final_rows, gains_rows[2], final_grad)
 
@@ -512,16 +513,39 @@
             dot(second_in, gateup_grad, ((0,), (0,)), bf16),
         ],
     )
-    (down_grad, gateup_w), head_part = tie((down_grad, gateup_w), head_part)
+    down_grad, head_part = tie(down_grad, head_part)
     down_part = reduce_to(down_grad, 1)
+    second_grad, down_part = tie(second_grad, down_part)
     gateup_part = reduce_to(gateup_w, 0)
     middle_extra, middle_gain = norm_back(middle_rows, gains_rows[1], second_grad)
     residual = residual + middle_extra
 
     branch = residual.astype(bf16)
-    branch, output_w = tie(branch, dot(mixed, branch, ((0,), (0,)), bf16))
-    output_w, down_part = tie(output_w, down_part)
-    output_w = reduce_to(output_w, 1)
+    place = lax.axis_index("dp")
+    by_owner = branch.reshape(home, n_dp // 2, 2, table_cols)
+
+    def columns_for(parity):
+        return lax.dynamic_index_in_dim(by_owner, parity, 2, False).reshape(home, -1)
+
+    given = dot(mixed, columns_for(1 - place % 2), ((0,), (0,)), bf16)
+    kept = dot(mixed, columns_for(place % 2), ((0,), (0,)), bf16)
+    branch, (given, kept) = tie(branch, (given, kept))
+    taken = lax.ppermute(given, "dp", [(k, k ^ 1) for k in range(n_dp)])
+
+    def owner_columns(hop):
+        at = ((place // 2) ^ hop) * table_cols
+        return (
+            lax.dynamic_slice_in_dim(kept, at, table_cols, 1).astype(f32)
+            + lax.dynamic_slice_in_dim(taken, at, table_cols, 1).astype(f32)
+        )
+
+    output_w = [owner_columns(0)]
+    for hop in range(1, n_dp // 2):
+        output_w.append(
+            lax.ppermute(
+                owner_columns(hop).astype(bf16), "dp", [(k, k ^ (2 * hop)) for k in range(n_dp)]
+            )
+        )
     mixed_grad = dot(branch, output_full, ((1,), (1,)), bf16)
     query_pre, kv_grad = attend_back(rope, kv, lse, mixed_grad, cosine, sine, places, key_places)
     kv_halves = kv_grad.reshape(2, n_mp, strip, kv_cols)
@@ -540,22 +564,28 @@
     moved = jnp.concatenate([start_grad, gains_grad, jnp.zeros((13, start_grad.shape[1]), bf16)])
     moved = moved.reshape(-1, n_dp, table_cols).transpose(1, 0, 2)
     moved = lax.all_to_all(moved, "dp", 0, 0)
-    kvq_w, (gateup_part, _) = tie(kvq_w, (gateup_part, moved[0, :16]))
-    gateup_part = gateup_part.reshape(table_cols, 2, -1).transpose(1, 0, 2)
+    kvq_w, gateup_part = tie(kvq_w, gateup_part)
+    kvq_w = reduce_to(kvq_w, 0)
+    gateup_part = gateup_part.reshape(table_cols, 2, half).transpose(1, 0, 2)
     gains_part = ring_scatter([jnp.sum(moved[:, home : home + 3].astype(f32), 0)] * n_mp)
     embed_part = None
     ids_home = by_piece(ids, jnp.arange(n_mp)).transpose(1, 0, 2).reshape(n_mp, -1) - vocab_start
-    for device, shard in arrivals(moved[:, :home].reshape(n_dp * home, table_cols)):
+    for number, (device, shard) in enumerate(
+        arrivals(moved[:, :home].reshape(n_dp * home, table_cols))
+    ):
         onehot = (ids_home[device][None, :] == jnp.arange(table_rows)[:, None]).astype(bf16)
         part = dot(onehot, shard)
         embed_part = part if embed_part is None else embed_part + part
-
-    kvq_w = reduce_to(kvq_w, 0)
-    output_w, embed_part = tie(output_w, embed_part)
+        if number == n_mp // 2:
+            output_w, embed_part = tie(output_w, embed_part)
+            output_w = sum(piece.astype(f32) for piece in output_w).astype(bf16)
+
     query_part = ring_scatter(
         [piece_of(kvq_w[:, kv_cols:], i, 1, q_cols) for i in range(n_mp)]
     )
-    keyvalue_part = ring_scatter([kvq_w[:, :kv_cols]] * n_mp)
+    kv_rows = table_cols // n_mp
+    keyvalue_part = ring_scatter([piece_of(kvq_w[:, :kv_cols], i, 0, kv_rows) for i in range(n_mp)])
+    keyvalue_part = ordered(ring_gather(keyvalue_part), 0)
     keyvalue_part = keyvalue_part.reshape(-1, KVH, 2, HD).transpose(0, 2, 1, 3).reshape(-1, kv_cols)
     output_part = ring_scatter(
         [piece_of(output_w, i, 0, output_weight.shape[0]) for i in range(n_mp)]

time: 1380 us -> 1360 us (0.986)
  waiting for transfers between devices: 530 us -> 457 us
  starting transfers between devices: 156 us -> 205 us
  blocking collectives: 27.9 us -> 10.7 us
  other arithmetic: 162 us -> 176 us
    ppermute x9, waiting for transfers between devices: 0.02 us -> 47.2 us  [line_gather(): lax.ppermute(ups[-1], 'mp', [(k, k + 1) for k in range(step - 1, size - 1)])]
    ppermute x9, waiting for transfers between devices: 177 us -> 131 us  [line_gather(): lax.ppermute(downs[-1], 'mp', [(k + 1, k) for k in range(size - step)])]
    reduce_scatter x5 -> x4, waiting for transfers between devices: 41.5 us -> 0.02 us  [reduce_to(): return lax.psum_scatter(grad, 'dp', scatter_dimension=axis, tiled=True)]
    ppermute x12, waiting for transfers between devices: 156 us -> 122 us  [line_scatter(): lax.ppermute(mine_up, 'mp', [(k, k + 1) for k in range(min(step, size - 1...]
    ppermute x30 -> x33, waiting for transfers between devices: 76.5 us -> 43.6 us  [ring(): return lax.ppermute(x, 'mp', [(k, (k + hop) % size) for k in range(size)])]
    ppermute x0 -> x4, waiting for transfers between devices: none -> 27.2 us  [the longest x3 27.2 us: body(): lax.ppermute(owner_columns(hop).astype(bf16), 'dp', [(k, k ^ 2 * hop) for...]
    ppermute x12, starting transfers between devices: 45.4 us -> 71 us  [line_scatter(): lax.ppermute(mine_up, 'mp', [(k, k + 1) for k in range(min(step, size - 1...]
    ppermute x12, waiting for transfers between devices: 24.4 us -> 45.8 us  [line_scatter(): lax.ppermute(mine_down, 'mp', [(k + 1, k) for k in range(max(size - 1 - s...]
  transfers between devices with their start and end apart: 92 -> 99, of which waited for: 47 -> 49; matrix products, arithmetic and copies ran while one was open for 28% -> 29% of each run, Pallas kernels for 5% -> 5%
where the time goes in v4:
time: 1360 us; the launch traced here: 1350 us
  waiting for transfers between devices  457 us (34%)
  matrix products  326 us (24%)
  starting transfers between devices  205 us (15%)
  other arithmetic  176 us (13%)
  local copies, waits for them, and re-layouts  81.8 us (6%)
  Pallas kernels  67.7 us (5%)
  between operations  24.7 us (2%)
    dot_general x23, matrix products, dot(): lax.dot_general(a, b, (dims, ((), ())), preferred_element_type=f32)  326 us
    ppermute x9, waiting for transfers between devices, line_gather(): lax.ppermute(downs[-1], 'mp', [(k + 1, k) for k in range(size - step)])  131 us
    ppermute x12, waiting for transfers between devices, line_scatter(): lax.ppermute(mine_up, 'mp', [(k, k + 1) for k in range(min(step, size - 1...  122 us
    ppermute x12, starting transfers between devices, line_scatter(): lax.ppermute(mine_up, 'mp', [(k, k + 1) for k in range(min(step, size - 1...  71 us
    sub x8, other arithmetic, adamw(): return (weight - rate * (ratio + decay * weight), mean_new, square_new)  59.5 us
    ppermute x33, starting transfers between devices, ring(): return lax.ppermute(x, 'mp', [(k, (k + hop) % size) for k in range(size)])  53.5 us
    ppermute x9, waiting for transfers between devices, line_gather(): lax.ppermute(ups[-1], 'mp', [(k, k + 1) for k in range(step - 1, size - 1)])  47.2 us
    ppermute x12, waiting for transfers between devices, line_scatter(): lax.ppermute(mine_down, 'mp', [(k + 1, k) for k in range(max(size - 1 - s...  45.8 us
  transfers between devices with their start and end apart: 99, of which 49 were waited for; matrix products, arithmetic and copies ran while one was open for 29% of the time, Pallas kernels for 5%

profile of v4, /device:TPU:0, one launch (start us, length us, event | category | flops | bytes accessed | tf_op | source)
XLA Modules:
  0.0 1348.2 jit_solution(7540146257823906088)
XLA Ops:
  32.0 34.5 %gather_fusion.2 = bf16[8192,256]{1,0:T(8,128)(2,1)} fusion(f32[8000,256]{1,0:T(8,128)} %param.34, s32[8192]{0:T(1024)S(1)} %broadcast_clamp_fusion), kind=kCustom, calls=%fused_computation.2 | custom fusion | bytes 8421376 | tf_op jit(solution)/shard_map/gather | solution.py:414
  91.7 16.7 %collective-permute-done.6 = bf16[2048,256]{1,0:T(8,128)(2,1)} collective-permute-done((bf16[2048,256]{1,0:T(8,128)(2,1)}, bf16[2048,256]{1,0:T(8,128)(2,1)}, u32[]{:S(2)}, u32[]{:S(2)}) %collective-permute-start.6) | collective-permute-done | bytes 1048608 | tf_op jit(solution)/shard_map/ppermute | solution.py:318
  119.0 15.5 %collective-permute-done.8 = bf16[2048,256]{1,0:T(8,128)(2,1)} collective-permute-done((bf16[2048,256]{1,0:T(8,128)(2,1)S(1)}, bf16[2048,256]{1,0:T(8,128)(2,1)}, u32[]{:S(2)}, u32[]{:S(2)}) %collective-permute-start.8) | collective-permute-done | bytes 1048608 | tf_op jit(solution)/shard_map/ppermute | solution.py:318
  183.8 22.9 %all-to-all-done = bf16[8,256,256]{2,1,0:T(8,128)(2,1)S(1)} async-done(((bf16[8,256,256]{2,1,0:T(8,128)(2,1)}), bf16[8,256,256]{2,1,0:T(8,128)(2,1)S(1)}, u32[]{:S(2)}, u32[]{:S(2)}) %all-to-all-start) | async-done | bytes 1048608 | tf_op jit(solution)/shard_map/all_to_all | solution.py:448
  235.3 29.4 %attend.1 = (bf16[256,2048]{1,0:T(8,128)(2,1)}, bf16[256,2048]{1,0:T(8,128)(2,1)}, f32[16,2,256]{2,1,0:T(2,128)}) custom-call(f32[256,2048]{1,0:T(8,128)} %fusion.11.q_ref, bf16[1024,512]{1,0:T(8,128)(2,1)} %copy-done.22, f32[256,128]{1,0:T(8,128)} %pad_maximum_fusion.19.cos_ref, f32[256,128]{1,0:T(8,128)} %pad_maximum_fusion.20.sin_ref, ...), custom_call_target="tpu_custom_call" | custom-call | tf_op jit(solution)/shard_map/attend/pallas_call | solution.py:142
  280.2 20.4 %collective-permute-done.15 = bf16[256,2048]{1,0:T(8,128)(2,1)S(1)} collective-permute-done((bf16[256,2048]{1,0:T(8,128)(2,1)S(1)}, bf16[256,2048]{1,0:T(8,128)(2,1)S(1)}, u32[]{:S(2)}, u32[]{:S(2)}) %collective-permute-start.15) | collective-permute-done | bytes 1048608 | tf_op jit(solution)/shard_map/ppermute | solution.py:284
  307.9 22.4 %collective-permute-done.17 = bf16[256,2048]{1,0:T(8,128)(2,1)} collective-permute-done((bf16[256,2048]{1,0:T(8,128)(2,1)}, bf16[256,2048]{1,0:T(8,128)(2,1)}, u32[]{:S(2)}, u32[]{:S(2)}) %collective-permute-start.17) | collective-permute-done | bytes 1048608 | tf_op jit(solution)/shard_map/ppermute | solution.py:285
  336.4 18.1 %collective-permute-done.18 = bf16[256,2048]{1,0:T(8,128)(2,1)S(1)} collective-permute-done((bf16[256,2048]{1,0:T(8,128)(2,1)}, bf16[256,2048]{1,0:T(8,128)(2,1)S(1)}, u32[]{:S(2)}, u32[]{:S(2)}) %collective-permute-start.18) | collective-permute-done | bytes 1048608 | tf_op jit(solution)/shard_map/ppermute | solution.py:285
  355.7 18.7 %fusion.55 = f32[1024,2816]{1,0:T(8,128)} fusion(bf16[2048,2816]{0,1:T(8,128)(2,1)} %all-gather.12.cloned.1.call-done, bf16[256,2048]{1,0:T(8,128)(2,1)S(1)} %multiply_convert_fusion.5, bf16[256,2048]{1,0:T(8,128)(2,1)} %broadcast_select_fusion.2, bf16[256,2048]{1,0:T(8,128)(2,1)} %broadcast_select_fusion.5, bf16[256,2048]{1,0:T(8,128)(2,1)} %broadcast_select_fusion.8), kind=kOutput, calls=%fused_computation.168 | convolution fusion | flops 11827937280 | bytes 27262976 | tf_op jit(solution)/shard_map/dot_general | solution.py:343
  393.8 14.5 %collective-permute-done.21 = bf16[256,2048]{1,0:T(8,128)(2,1)S(1)} collective-permute-done((bf16[256,2048]{1,0:T(8,128)(2,1)S(1)}, bf16[256,2048]{1,0:T(8,128)(2,1)S(1)}, u32[]{:S(2)}, u32[]{:S(2)}) %collective-permute-start.21) | collective-permute-done | bytes 1048608 | tf_op jit(solution)/shard_map/ppermute | solution.py:318
  413.6 17.3 %collective-permute-done.22 = bf16[256,2048]{1,0:T(8,128)(2,1)S(1)} collective-permute-done((bf16[256,2048]{1,0:T(8,128)(2,1)S(1)}, bf16[256,2048]{1,0:T(8,128)(2,1)S(1)}, u32[]{:S(2)}, u32[]{:S(2)}) %collective-permute-start.22) | collective-permute-done | bytes 1048608 | tf_op jit(solution)/shard_map/ppermute | solution.py:318
  442.4 16.7 %collective-permute-done.26 = bf16[256,2048]{1,0:T(8,128)(2,1)S(1)} collective-permute-done((bf16[256,2048]{1,0:T(8,128)(2,1)S(1)}, bf16[256,2048]{1,0:T(8,128)(2,1)S(1)}, u32[]{:S(2)}, u32[]{:S(2)}) %collective-permute-start.26) | collective-permute-done | bytes 1048608 | tf_op jit(solution)/shard_map/ppermute | solution.py:319
  468.4 15.8 %collective-permute-done.27 = bf16[256,2048]{1,0:T(8,128)(2,1)S(1)} collective-permute-done((bf16[256,2048]{1,0:T(8,128)(2,1)S(1)}, bf16[256,2048]{1,0:T(8,128)(2,1)S(1)}, u32[]{:S(2)}, u32[]{:S(2)}) %collective-permute-start.27) | collective-permute-done | bytes 1048608 | tf_op jit(solution)/shard_map/ppermute | solution.py:284
  495.6 17.8 %collective-permute-done.29 = bf16[256,2048]{1,0:T(8,128)(2,1)} collective-permute-done((bf16[256,2048]{1,0:T(8,128)(2,1)S(1)}, bf16[256,2048]{1,0:T(8,128)(2,1)}, u32[]{:S(2)}, u32[]{:S(2)}) %collective-permute-start.29) | collective-permute-done | bytes 1048608 | tf_op jit(solution)/shard_map/ppermute | solution.py:285
  517.7 15.6 %collective-permute-done.30 = bf16[256,2048]{1,0:T(8,128)(2,1)S(1)} collective-permute-done((bf16[256,2048]{1,0:T(8,128)(2,1)}, bf16[256,2048]{1,0:T(8,128)(2,1)S(1)}, u32[]{:S(2)}, u32[]{:S(2)}) %collective-permute-start.30) | collective-permute-done | bytes 1048608 | tf_op jit(solution)/shard_map/ppermute | solution.py:285
  534.4 41.6 %fusion.107 = (f32[1024]{0:T(1024)S(1)}, f32[1024,8000]{0,1:T(8,128)}) fusion(bf16[2048,8000]{0,1:T(8,128)(2,1)} %all-gather.16.cloned.1.call-done, bf16[256,2048]{1,0:T(8,128)(2,1)S(1)} %multiply_convert_fusion.4, bf16[256,2048]{1,0:T(8,128)(2,1)S(1)} %broadcast_select_fusion.1, bf16[256,2048]{1,0:T(8,128)(2,1)S(1)} %broadcast_select_fusion.4, ...), kind=kOutput, calls=%fused_computation.363 | convolution fusion | flops 33579401216 | bytes 69734400 | tf_op jit(solution)/shard_map/dot_general | solution.py:343
  576.0 14.8 %exponential_reduce_fusion = (f32[1024]{0:T(1024)S(1)}, f32[1024]{0:T(1024)S(1)}) fusion(f32[1024,8000]{0,1:T(8,128)} %get-tuple-element.256, f32[1024]{0:T(1024)S(1)} %get-tuple-element.255, s32[1024]{0:T(1024)S(1)} %bitcast.275), kind=kLoop, calls=%fused_computation.29 | loop fusion | flops 40957952 | bytes 32784384 | tf_op jit(solution)/shard_map/reduce_sum | solution.py:476
  599.9 44.6 %convolution_convert_fusion = bf16[2048,8000]{0,1:T(8,128)(2,1)} fusion(bf16[256,2048]{1,0:T(8,128)(2,1)S(1)} %multiply_convert_fusion.4, bf16[256,2048]{1,0:T(8,128)(2,1)S(1)} %broadcast_select_fusion.1, bf16[256,2048]{1,0:T(8,128)(2,1)S(1)} %broadcast_select_fusion.4, bf16[256,2048]{1,0:T(8,128)(2,1)} %broadcast_select_fusion.7, ...), kind=kOutput, calls=%fused_computation.30 | convolution fusion | flops 33636745216 | bytes 69742592 | tf_op jit(solution)/shard_map/dot_general | solution.py:343
  644.7 42.9 %convolution_convert_fusion.4 = bf16[1024,2048]{1,0:T(8,128)(2,1)S(1)} fusion(bf16[2048,8000]{0,1:T(8,128)(2,1)} %all-gather.16.cloned.1.call-done, f32[1024,8000]{0,1:T(8,128)} %get-tuple-element.256, f32[1024]{0:T(1024)S(1)} %get-tuple-element.245, f32[1024]{0:T(1024)S(1)} %get-tuple-element.168, s32[1024]{0:T(1024)S(1)} %bitcast.277), kind=kOutput, calls=%fused_computation.66 | convolution fusion | flops 33605681152 | bytes 69742592 | tf_op jit(solution)/shard_map/dot_general | solution.py:343
  690.2 17.8 %collective-permute-done.36 = bf16[256,2048]{1,0:T(8,128)(2,1)S(1)} collective-permute-done((bf16[256,2048]{1,0:T(8,128)(2,1)S(1)}, bf16[256,2048]{1,0:T(8,128)(2,1)S(1)}, u32[]{:S(2)}, u32[]{:S(2)}) %collective-permute-start.36) | collective-permute-done | bytes 1048608 | tf_op jit(solution)/shard_map/ppermute | solution.py:318
  713.6 15.8 %collective-permute-done.37 = bf16[256,2048]{1,0:T(8,128)(2,1)S(1)} collective-permute-done((bf16[256,2048]{1,0:T(8,128)(2,1)S(1)}, bf16[256,2048]{1,0:T(8,128)(2,1)S(1)}, u32[]{:S(2)}, u32[]{:S(2)}) %collective-permute-start.37) | collective-permute-done | bytes 1048608 | tf_op jit(solution)/shard_map/ppermute | solution.py:318
  743.6 15.0 %collective-permute-done.41 = bf16[256,2048]{1,0:T(8,128)(2,1)S(1)} collective-permute-done((bf16[256,2048]{1,0:T(8,128)(2,1)S(1)}, bf16[256,2048]{1,0:T(8,128)(2,1)S(1)}, u32[]{:S(2)}, u32[]{:S(2)}) %collective-permute-start.41) | collective-permute-done | bytes 1048608 | tf_op jit(solution)/shard_map/ppermute | solution.py:319
  800.0 22.2 %collective-permute-done.44 = bf16[256,2048]{1,0:T(8,128)(2,1)S(1)} collective-permute-done((bf16[256,2048]{1,0:T(8,128)(2,1)S(1)}, bf16[256,2048]{1,0:T(8,128)(2,1)S(1)}, u32[]{:S(2)}, u32[]{:S(2)}) %collective-permute-start.44) | collective-permute-done | bytes 1048608 | tf_op jit(solution)/shard_map/ppermute | solution.py:285
  839.9 16.4 %multiply_convert_fusion.1 = (bf16[1024,1408]{1,0:T(8,128)(2,1)}, bf16[1024,1408]{1,0:T(8,128)(2,1)}) fusion(f32[1024,2816]{1,0:T(8,128)} %fusion.55, bf16[1408,2048]{1,0:T(8,128)(2,1)} %all-gather.14.cloned.1.call-done, bf16[256,2048]{1,0:T(8,128)(2,1)} %copy-done.48, bf16[256,2048]{1,0:T(8,128)(2,1)S(1)} %broadcast_select_fusion, ...), kind=kOutput, calls=%fused_computation.56 | convolution fusion | flops 5941100544 | bytes 27262976 | tf_op jit(solution)/shard_map/dot_general | solution.py:343
  906.5 19.0 %convolution_convert_fusion.2 = bf16[2048,2816]{1,0:T(8,128)(2,1)} fusion(bf16[1024,1408]{1,0:T(8,128)(2,1)} %get-tuple-element.173, bf16[1024,1408]{1,0:T(8,128)(2,1)} %get-tuple-element.174, bf16[256,2048]{1,0:T(8,128)(2,1)S(1)} %copy-done.37, bf16[256,2048]{1,0:T(8,128)(2,1)S(1)} %copy-done.38, bf16[256,2048]{1,0:T(8,128)(2,1)S(1)} %copy-done.39, ...), kind=kOutput, calls=%fused_computation.34 | convolution fusion | flops 11845238784 | bytes 21495808 | tf_op jit(solution)/shard_map/dot_general | solution.py:343
  983.6 31.2 %attend_back.1 = (bf16[256,2048]{1,0:T(8,128)(2,1)}, bf16[1024,512]{1,0:T(8,128)(2,1)}) custom-call(bf16[256,2048]{1,0:T(8,128)(2,1)} %get-tuple-element.108.q_ref, bf16[1024,512]{1,0:T(8,128)(2,1)} %copy-done.22, f32[16,2,256]{2,1,0:T(2,128)} %get-tuple-element.109.lse_ref, bf16[256,2048]{1,0:T(8,128)(2,1)} %convolution_convert_fusion.11.grad_ref, ...), custom_call_target="tpu_custom_call" | custom-call | tf_op jit(solution)/shard_map/attend_back/pallas_call | solution.py:219
  1106.6 16.8 %fusion.9 = f32[8000,256]{1,0:T(8,128)} fusion(f32[8000,256]{1,0:T(8,128)} %fusion, s32[2048]{0:T(1024)S(1)} %bitcast.287, bf16[2048,256]{1,0:T(8,128)(2,1)S(1)} %collective-permute-done.61, bf16[2048,256]{1,0:T(8,128)(2,1)S(1)} %collective-permute-done.62, pred[]{:T(512)S(6)} %eq.129), kind=kOutput, calls=%fused_computation.36 | convolution fusion | flops 8407564288 | bytes 18489344 | tf_op jit(solution)/shard_map/dot_general | solution.py:343
  1141.1 16.2 %fusion.8 = f32[8000,256]{1,0:T(8,128)} fusion(f32[8000,256]{1,0:T(8,128)} %fusion.9, s32[2048]{0:T(1024)S(1)} %bitcast.286, bf16[2048,256]{1,0:T(8,128)(2,1)S(1)} %collective-permute-done.61, bf16[2048,256]{1,0:T(8,128)(2,1)S(1)} %collective-permute-done.63, bf16[2048,256]{1,0:T(8,128)(2,1)S(1)} %collective-permute-done.64, pred[]{:T(512)S(6)} %eq.134, ...), kind=kOutput, calls=%fused_computation.35 | convolution fusion | flops 8408088576 | bytes 19537922 | tf_op jit(solution)/shard_map/dot_general | solution.py:343
  1163.6 20.8 %collective-permute-done.56 = bf16[2048,256]{1,0:T(8,128)(2,1)S(1)} collective-permute-done((bf16[2048,256]{1,0:T(8,128)(2,1)S(1)}, bf16[2048,256]{1,0:T(8,128)(2,1)S(1)}, u32[]{:S(2)}, u32[]{:S(2)}) %collective-permute-start.56) | collective-permute-done | bytes 1048608 | tf_op jit(solution)/shard_map/ppermute | solution.py:545
  1193.1 17.4 %multiply_reduce_fusion = (f32[]{:T(128)}, f32[8000,256]{1,0:T(8,128)}) fusion(f32[8000,256]{1,0:T(8,128)} %fusion.8, bf16[2048,256]{1,0:T(8,128)(2,1)S(1)} %collective-permute-done.61, bf16[2048,256]{1,0:T(8,128)(2,1)S(1)} %collective-permute-done.63, bf16[2048,256]{1,0:T(8,128)(2,1)S(1)} %collective-permute-done.65, ...), kind=kOutput, calls=%fused_computation.49 | convolution fusion | flops 8412708864 | bytes 20586504 | tf_op jit(solution)/shard_map/dot_general | solution.py:343
  1285.9 20.2 %multiply_subtract_fusion = (f32[256,8000]{0,1:T(8,128)}, f32[256,8000]{0,1:T(8,128)}, f32[256,8000]{0,1:T(8,128)}) fusion(f32[256,8000]{0,1:T(8,128)} %param.40, f32[]{:T(128)S(6)} %min.19, bf16[256,8000]{0,1:T(8,128)(2,1)} %reduce-scatter.5.cloned.1.call-done, f32[256,8000]{0,1:T(8,128)} %param.48, f32[256,8000]{0,1:T(8,128)} %param.56), kind=kLoop, calls=%fused_computation.47 | loop fusion | flops 34816000 | bytes 53248004 | tf_op jit(solution)/shard_map/sub | solution.py:339
  1306.1 21.8 %multiply_subtract_fusion.1 = (f32[8000,256]{1,0:T(8,128)}, f32[8000,256]{1,0:T(8,128)}, f32[8000,256]{1,0:T(8,128)}) fusion(f32[8000,256]{1,0:T(8,128)} %param.34, f32[8000,256]{1,0:T(8,128)} %param.42, f32[8000,256]{1,0:T(8,128)} %param.50, f32[8000,256]{1,0:T(8,128)} %get-tuple-element.259, f32[]{:T(128)S(6)} %min.19), kind=kLoop, calls=%fused_computation.48 | loop fusion | flops 32768000 | bytes 57344004 | tf_op jit(solution)/shard_map/sub | solution.py:339
  (570 shorter events, 632.6 us)
Async XLA Ops:
  7.2 201.5 %all-gather.8.cloned.1.call-start = ((), (), s32[]{:S(2)}) async-start(), calls=%async_computation.6 | async-start | bytes 11796480 | tf_op jit(solution)/shard_map/all_gather | solution.py:427
  22.3 44.2 %collective-permute-start = (bf16[256,512]{1,0:T(8,128)(2,1)S(1)}, bf16[256,512]{1,0:T(8,128)(2,1)S(1)}, u32[]{:S(2)}, u32[]{:S(2)}) collective-permute-start(bf16[256,512]{1,0:T(8,128)(2,1)S(1)} %convert_element_type.304), channel_id=1, source_target_pairs={{0,1},{1,2},{2,3},{3,0},{4,5},{5,6},{6,7},{7,4},{8,9},{9,10},{10,1... | collective-permute-start | bytes 786440 | tf_op jit(solution)/shard_map/ppermute | solution.py:253
  23.9 50.9 %collective-permute-start.1 = (bf16[256,512]{1,0:T(8,128)(2,1)S(1)}, bf16[256,512]{1,0:T(8,128)(2,1)S(1)}, u32[]{:S(2)}, u32[]{:S(2)}) collective-permute-start(bf16[256,512]{1,0:T(8,128)(2,1)S(1)} %convert_element_type.304), channel_id=1, source_target_pairs={{0,2},{1,3},{2,0},{3,1},{4,6},{5,7},{6,4},{7,5},{8,10},{9,11},{10,... | collective-permute-start | bytes 786440 | tf_op jit(solution)/shard_map/ppermute | solution.py:253
  26.5 48.3 %collective-permute-start.2 = (bf16[256,512]{1,0:T(8,128)(2,1)S(1)}, bf16[256,512]{1,0:T(8,128)(2,1)}, u32[]{:S(2)}, u32[]{:S(2)}) collective-permute-start(bf16[256,512]{1,0:T(8,128)(2,1)S(1)} %convert_element_type.304), channel_id=1, source_target_pairs={{0,3},{1,0},{2,1},{3,2},{4,7},{5,4},{6,5},{7,6},{8,11},{9,8},{10,9... | collective-permute-start | bytes 786440 | tf_op jit(solution)/shard_map/ppermute | solution.py:253
  27.9 46.9 %collective-permute-start.3 = (bf16[512,256]{1,0:T(8,128)(2,1)S(1)}, bf16[512,256]{1,0:T(8,128)(2,1)S(1)}, u32[]{:S(2)}, u32[]{:S(2)}) collective-permute-start(bf16[512,256]{1,0:T(8,128)(2,1)S(1)} %convert_element_type.305), channel_id=1, source_target_pairs={{0,1},{1,2},{2,3},{3,0},{4,5},{5,6},{6,7},{7,4},{8,9},{9,10},{10,1... | collective-permute-start | bytes 786440 | tf_op jit(solution)/shard_map/ppermute | solution.py:253
  28.5 46.3 %collective-permute-start.4 = (bf16[512,256]{1,0:T(8,128)(2,1)S(1)}, bf16[512,256]{1,0:T(8,128)(2,1)S(1)}, u32[]{:S(2)}, u32[]{:S(2)}) collective-permute-start(bf16[512,256]{1,0:T(8,128)(2,1)S(1)} %convert_element_type.305), channel_id=1, source_target_pairs={{0,2},{1,3},{2,0},{3,1},{4,6},{5,7},{6,4},{7,5},{8,10},{9,11},{10,... | collective-permute-start | bytes 786440 | tf_op jit(solution)/shard_map/ppermute | solution.py:253
  78.4 186.4 %all-gather.10.cloned.1.call-start = ((), (), s32[]{:S(2)}) async-start(), calls=%async_computation.7 | async-start | bytes 9437184 | tf_op jit(solution)/shard_map/all_gather | solution.py:438
  80.7 275.0 %all-gather.12.cloned.1.call-start = ((), (), s32[]{:S(2)}) async-start(), calls=%async_computation.8 | async-start | bytes 12976128 | tf_op jit(solution)/shard_map/all_gather | solution.py:437
  108.4 272.3 %all-gather.14.cloned.1.call-start = ((), (), s32[]{:S(2)}) async-start(), calls=%async_computation.9 | async-start | bytes 6488064 | tf_op jit(solution)/shard_map/all_gather | solution.py:439
  134.6 399.8 %all-gather.16.cloned.1.call-start = ((), (), s32[]{:S(2)}) async-start(), calls=%async_computation.10 | async-start | bytes 36864000 | tf_op jit(solution)/shard_map/all_gather | solution.py:440
  138.0 28.8 %collective-permute-start.10 = (bf16[2048,256]{1,0:T(8,128)(2,1)}, bf16[2048,256]{1,0:T(8,128)(2,1)S(1)}, u32[]{:S(2)}, u32[]{:S(2)}) collective-permute-start(bf16[2048,256]{1,0:T(8,128)(2,1)} %get-tuple-element.186), channel_id=1, source_target_pairs={{0,1},{1,2},{2,3},{4,5},{5,6},{6,7},{8,9},{9,10},{10,11},{12,13},{... | collective-permute-start | bytes 3145736 | tf_op jit(solution)/shard_map/ppermute | solution.py:318
  176.2 30.4 %all-to-all-start = ((bf16[8,256,256]{2,1,0:T(8,128)(2,1)}), bf16[8,256,256]{2,1,0:T(8,128)(2,1)S(1)}, u32[]{:S(2)}, u32[]{:S(2)}) async-start(bf16[8,256,256]{2,1,0:T(8,128)(2,1)} %bitcast.8), calls=%async_computation | async-start | bytes 2097152 | tf_op jit(solution)/shard_map/all_to_all | solution.py:448
  179.8 704.5 %reduce-scatter.5.cloned.1.call-start = ((), (), s32[]{:S(2)}) async-start(), calls=%async_computation.11 | async-start | bytes 36864000 | tf_op jit(solution)/shard_map/reduce_scatter | solution.py:494
  272.0 28.6 %collective-permute-start.15 = (bf16[256,2048]{1,0:T(8,128)(2,1)S(1)}, bf16[256,2048]{1,0:T(8,128)(2,1)S(1)}, u32[]{:S(2)}, u32[]{:S(2)}) collective-permute-start(bf16[256,2048]{1,0:T(8,128)(2,1)S(1)} %multiply_convert_fusion.5), channel_id=1, source_target_pairs={{0,1},{1,2},{2,3},{4,5},{5,6},{6,7},{8,9},{9,10},{10,11},{12,13},{... | collective-permute-start | bytes 3145736 | tf_op jit(solution)/shard_map/ppermute | solution.py:284
  278.9 26.0 %collective-permute-start.16 = (bf16[256,2048]{1,0:T(8,128)(2,1)S(1)}, bf16[256,2048]{1,0:T(8,128)(2,1)}, u32[]{:S(2)}, u32[]{:S(2)}) collective-permute-start(bf16[256,2048]{1,0:T(8,128)(2,1)S(1)} %multiply_convert_fusion.5), channel_id=1, source_target_pairs={{1,0},{2,1},{3,2},{5,4},{6,5},{7,6},{9,8},{10,9},{11,10},{13,12},{... | collective-permute-start | bytes 3145736 | tf_op jit(solution)/shard_map/ppermute | solution.py:285
  306.2 27.9 %collective-permute-start.20 = (bf16[256,2048]{1,0:T(8,128)(2,1)}, bf16[256,2048]{1,0:T(8,128)(2,1)}, u32[]{:S(2)}, u32[]{:S(2)}) collective-permute-start(bf16[256,2048]{1,0:T(8,128)(2,1)} %collective-permute-done.19), channel_id=1, source_target_pairs={{2,3},{6,7},{10,11},{14,15},{18,19},{22,23},{26,27},{30,31}} | collective-permute-start | bytes 3145736 | tf_op jit(solution)/shard_map/ppermute | solution.py:284
  431.2 28.0 %collective-permute-start.26 = (bf16[256,2048]{1,0:T(8,128)(2,1)S(1)}, bf16[256,2048]{1,0:T(8,128)(2,1)S(1)}, u32[]{:S(2)}, u32[]{:S(2)}) collective-permute-start(bf16[256,2048]{1,0:T(8,128)(2,1)S(1)} %get-tuple-element.198), channel_id=1, source_target_pairs={{1,0},{2,1},{3,2},{5,4},{6,5},{7,6},{9,8},{10,9},{11,10},{13,12},{... | collective-permute-start | bytes 3145736 | tf_op jit(solution)/shard_map/ppermute | solution.py:319
  432.5 27.8 %collective-permute-start.23 = (bf16[256,2048]{1,0:T(8,128)(2,1)S(1)}, bf16[256,2048]{1,0:T(8,128)(2,1)S(1)}, u32[]{:S(2)}, u32[]{:S(2)}) collective-permute-start(bf16[256,2048]{1,0:T(8,128)(2,1)S(1)} %get-tuple-element.197), channel_id=1, source_target_pairs={{0,1},{1,2},{2,3},{4,5},{5,6},{6,7},{8,9},{9,10},{10,11},{12,13},{... | collective-permute-start | bytes 3145736 | tf_op jit(solution)/shard_map/ppermute | solution.py:318
  644.5 310.1 %reduce-scatter.7.cloned.1.call-start = ((), (), s32[]{:S(2)}) async-start(), calls=%async_computation.12 | async-start | bytes 6488064 | tf_op jit(solution)/shard_map/reduce_scatter | solution.py:494
  729.6 29.0 %collective-permute-start.41 = (bf16[256,2048]{1,0:T(8,128)(2,1)S(1)}, bf16[256,2048]{1,0:T(8,128)(2,1)S(1)}, u32[]{:S(2)}, u32[]{:S(2)}) collective-permute-start(bf16[256,2048]{1,0:T(8,128)(2,1)S(1)} %get-tuple-element.180), channel_id=1, source_target_pairs={{1,0},{2,1},{3,2},{5,4},{6,5},{7,6},{9,8},{10,9},{11,10},{13,12},{... | collective-permute-start | bytes 3145736 | tf_op jit(solution)/shard_map/ppermute | solution.py:319
  731.0 34.7 %collective-permute-start.38 = (bf16[256,2048]{1,0:T(8,128)(2,1)S(1)}, bf16[256,2048]{1,0:T(8,128)(2,1)S(1)}, u32[]{:S(2)}, u32[]{:S(2)}) collective-permute-start(bf16[256,2048]{1,0:T(8,128)(2,1)S(1)} %get-tuple-element.179), channel_id=1, source_target_pairs={{0,1},{1,2},{2,3},{4,5},{5,6},{6,7},{8,9},{9,10},{10,11},{12,13},{... | collective-permute-start | bytes 3145736 | tf_op jit(solution)/shard_map/ppermute | solution.py:318
  884.3 158.4 %reduce-scatter.9.cloned.1.call-start = ((), (), s32[]{:S(2)}) async-start(), calls=%async_computation.13 | async-start | bytes 12976128 | tf_op jit(solution)/shard_map/reduce_scatter | solution.py:494
  899.1 26.4 %collective-permute-start.50 = (bf16[256,2048]{1,0:T(8,128)(2,1)}, bf16[256,2048]{1,0:T(8,128)(2,1)}, u32[]{:S(2)}, u32[]{:S(2)}) collective-permute-start(bf16[256,2048]{1,0:T(8,128)(2,1)} %get-tuple-element.194), channel_id=1, source_target_pairs={{0,1},{1,2},{4,5},{5,6},{8,9},{9,10},{12,13},{13,14},{16,17},{17,1... | collective-permute-start | bytes 3145736 | tf_op jit(solution)/shard_map/ppermute | solution.py:318
  925.5 285.0 %reduce-scatter.11.cloned.1.call-start = ((), (), s32[]{:S(2)}) async-start(), calls=%async_computation.14 | async-start | bytes 11796480 | tf_op jit(solution)/shard_map/reduce_scatter | solution.py:494
  1065.8 64.0 %collective-permute-start.54 = (bf16[2048,1024]{1,0:T(8,128)(2,1)}, bf16[2048,1024]{1,0:T(8,128)(2,1)}, u32[]{:S(2)}, u32[]{:S(2)}) collective-permute-start(bf16[2048,1024]{1,0:T(8,128)(2,1)} %convolution_convert_fusion.6), channel_id=1, source_target_pairs={{0,4},{4,0},{8,12},{12,8},{16,20},{20,16},{24,28},{28,24},{1,5},{5... | collective-permute-start | bytes 12582920 | tf_op jit(solution)/shard_map/ppermute | solution.py:533
  1127.8 65.3 %collective-permute-start.65 = (bf16[2048,256]{1,0:T(8,128)(2,1)S(1)}, bf16[2048,256]{1,0:T(8,128)(2,1)S(1)}, u32[]{:S(2)}, u32[]{:S(2)}) collective-permute-start(bf16[2048,256]{1,0:T(8,128)(2,1)S(1)} %collective-permute-done.63), channel_id=1, source_target_pairs={{1,0},{5,4},{9,8},{13,12},{17,16},{21,20},{25,24},{29,28}} | collective-permute-start | bytes 3145736 | tf_op jit(solution)/shard_map/ppermute | solution.py:299
  1129.1 64.0 %collective-permute-start.66 = (bf16[2048,256]{1,0:T(8,128)(2,1)S(1)}, bf16[2048,256]{1,0:T(8,128)(2,1)S(1)}, u32[]{:S(2)}, u32[]{:S(2)}) collective-permute-start(bf16[2048,256]{1,0:T(8,128)(2,1)S(1)} %collective-permute-done.64), channel_id=1, source_target_pairs={{2,3},{6,7},{10,11},{14,15},{18,19},{22,23},{26,27},{30,31}} | collective-permute-start | bytes 3145736 | tf_op jit(solution)/shard_map/ppermute | solution.py:298
  1133.7 30.0 %collective-permute-start.55 = (bf16[2048,256]{1,0:T(8,128)(2,1)S(1)}, bf16[2048,256]{1,0:T(8,128)(2,1)S(1)}, u32[]{:S(2)}, u32[]{:S(2)}) collective-permute-start(bf16[2048,256]{1,0:T(8,128)(2,1)S(1)} %get-tuple-element.177), channel_id=1, source_target_pairs={{0,8},{4,12},{8,0},{12,4},{16,24},{20,28},{24,16},{28,20},{1,9},{5... | collective-permute-start | bytes 3145736 | tf_op jit(solution)/shard_map/ppermute | solution.py:545
  1139.5 44.9 %collective-permute-start.56 = (bf16[2048,256]{1,0:T(8,128)(2,1)S(1)}, bf16[2048,256]{1,0:T(8,128)(2,1)S(1)}, u32[]{:S(2)}, u32[]{:S(2)}) collective-permute-start(bf16[2048,256]{1,0:T(8,128)(2,1)S(1)} %get-tuple-element.176), channel_id=1, source_target_pairs={{0,16},{4,20},{8,24},{12,28},{16,0},{20,4},{24,8},{28,12},{1,17},{... | collective-permute-start | bytes 3145736 | tf_op jit(solution)/shard_map/ppermute | solution.py:545
  1139.7 44.7 %collective-permute-start.57 = (bf16[2048,256]{1,0:T(8,128)(2,1)S(1)}, bf16[2048,256]{1,0:T(8,128)(2,1)S(1)}, u32[]{:S(2)}, u32[]{:S(2)}) collective-permute-start(bf16[2048,256]{1,0:T(8,128)(2,1)S(1)} %get-tuple-element.175), channel_id=1, source_target_pairs={{0,24},{4,28},{8,16},{12,20},{16,8},{20,12},{24,0},{28,4},{1,25},{... | collective-permute-start | bytes 3145736 | tf_op jit(solution)/shard_map/ppermute | solution.py:545
  1185.0 27.1 %collective-permute-start.72 = (bf16[512,256]{1,0:T(8,128)(2,1)S(1)}, bf16[512,256]{1,0:T(8,128)(2,1)S(1)}, u32[]{:S(2)}, u32[]{:S(2)}) collective-permute-start(bf16[512,256]{1,0:T(8,128)(2,1)S(1)} %get-tuple-element.204), channel_id=1, source_target_pairs={{0,1},{1,2},{2,3},{3,0},{4,5},{5,6},{6,7},{7,4},{8,9},{9,10},{10,1... | collective-permute-start | bytes 786440 | tf_op jit(solution)/shard_map/ppermute | solution.py:253
  1187.5 27.9 %collective-permute-start.71 = (bf16[512,256]{1,0:T(8,128)(2,1)S(1)}, bf16[512,256]{1,0:T(8,128)(2,1)S(1)}, u32[]{:S(2)}, u32[]{:S(2)}) collective-permute-start(bf16[512,256]{1,0:T(8,128)(2,1)S(1)} %get-tuple-element.205), channel_id=1, source_target_pairs={{0,2},{1,3},{2,0},{3,1},{4,6},{5,7},{6,4},{7,5},{8,10},{9,11},{10,... | collective-permute-start | bytes 786440 | tf_op jit(solution)/shard_map/ppermute | solution.py:253
  (147 other events, 3231.5 us)
Sparse Core Ops, SparseCore 0:
  78.5 65.1 all-gather.7
  146.2 67.1 all-gather.9
  215.8 69.8 all-gather.11
  288.1 44.3 all-gather.13
  334.8 163.9 all-gather.15
  644.6 200.8 reduce-scatter.4
  884.5 59.4 reduce-scatter.6
  947.8 86.7 reduce-scatter.8
  1042.9 85.6 reduce-scatter.10

commit v5 on v4

--- a/solution.py
+++ b/solution.py
@@ -276,17 +276,33 @@
     return order + [0]
 
 
-def line_gather(shard):
-    size = lax.axis_size("mp")
-    me = lax.axis_index("mp")
-    ups, downs = [shard], [shard]
-    for step in range(1, size):
-        ups.append(lax.ppermute(ups[-1], "mp", [(k, k + 1) for k in range(step - 1, size - 1)]))
-        downs.append(lax.ppermute(downs[-1], "mp", [(k + 1, k) for k in range(size - step)]))
-    pieces = [shard] + [
+def relay(ups, downs):
+    size, step = lax.axis_size("mp"), len(ups)
+    ups.append(lax.ppermute(ups[-1], "mp", [(k, k + 1) for k in range(step - 1, size - 1)]))
+    downs.append(lax.ppermute(downs[-1], "mp", [(k + 1, k) for k in range(size - step)]))
+
+
+def relay_tied(value, ups, downs, last=False):
+    relay(ups, downs)
+    while last and len(ups) < lax.axis_size("mp"):
+        relay(ups, downs)
+    value, (ups[-1], downs[-1]) = tie(value, (ups[-1], downs[-1]))
+    return value
+
+
+def line_pieces(ups, downs):
+    size, me = len(ups), lax.axis_index("mp")
+    pieces = [ups[0]] + [
         jnp.where(me >= hop, ups[hop], downs[size - hop]) for hop in range(1, size)
     ]
     return jnp.concatenate([pieces[i] for i in piece_order()])
+
+
+def line_gather(shard):
+    ups, downs = [shard], [shard]
+    while len(ups) < lax.axis_size("mp"):
+        relay(ups, downs)
+    return line_pieces(ups, downs)
 
 
 def arrivals(shard):
@@ -454,6 +470,8 @@
     kv_pieces = ring_gather(kv_own)
     kv = jnp.concatenate([p[:strip] for p in kv_pieces] + [p[strip:] for p in kv_pieces])
     mixed, rope, lse = attend(queries, kv, cosine, sine, places, key_places)
+    ups, downs = [first_in], [first_in]
+    mixed = relay_tied(mixed, ups, downs)
     middle_rows = start_rows + dot(mixed, output_full)
 
     second_in = line_gather(normed(middle_rows, gains_rows[1]).astype(bf16))
@@ -493,8 +511,13 @@
     def reduce_to(grad, axis):
         return lax.psum_scatter(grad, "dp", scatter_dimension=axis, tiled=True)
 
-    head_full, head_grad = tie(head_full, dot(final_in, logit_grad, ((0,), (0,)), bf16))
-    final_grad, _ = line_scatter([dot(logit_grad, head_full, ((1,), (1,)), bf16)])
+    head_grad = relay_tied(dot(final_in, logit_grad, ((0,), (0,)), bf16), ups, downs)
+    head_full, head_grad = tie(head_full, head_grad)
+    final_partial = relay_tied(
+        dot(logit_grad, head_full, ((1,), (1,)), bf16), ups, downs, last=True
+    )
+    first_all = line_pieces(ups, downs)
+    final_grad, _ = line_scatter([final_partial])
     head_part = reduce_to(head_grad, 0)
     residual, final_gain = norm_back(final_rows, gains_rows[2], final_grad)
 
@@ -552,7 +575,23 @@
     kv_grad = ring_scatter([jnp.concatenate([kv_halves[0, i], kv_halves[1, i]]) for i in range(n_mp)])
     pair_grad = turn_keys(kv_grad, cosine, sine, -1.0, KVH)
     kvq_grad = jnp.concatenate([pair_grad, query_pre], 1)
-    kvq_grad, kvq_w = tie(kvq_grad, dot(first_in, kvq_grad, ((0,), (0,)), bf16))
+    kv_own = kv_cols // n_mp
+
+    def piece_columns(hop):
+        there = (group - hop) % n_mp
+        return jnp.concatenate(
+            [
+                lax.dynamic_slice_in_dim(kvq_grad, there * kv_own, kv_own, 1),
+                lax.dynamic_slice_in_dim(kvq_grad, kv_cols + there * q_cols, q_cols, 1),
+            ],
+            1,
+        )
+
+    columns = {0: piece_columns(0)}
+    for hop in range(1, n_mp):
+        columns[n_mp - hop] = ring(piece_columns(hop), -hop)
+    columns = jnp.concatenate([columns[i] for i in piece_order()])
+    kvq_w = dot(first_all, columns, ((0,), (0,)), bf16)
     first_grad = dot(kvq_grad, kvq_full, ((1,), (1,)))
     start_extra, start_gain = norm_back(start_rows, gains_rows[0], first_grad)
     start_grad = (residual + start_extra).astype(bf16)
@@ -564,6 +603,7 @@
     moved = jnp.concatenate([start_grad, gains_grad, jnp.zeros((13, start_grad.shape[1]), bf16)])
     moved = moved.reshape(-1, n_dp, table_cols).transpose(1, 0, 2)
     moved = lax.all_to_all(moved, "dp", 0, 0)
+    moved, kvq_w = tie(moved, kvq_w)
     kvq_w, gateup_part = tie(kvq_w, gateup_part)
     kvq_w = reduce_to(kvq_w, 0)
     gateup_part = gateup_part.reshape(table_cols, 2, half).transpose(1, 0, 2)
@@ -580,12 +620,8 @@
             output_w, embed_part = tie(output_w, embed_part)
             output_w = sum(piece.astype(f32) for piece in output_w).astype(bf16)
 
-    query_part = ring_scatter(
-        [piece_of(kvq_w[:, kv_cols:], i, 1, q_cols) for i in range(n_mp)]
-    )
-    kv_rows = table_cols // n_mp
-    keyvalue_part = ring_scatter([piece_of(kvq_w[:, :kv_cols], i, 0, kv_rows) for i in range(n_mp)])
-    keyvalue_part = ordered(ring_gather(keyvalue_part), 0)
+    query_part = kvq_w[:, kv_own:]
+    keyvalue_part = ordered(ring_gather(kvq_w[:, :kv_own]), 1)
     keyvalue_part = keyvalue_part.reshape(-1, KVH, 2, HD).transpose(0, 2, 1, 3).reshape(-1, kv_cols)
     output_part = ring_scatter(
         [piece_of(output_w, i, 0, output_weight.shape[0]) for i in range(n_mp)]

time: 1360 us -> 1350 us (level)
    ppermute x33 -> x30, waiting for transfers between devices: 43.6 us -> 63.1 us  [ring(): return lax.ppermute(x, 'mp', [(k, (k + hop) % size) for k in range(size)])]
    ppermute x18 -> x24, waiting for transfers between devices: 178 us -> 166 us  [the longest x12 126 us: relay(): lax.ppermute(downs[-1], 'mp', [(k + 1, k) for k in range(size - step)])]
    ppermute x18 -> x24, starting transfers between devices: 35.7 us -> 41.9 us  [the longest x12 25.3 us: relay(): lax.ppermute(ups[-1], 'mp', [(k, k + 1) for k in range(step - 1, size - 1)])]
    ppermute x33 -> x30, starting transfers between devices: 53.5 us -> 55.1 us  [ring(): return lax.ppermute(x, 'mp', [(k, (k + hop) % size) for k in range(size)])]
  transfers between devices with their start and end apart: 99 -> 102, of which waited for: 49 -> 44; matrix products, arithmetic and copies ran while one was open for 29% -> 32% of each run, Pallas kernels for 5% -> 5%
where the time goes in v5:
time: 1350 us; the launch traced here: 1340 us
  waiting for transfers between devices  447 us (33%)
  matrix products  321 us (24%)
  starting transfers between devices  213 us (16%)
  other arithmetic  175 us (13%)
  local copies, waits for them, and re-layouts  77.5 us (6%)
  Pallas kernels  68.3 us (5%)
  between operations  25 us (2%)
    dot_general x23, matrix products, dot(): lax.dot_general(a, b, (dims, ((), ())), preferred_element_type=f32)  321 us
    ppermute x12, waiting for transfers between devices, line_scatter(): lax.ppermute(mine_up, 'mp', [(k, k + 1) for k in range(min(step, size - 1...  132 us
    ppermute x12, waiting for transfers between devices, relay(): lax.ppermute(downs[-1], 'mp', [(k + 1, k) for k in range(size - step)])  126 us
    ppermute x12, starting transfers between devices, line_scatter(): lax.ppermute(mine_up, 'mp', [(k, k + 1) for k in range(min(step, size - 1...  68.5 us
    ppermute x30, waiting for transfers between devices, ring(): return lax.ppermute(x, 'mp', [(k, (k + hop) % size) for k in range(size)])  63.1 us
    sub x8, other arithmetic, adamw(): return (weight - rate * (ratio + decay * weight), mean_new, square_new)  60.8 us
    ppermute x30, starting transfers between devices, ring(): return lax.ppermute(x, 'mp', [(k, (k + hop) % size) for k in range(size)])  55.1 us
    ppermute x12, waiting for transfers between devices, line_scatter(): lax.ppermute(mine_down, 'mp', [(k + 1, k) for k in range(max(size - 1 - s...  39.7 us
  transfers between devices with their start and end apart: 102, of which 44 were waited for; matrix products, arithmetic and copies ran while one was open for 32% of the time, Pallas kernels for 5%

profile of v5, /device:TPU:0, one launch (start us, length us, event | category | flops | bytes accessed | tf_op | source)
XLA Modules:
  0.0 1336.6 jit_solution(17723764280846059940)
XLA Ops:
  32.0 34.5 %gather_fusion.2 = bf16[8192,256]{1,0:T(8,128)(2,1)} fusion(f32[8000,256]{1,0:T(8,128)} %param.34, s32[8192]{0:T(1024)S(1)} %broadcast_clamp_fusion), kind=kCustom, calls=%fused_computation.2 | custom fusion | bytes 8421376 | tf_op jit(solution)/shard_map/gather | solution.py:430
  91.7 16.7 %collective-permute-done.6 = bf16[2048,256]{1,0:T(8,128)(2,1)} collective-permute-done((bf16[2048,256]{1,0:T(8,128)(2,1)}, bf16[2048,256]{1,0:T(8,128)(2,1)}, u32[]{:S(2)}, u32[]{:S(2)}) %collective-permute-start.6) | collective-permute-done | bytes 1048608 | tf_op jit(solution)/shard_map/ppermute | solution.py:334
  119.0 15.5 %collective-permute-done.8 = bf16[2048,256]{1,0:T(8,128)(2,1)} collective-permute-done((bf16[2048,256]{1,0:T(8,128)(2,1)S(1)}, bf16[2048,256]{1,0:T(8,128)(2,1)}, u32[]{:S(2)}, u32[]{:S(2)}) %collective-permute-start.8) | collective-permute-done | bytes 1048608 | tf_op jit(solution)/shard_map/ppermute | solution.py:334
  184.2 22.9 %all-to-all-done = bf16[8,256,256]{2,1,0:T(8,128)(2,1)S(1)} async-done(((bf16[8,256,256]{2,1,0:T(8,128)(2,1)}), bf16[8,256,256]{2,1,0:T(8,128)(2,1)S(1)}, u32[]{:S(2)}, u32[]{:S(2)}) %all-to-all-start) | async-done | bytes 1048608 | tf_op jit(solution)/shard_map/all_to_all | solution.py:464
  255.2 29.4 %attend.1 = (bf16[256,2048]{1,0:T(8,128)(2,1)}, bf16[256,2048]{1,0:T(8,128)(2,1)}, f32[16,2,256]{2,1,0:T(2,128)}) custom-call(f32[256,2048]{1,0:T(8,128)} %fusion.11.q_ref, bf16[1024,512]{1,0:T(8,128)(2,1)} %copy-done.20, f32[256,128]{1,0:T(8,128)} %pad_maximum_fusion.24.cos_ref, f32[256,128]{1,0:T(8,128)} %pad_maximum_fusion.25.sin_ref, ...), custom_call_target="tpu_custom_call" | custom-call | tf_op jit(solution)/shard_map/attend/pallas_call | solution.py:142
  299.2 17.2 %collective-permute-done.17 = bf16[256,2048]{1,0:T(8,128)(2,1)S(1)} collective-permute-done((bf16[256,2048]{1,0:T(8,128)(2,1)S(1)}, bf16[256,2048]{1,0:T(8,128)(2,1)S(1)}, u32[]{:S(2)}, u32[]{:S(2)}) %collective-permute-start.17) | collective-permute-done | bytes 1048608 | tf_op jit(solution)/shard_map/ppermute | solution.py:281
  324.0 20.4 %collective-permute-done.19 = bf16[256,2048]{1,0:T(8,128)(2,1)} collective-permute-done((bf16[256,2048]{1,0:T(8,128)(2,1)}, bf16[256,2048]{1,0:T(8,128)(2,1)}, u32[]{:S(2)}, u32[]{:S(2)}) %collective-permute-start.19) | collective-permute-done | bytes 1048608 | tf_op jit(solution)/shard_map/ppermute | solution.py:282
  350.9 14.6 %collective-permute-done.20 = bf16[256,2048]{1,0:T(8,128)(2,1)S(1)} collective-permute-done((bf16[256,2048]{1,0:T(8,128)(2,1)}, bf16[256,2048]{1,0:T(8,128)(2,1)S(1)}, u32[]{:S(2)}, u32[]{:S(2)}) %collective-permute-start.20) | collective-permute-done | bytes 1048608 | tf_op jit(solution)/shard_map/ppermute | solution.py:282
  366.7 18.5 %fusion.77 = f32[1024,2816]{1,0:T(8,128)} fusion(bf16[2048,2816]{0,1:T(8,128)(2,1)} %all-gather.12.cloned.1.call-done, bf16[256,2048]{1,0:T(8,128)(2,1)S(1)} %multiply_convert_fusion.5, bf16[256,2048]{1,0:T(8,128)(2,1)} %broadcast_select_fusion.3, bf16[256,2048]{1,0:T(8,128)(2,1)} %broadcast_select_fusion.7, bf16[256,2048]{1,0:T(8,128)(2,1)} %broadcast_select_fusion.11), kind=kOutput, calls=%fused_computation.204 | convolution fusion | flops 11827937280 | bytes 27262976 | tf_op jit(solution)/shard_map/dot_general | solution.py:359
  404.6 14.2 %collective-permute-done.23 = bf16[256,2048]{1,0:T(8,128)(2,1)S(1)} collective-permute-done((bf16[256,2048]{1,0:T(8,128)(2,1)S(1)}, bf16[256,2048]{1,0:T(8,128)(2,1)S(1)}, u32[]{:S(2)}, u32[]{:S(2)}) %collective-permute-start.23) | collective-permute-done | bytes 1048608 | tf_op jit(solution)/shard_map/ppermute | solution.py:334
  424.2 15.9 %collective-permute-done.24 = bf16[256,2048]{1,0:T(8,128)(2,1)S(1)} collective-permute-done((bf16[256,2048]{1,0:T(8,128)(2,1)S(1)}, bf16[256,2048]{1,0:T(8,128)(2,1)S(1)}, u32[]{:S(2)}, u32[]{:S(2)}) %collective-permute-start.24) | collective-permute-done | bytes 1048608 | tf_op jit(solution)/shard_map/ppermute | solution.py:334
  501.0 19.6 %collective-permute-done.31 = bf16[256,2048]{1,0:T(8,128)(2,1)} collective-permute-done((bf16[256,2048]{1,0:T(8,128)(2,1)S(1)}, bf16[256,2048]{1,0:T(8,128)(2,1)}, u32[]{:S(2)}, u32[]{:S(2)}) %collective-permute-start.31) | collective-permute-done | bytes 1048608 | tf_op jit(solution)/shard_map/ppermute | solution.py:282
  525.2 12.3 collective-permute-done.32
  538.6 41.6 %fusion.145 = (f32[1024]{0:T(1024)S(1)}, f32[1024,8000]{0,1:T(8,128)}) fusion(bf16[2048,8000]{0,1:T(8,128)(2,1)} %all-gather.16.cloned.1.call-done, bf16[256,2048]{1,0:T(8,128)(2,1)S(1)} %multiply_convert_fusion.4, bf16[256,2048]{1,0:T(8,128)(2,1)S(1)} %broadcast_select_fusion.2, bf16[256,2048]{1,0:T(8,128)(2,1)S(1)} %broadcast_select_fusion.6, ...), kind=kOutput, calls=%fused_computation.409 | convolution fusion | flops 33579401216 | bytes 69734400 | tf_op jit(solution)/shard_map/dot_general | solution.py:359
  580.2 15.0 %exponential_reduce_fusion = (f32[1024]{0:T(1024)S(1)}, f32[1024]{0:T(1024)S(1)}) fusion(f32[1024,8000]{0,1:T(8,128)} %get-tuple-element.276, f32[1024]{0:T(1024)S(1)} %get-tuple-element.275, s32[1024]{0:T(1024)S(1)} %bitcast.285), kind=kLoop, calls=%fused_computation.29 | loop fusion | flops 40957952 | bytes 32784384 | tf_op jit(solution)/shard_map/reduce_sum | solution.py:494
  604.0 43.5 %convolution_convert_fusion = bf16[2048,8000]{0,1:T(8,128)(2,1)} fusion(bf16[256,2048]{1,0:T(8,128)(2,1)} %copy-done.56, bf16[256,2048]{1,0:T(8,128)(2,1)} %copy-done.58, bf16[256,2048]{1,0:T(8,128)(2,1)} %copy-done.59, bf16[256,2048]{1,0:T(8,128)(2,1)} %broadcast_select_fusion.10, f32[1024,8000]{0,1:T(8,128)} %get-tuple-element.276, ...), kind=kOutput, calls=%fused_computation.30 | convolution fusion | flops 33636745216 | bytes 69742592 | tf_op jit(solution)/shard_map/dot_general | solution.py:359
  650.9 43.0 %convolution_convert_fusion.3 = bf16[1024,2048]{1,0:T(8,128)(2,1)S(1)} fusion(bf16[2048,8000]{0,1:T(8,128)(2,1)} %all-gather.16.cloned.1.call-done, f32[1024,8000]{0,1:T(8,128)} %get-tuple-element.276, f32[1024]{0:T(1024)S(1)} %get-tuple-element.265, f32[1024]{0:T(1024)S(1)} %get-tuple-element.184, s32[1024]{0:T(1024)S(1)} %bitcast.287), kind=kOutput, calls=%fused_computation.82 | convolution fusion | flops 33605681152 | bytes 69742592 | tf_op jit(solution)/shard_map/dot_general | solution.py:359
  700.3 22.5 %collective-permute-done.42 = bf16[256,2048]{1,0:T(8,128)(2,1)S(1)} collective-permute-done((bf16[256,2048]{1,0:T(8,128)(2,1)S(1)}, bf16[256,2048]{1,0:T(8,128)(2,1)S(1)}, u32[]{:S(2)}, u32[]{:S(2)}) %collective-permute-start.42) | collective-permute-done | bytes 1048608 | tf_op jit(solution)/shard_map/ppermute | solution.py:334
  728.3 21.4 %collective-permute-done.43 = bf16[256,2048]{1,0:T(8,128)(2,1)S(1)} collective-permute-done((bf16[256,2048]{1,0:T(8,128)(2,1)S(1)}, bf16[256,2048]{1,0:T(8,128)(2,1)S(1)}, u32[]{:S(2)}, u32[]{:S(2)}) %collective-permute-start.43) | collective-permute-done | bytes 1048608 | tf_op jit(solution)/shard_map/ppermute | solution.py:334
  759.0 17.8 %collective-permute-done.47 = bf16[256,2048]{1,0:T(8,128)(2,1)S(1)} collective-permute-done((bf16[256,2048]{1,0:T(8,128)(2,1)S(1)}, bf16[256,2048]{1,0:T(8,128)(2,1)S(1)}, u32[]{:S(2)}, u32[]{:S(2)}) %collective-permute-start.47) | collective-permute-done | bytes 1048608 | tf_op jit(solution)/shard_map/ppermute | solution.py:335
  812.8 20.7 %collective-permute-done.50 = bf16[256,2048]{1,0:T(8,128)(2,1)S(1)} collective-permute-done((bf16[256,2048]{1,0:T(8,128)(2,1)S(1)}, bf16[256,2048]{1,0:T(8,128)(2,1)S(1)}, u32[]{:S(2)}, u32[]{:S(2)}) %collective-permute-start.50) | collective-permute-done | bytes 1048608 | tf_op jit(solution)/shard_map/ppermute | solution.py:282
  836.1 14.0 %collective-permute-done.51 = bf16[256,2048]{1,0:T(8,128)(2,1)S(1)} collective-permute-done((bf16[256,2048]{1,0:T(8,128)(2,1)S(1)}, bf16[256,2048]{1,0:T(8,128)(2,1)S(1)}, u32[]{:S(2)}, u32[]{:S(2)}) %collective-permute-start.51) | collective-permute-done | bytes 1048608 | tf_op jit(solution)/shard_map/ppermute | solution.py:282
  851.2 16.4 %multiply_convert_fusion.1 = (bf16[1024,1408]{1,0:T(8,128)(2,1)}, bf16[1024,1408]{1,0:T(8,128)(2,1)}) fusion(f32[1024,2816]{1,0:T(8,128)} %fusion.77, bf16[1408,2048]{1,0:T(8,128)(2,1)} %all-gather.14.cloned.1.call-done, bf16[256,2048]{1,0:T(8,128)(2,1)} %copy-done.68, bf16[256,2048]{1,0:T(8,128)(2,1)S(1)} %broadcast_select_fusion.1, ...), kind=kOutput, calls=%fused_computation.55 | convolution fusion | flops 5941100544 | bytes 27262976 | tf_op jit(solution)/shard_map/dot_general | solution.py:359
  919.1 18.1 %convolution_convert_fusion.1 = bf16[2048,2816]{1,0:T(8,128)(2,1)} fusion(bf16[1024,1408]{1,0:T(8,128)(2,1)} %get-tuple-element.189, bf16[1024,1408]{1,0:T(8,128)(2,1)} %get-tuple-element.190, bf16[256,2048]{1,0:T(8,128)(2,1)S(1)} %copy-done.49, bf16[256,2048]{1,0:T(8,128)(2,1)S(1)} %copy-done.52, bf16[256,2048]{1,0:T(8,128)(2,1)S(1)} %copy-done.53, ...), kind=kOutput, calls=%fused_computation.33 | convolution fusion | flops 11845238784 | bytes 21495808 | tf_op jit(solution)/shard_map/dot_general | solution.py:359
  994.3 31.8 %attend_back.1 = (bf16[256,2048]{1,0:T(8,128)(2,1)}, bf16[1024,512]{1,0:T(8,128)(2,1)}) custom-call(bf16[256,2048]{1,0:T(8,128)(2,1)} %get-tuple-element.124.q_ref, bf16[1024,512]{1,0:T(8,128)(2,1)} %copy-done.20, f32[16,2,256]{2,1,0:T(2,128)} %get-tuple-element.125.lse_ref, bf16[256,2048]{1,0:T(8,128)(2,1)} %convolution_convert_fusion.10.grad_ref, ...), custom_call_target="tpu_custom_call" | custom-call | tf_op jit(solution)/shard_map/attend_back/pallas_call | solution.py:219
  1114.3 12.8 fusion
  1143.5 16.3 %fusion.9 = f32[8000,256]{1,0:T(8,128)} fusion(f32[8000,256]{1,0:T(8,128)S(1)} %fusion, s32[2048]{0:T(1024)S(1)} %bitcast.297, bf16[2048,256]{1,0:T(8,128)(2,1)} %collective-permute-done.70, bf16[2048,256]{1,0:T(8,128)(2,1)} %collective-permute-done.71, pred[]{:T(512)S(6)} %eq.125), kind=kOutput, calls=%fused_computation.35 | convolution fusion | flops 8407564288 | bytes 18489344 | tf_op jit(solution)/shard_map/dot_general | solution.py:359
  1177.8 16.3 %fusion.8 = f32[8000,256]{1,0:T(8,128)} fusion(f32[8000,256]{1,0:T(8,128)S(1)} %copy-done.98, s32[2048]{0:T(1024)S(1)} %bitcast.296, bf16[2048,256]{1,0:T(8,128)(2,1)} %collective-permute-done.70, bf16[2048,256]{1,0:T(8,128)(2,1)} %collective-permute-done.72, bf16[2048,256]{1,0:T(8,128)(2,1)} %collective-permute-done.73, pred[]{:T(512)S(6)} %eq.130, ...), kind=kOutput, calls=%fused_computation.34 | convolution fusion | flops 8408088576 | bytes 19537922 | tf_op jit(solution)/shard_map/dot_general | solution.py:359
  1200.4 17.3 %collective-permute-done.62 = bf16[2048,256]{1,0:T(8,128)(2,1)} collective-permute-done((bf16[2048,256]{1,0:T(8,128)(2,1)}, bf16[2048,256]{1,0:T(8,128)(2,1)}, u32[]{:S(2)}, u32[]{:S(2)}) %collective-permute-start.62) | collective-permute-done | bytes 1048608 | tf_op jit(solution)/shard_map/ppermute | solution.py:568
  1224.7 17.6 %multiply_reduce_fusion = (f32[]{:T(128)}, f32[8000,256]{1,0:T(8,128)}) fusion(f32[8000,256]{1,0:T(8,128)} %fusion.8, bf16[2048,256]{1,0:T(8,128)(2,1)} %collective-permute-done.70, bf16[2048,256]{1,0:T(8,128)(2,1)} %collective-permute-done.72, bf16[2048,256]{1,0:T(8,128)(2,1)} %collective-permute-done.74, bf16[2048,256]{1,0:T(8,128)(2,1)} %collective-permute-done.75, ...), kind=kOutput, calls=%fused_computation.48 | convolution fusion | flops 8412708864 | bytes 20586504 | tf_op jit(solution)/shard_map/dot_general | solution.py:359
  1273.1 20.2 %multiply_subtract_fusion = (f32[256,8000]{0,1:T(8,128)}, f32[256,8000]{0,1:T(8,128)}, f32[256,8000]{0,1:T(8,128)}) fusion(f32[256,8000]{0,1:T(8,128)} %param.40, f32[]{:T(128)S(6)} %min.19, bf16[256,8000]{0,1:T(8,128)(2,1)} %reduce-scatter.5.cloned.1.call-done, f32[256,8000]{0,1:T(8,128)} %param.48, f32[256,8000]{0,1:T(8,128)} %param.56), kind=kLoop, calls=%fused_computation.46 | loop fusion | flops 34816000 | bytes 53248004 | tf_op jit(solution)/shard_map/sub | solution.py:355
  1293.3 21.8 %multiply_subtract_fusion.1 = (f32[8000,256]{1,0:T(8,128)}, f32[8000,256]{1,0:T(8,128)}, f32[8000,256]{1,0:T(8,128)}) fusion(f32[8000,256]{1,0:T(8,128)} %param.34, f32[8000,256]{1,0:T(8,128)} %param.42, f32[8000,256]{1,0:T(8,128)} %param.50, f32[8000,256]{1,0:T(8,128)} %get-tuple-element.279, f32[]{:T(128)S(6)} %min.19), kind=kLoop, calls=%fused_computation.47 | loop fusion | flops 32768000 | bytes 57344004 | tf_op jit(solution)/shard_map/sub | solution.py:355
  (616 shorter events, 632.1 us)
Async XLA Ops:
  7.2 205.4 %all-gather.8.cloned.1.call-start = ((), (), s32[]{:S(2)}) async-start(), calls=%async_computation.6 | async-start | bytes 11796480 | tf_op jit(solution)/shard_map/all_gather | solution.py:443
  22.3 44.2 %collective-permute-start = (bf16[256,512]{1,0:T(8,128)(2,1)S(1)}, bf16[256,512]{1,0:T(8,128)(2,1)S(1)}, u32[]{:S(2)}, u32[]{:S(2)}) collective-permute-start(bf16[256,512]{1,0:T(8,128)(2,1)S(1)} %convert_element_type.292), channel_id=1, source_target_pairs={{0,1},{1,2},{2,3},{3,0},{4,5},{5,6},{6,7},{7,4},{8,9},{9,10},{10,1... | collective-permute-start | bytes 786440 | tf_op jit(solution)/shard_map/ppermute | solution.py:253
  23.9 50.9 %collective-permute-start.1 = (bf16[256,512]{1,0:T(8,128)(2,1)S(1)}, bf16[256,512]{1,0:T(8,128)(2,1)S(1)}, u32[]{:S(2)}, u32[]{:S(2)}) collective-permute-start(bf16[256,512]{1,0:T(8,128)(2,1)S(1)} %convert_element_type.292), channel_id=1, source_target_pairs={{0,2},{1,3},{2,0},{3,1},{4,6},{5,7},{6,4},{7,5},{8,10},{9,11},{10,... | collective-permute-start | bytes 786440 | tf_op jit(solution)/shard_map/ppermute | solution.py:253
  26.5 48.3 %collective-permute-start.2 = (bf16[256,512]{1,0:T(8,128)(2,1)S(1)}, bf16[256,512]{1,0:T(8,128)(2,1)}, u32[]{:S(2)}, u32[]{:S(2)}) collective-permute-start(bf16[256,512]{1,0:T(8,128)(2,1)S(1)} %convert_element_type.292), channel_id=1, source_target_pairs={{0,3},{1,0},{2,1},{3,2},{4,7},{5,4},{6,5},{7,6},{8,11},{9,8},{10,9... | collective-permute-start | bytes 786440 | tf_op jit(solution)/shard_map/ppermute | solution.py:253
  27.9 46.9 %collective-permute-start.3 = (bf16[512,256]{1,0:T(8,128)(2,1)S(1)}, bf16[512,256]{1,0:T(8,128)(2,1)S(1)}, u32[]{:S(2)}, u32[]{:S(2)}) collective-permute-start(bf16[512,256]{1,0:T(8,128)(2,1)S(1)} %convert_element_type.293), channel_id=1, source_target_pairs={{0,1},{1,2},{2,3},{3,0},{4,5},{5,6},{6,7},{7,4},{8,9},{9,10},{10,1... | collective-permute-start | bytes 786440 | tf_op jit(solution)/shard_map/ppermute | solution.py:253
  28.5 46.3 %collective-permute-start.4 = (bf16[512,256]{1,0:T(8,128)(2,1)S(1)}, bf16[512,256]{1,0:T(8,128)(2,1)S(1)}, u32[]{:S(2)}, u32[]{:S(2)}) collective-permute-start(bf16[512,256]{1,0:T(8,128)(2,1)S(1)} %convert_element_type.293), channel_id=1, source_target_pairs={{0,2},{1,3},{2,0},{3,1},{4,6},{5,7},{6,4},{7,5},{8,10},{9,11},{10,... | collective-permute-start | bytes 786440 | tf_op jit(solution)/shard_map/ppermute | solution.py:253
  78.3 207.2 %all-gather.10.cloned.1.call-start = ((), (), s32[]{:S(2)}) async-start(), calls=%async_computation.7 | async-start | bytes 9437184 | tf_op jit(solution)/shard_map/all_gather | solution.py:454
  80.7 286.0 %all-gather.12.cloned.1.call-start = ((), (), s32[]{:S(2)}) async-start(), calls=%async_computation.8 | async-start | bytes 12976128 | tf_op jit(solution)/shard_map/all_gather | solution.py:453
  108.4 283.1 %all-gather.14.cloned.1.call-start = ((), (), s32[]{:S(2)}) async-start(), calls=%async_computation.9 | async-start | bytes 6488064 | tf_op jit(solution)/shard_map/all_gather | solution.py:455
  134.6 404.0 %all-gather.16.cloned.1.call-start = ((), (), s32[]{:S(2)}) async-start(), calls=%async_computation.10 | async-start | bytes 36864000 | tf_op jit(solution)/shard_map/all_gather | solution.py:456
  176.7 30.4 %all-to-all-start = ((bf16[8,256,256]{2,1,0:T(8,128)(2,1)}), bf16[8,256,256]{2,1,0:T(8,128)(2,1)S(1)}, u32[]{:S(2)}, u32[]{:S(2)}) async-start(bf16[8,256,256]{2,1,0:T(8,128)(2,1)} %bitcast.8), calls=%async_computation | async-start | bytes 2097152 | tf_op jit(solution)/shard_map/all_to_all | solution.py:464
  180.2 717.1 %reduce-scatter.5.cloned.1.call-start = ((), (), s32[]{:S(2)}) async-start(), calls=%async_computation.11 | async-start | bytes 36864000 | tf_op jit(solution)/shard_map/reduce_scatter | solution.py:512
  209.2 75.4 %collective-permute-start.15 = (bf16[256,2048]{1,0:T(8,128)(2,1)S(1)}, bf16[256,2048]{1,0:T(8,128)(2,1)S(1)}, u32[]{:S(2)}, u32[]{:S(2)}) collective-permute-start(bf16[256,2048]{1,0:T(8,128)(2,1)S(1)} %multiply_convert_fusion.6), channel_id=1, source_target_pairs={{0,1},{1,2},{2,3},{4,5},{5,6},{6,7},{8,9},{9,10},{10,11},{12,13},{... | collective-permute-start | bytes 3145736 | tf_op jit(solution)/shard_map/ppermute | solution.py:281
  211.3 73.2 %collective-permute-start.16 = (bf16[256,2048]{1,0:T(8,128)(2,1)S(1)}, bf16[256,2048]{1,0:T(8,128)(2,1)S(1)}, u32[]{:S(2)}, u32[]{:S(2)}) collective-permute-start(bf16[256,2048]{1,0:T(8,128)(2,1)S(1)} %multiply_convert_fusion.6), channel_id=1, source_target_pairs={{1,0},{2,1},{3,2},{5,4},{6,5},{7,6},{9,8},{10,9},{11,10},{13,12},{... | collective-permute-start | bytes 3145736 | tf_op jit(solution)/shard_map/ppermute | solution.py:282
  222.0 32.1 %collective-permute-start.13 = (bf16[256,512]{1,0:T(8,128)(2,1)}, bf16[256,512]{1,0:T(8,128)(2,1)S(1)}, u32[]{:S(2)}, u32[]{:S(2)}) collective-permute-start(bf16[256,512]{1,0:T(8,128)(2,1)} %turn_keys.2), channel_id=1, source_target_pairs={{0,2},{1,3},{2,0},{3,1},{4,6},{5,7},{6,4},{7,5},{8,10},{9,11},{10,... | collective-permute-start | bytes 786440 | tf_op jit(solution)/shard_map/ppermute | solution.py:253
  222.0 32.1 %collective-permute-start.14 = (bf16[256,512]{1,0:T(8,128)(2,1)}, bf16[256,512]{1,0:T(8,128)(2,1)S(1)}, u32[]{:S(2)}, u32[]{:S(2)}) collective-permute-start(bf16[256,512]{1,0:T(8,128)(2,1)} %turn_keys.2), channel_id=1, source_target_pairs={{0,3},{1,0},{2,1},{3,2},{4,7},{5,4},{6,5},{7,6},{8,11},{9,8},{10,9... | collective-permute-start | bytes 786440 | tf_op jit(solution)/shard_map/ppermute | solution.py:253
  598.5 49.0 %collective-permute-start.38 = (bf16[256,2048]{1,0:T(8,128)(2,1)S(1)}, bf16[256,2048]{1,0:T(8,128)(2,1)S(1)}, u32[]{:S(2)}, u32[]{:S(2)}) collective-permute-start(bf16[256,2048]{1,0:T(8,128)(2,1)S(1)} %copy-done.39), channel_id=1, source_target_pairs={{1,2},{2,3},{5,6},{6,7},{9,10},{10,11},{13,14},{14,15},{17,18},{18... | collective-permute-start | bytes 3145736 | tf_op jit(solution)/shard_map/ppermute | solution.py:281
  599.3 48.3 %collective-permute-start.39 = (bf16[256,2048]{1,0:T(8,128)(2,1)S(1)}, bf16[256,2048]{1,0:T(8,128)(2,1)}, u32[]{:S(2)}, u32[]{:S(2)}) collective-permute-start(bf16[256,2048]{1,0:T(8,128)(2,1)S(1)} %copy-done.42), channel_id=1, source_target_pairs={{1,0},{2,1},{5,4},{6,5},{9,8},{10,9},{13,12},{14,13},{17,16},{18,1... | collective-permute-start | bytes 3145736 | tf_op jit(solution)/shard_map/ppermute | solution.py:282
  647.6 319.8 %reduce-scatter.7.cloned.1.call-start = ((), (), s32[]{:S(2)}) async-start(), calls=%async_computation.12 | async-start | bytes 6488064 | tf_op jit(solution)/shard_map/reduce_scatter | solution.py:512
  648.5 45.4 %collective-permute-start.40 = (bf16[256,2048]{1,0:T(8,128)(2,1)S(1)}, bf16[256,2048]{1,0:T(8,128)(2,1)S(1)}, u32[]{:S(2)}, u32[]{:S(2)}) collective-permute-start(bf16[256,2048]{1,0:T(8,128)(2,1)S(1)} %collective-permute-done.38), channel_id=1, source_target_pairs={{2,3},{6,7},{10,11},{14,15},{18,19},{22,23},{26,27},{30,31}} | collective-permute-start | bytes 3145736 | tf_op jit(solution)/shard_map/ppermute | solution.py:281
  649.2 44.7 %collective-permute-start.41 = (bf16[256,2048]{1,0:T(8,128)(2,1)}, bf16[256,2048]{1,0:T(8,128)(2,1)S(1)}, u32[]{:S(2)}, u32[]{:S(2)}) collective-permute-start(bf16[256,2048]{1,0:T(8,128)(2,1)} %collective-permute-done.39), channel_id=1, source_target_pairs={{1,0},{5,4},{9,8},{13,12},{17,16},{21,20},{25,24},{29,28}} | collective-permute-start | bytes 3145736 | tf_op jit(solution)/shard_map/ppermute | solution.py:282
  897.4 216.8 %reduce-scatter.9.cloned.1.call-start = ((), (), s32[]{:S(2)}) async-start(), calls=%async_computation.13 | async-start | bytes 12976128 | tf_op jit(solution)/shard_map/reduce_scatter | solution.py:512
  1058.7 42.1 %all-to-all-start.1 = ((bf16[8,272,256]{2,1,0:T(8,128)(2,1)}), bf16[8,272,256]{2,1,0:T(8,128)(2,1)S(1)}, u32[]{:S(2)}, u32[]{:S(2)}) async-start(bf16[8,272,256]{2,1,0:T(8,128)(2,1)} %bitcast.212), calls=%async_computation.3 | async-start | bytes 2228224 | tf_op jit(solution)/shard_map/all_to_all | solution.py:605
  1065.5 94.4 %reduce-scatter.11.cloned.1.call-start = ((), (), s32[]{:S(2)}) async-start(), calls=%async_computation.14 | async-start | bytes 2949120 | tf_op jit(solution)/shard_map/reduce_scatter | solution.py:512
  1076.3 89.0 %collective-permute-start.60 = (bf16[2048,1024]{1,0:T(8,128)(2,1)}, bf16[2048,1024]{1,0:T(8,128)(2,1)}, u32[]{:S(2)}, u32[]{:S(2)}) collective-permute-start(bf16[2048,1024]{1,0:T(8,128)(2,1)} %convolution_convert_fusion.5), channel_id=1, source_target_pairs={{0,4},{4,0},{8,12},{12,8},{16,20},{20,16},{24,28},{28,24},{1,5},{5... | collective-permute-start | bytes 12582920 | tf_op jit(solution)/shard_map/ppermute | solution.py:556
  1100.8 39.7 %collective-permute-start.70 = (bf16[2048,256]{1,0:T(8,128)(2,1)S(1)}, bf16[2048,256]{1,0:T(8,128)(2,1)}, u32[]{:S(2)}, u32[]{:S(2)}) collective-permute-start(bf16[2048,256]{1,0:T(8,128)(2,1)S(1)} %bitcast.228), channel_id=1, source_target_pairs={{1,0},{2,1},{3,2},{5,4},{6,5},{7,6},{9,8},{10,9},{11,10},{13,12},{... | collective-permute-start | bytes 3145736 | tf_op jit(solution)/shard_map/ppermute | solution.py:315
  1102.1 39.7 %collective-permute-start.71 = (bf16[2048,256]{1,0:T(8,128)(2,1)S(1)}, bf16[2048,256]{1,0:T(8,128)(2,1)}, u32[]{:S(2)}, u32[]{:S(2)}) collective-permute-start(bf16[2048,256]{1,0:T(8,128)(2,1)S(1)} %bitcast.229), channel_id=1, source_target_pairs={{0,1},{1,2},{2,3},{4,5},{5,6},{6,7},{8,9},{9,10},{10,11},{12,13},{... | collective-permute-start | bytes 3145736 | tf_op jit(solution)/shard_map/ppermute | solution.py:314
  1140.5 33.7 %collective-permute-start.72 = (bf16[2048,256]{1,0:T(8,128)(2,1)}, bf16[2048,256]{1,0:T(8,128)(2,1)}, u32[]{:S(2)}, u32[]{:S(2)}) collective-permute-start(bf16[2048,256]{1,0:T(8,128)(2,1)} %collective-permute-done.70), channel_id=1, source_target_pairs={{1,0},{2,1},{5,4},{6,5},{9,8},{10,9},{13,12},{14,13},{17,16},{18,1... | collective-permute-start | bytes 3145736 | tf_op jit(solution)/shard_map/ppermute | solution.py:315
  1141.8 32.8 %collective-permute-start.73 = (bf16[2048,256]{1,0:T(8,128)(2,1)}, bf16[2048,256]{1,0:T(8,128)(2,1)}, u32[]{:S(2)}, u32[]{:S(2)}) collective-permute-start(bf16[2048,256]{1,0:T(8,128)(2,1)} %collective-permute-done.71), channel_id=1, source_target_pairs={{1,2},{2,3},{5,6},{6,7},{9,10},{10,11},{13,14},{14,15},{17,18},{18... | collective-permute-start | bytes 3145736 | tf_op jit(solution)/shard_map/ppermute | solution.py:314
  1172.7 45.0 %collective-permute-start.62 = (bf16[2048,256]{1,0:T(8,128)(2,1)}, bf16[2048,256]{1,0:T(8,128)(2,1)}, u32[]{:S(2)}, u32[]{:S(2)}) collective-permute-start(bf16[2048,256]{1,0:T(8,128)(2,1)} %get-tuple-element.192), channel_id=1, source_target_pairs={{0,16},{4,20},{8,24},{12,28},{16,0},{20,4},{24,8},{28,12},{1,17},{... | collective-permute-start | bytes 3145736 | tf_op jit(solution)/shard_map/ppermute | solution.py:568
  1174.2 43.5 %collective-permute-start.63 = (bf16[2048,256]{1,0:T(8,128)(2,1)S(1)}, bf16[2048,256]{1,0:T(8,128)(2,1)}, u32[]{:S(2)}, u32[]{:S(2)}) collective-permute-start(bf16[2048,256]{1,0:T(8,128)(2,1)S(1)} %get-tuple-element.191), channel_id=1, source_target_pairs={{0,24},{4,28},{8,16},{12,20},{16,8},{20,12},{24,0},{28,4},{1,25},{... | collective-permute-start | bytes 3145736 | tf_op jit(solution)/shard_map/ppermute | solution.py:568
  1194.1 30.6 %collective-permute-start.74 = (bf16[2048,256]{1,0:T(8,128)(2,1)}, bf16[2048,256]{1,0:T(8,128)(2,1)}, u32[]{:S(2)}, u32[]{:S(2)}) collective-permute-start(bf16[2048,256]{1,0:T(8,128)(2,1)} %collective-permute-done.72), channel_id=1, source_target_pairs={{1,0},{5,4},{9,8},{13,12},{17,16},{21,20},{25,24},{29,28}} | collective-permute-start | bytes 3145736 | tf_op jit(solution)/shard_map/ppermute | solution.py:315
  (171 other events, 4018.6 us)
Sparse Core Ops, SparseCore 0:
  78.5 65.1 all-gather.7
  146.2 67.1 all-gather.9
  215.8 69.8 all-gather.11
  288.1 44.3 all-gather.13
  334.8 163.9 all-gather.15
  647.7 211.3 reduce-scatter.4
  897.5 65.7 reduce-scatter.6
  967.2 86.7 reduce-scatter.8
  1114.4 44.2 reduce-scatter.10
